TPU v7x, 1024 devices: a whole 4x4x32 slice. The times are simulated.
1024 devices in a mesh: row: 8 (over x, core), col: 128 (over y, z).
Axes of the slice: x: 4, y: 4, z: 32, core: 2. Of those that a mesh axis runs over, the one named last changes fastest.
Arguments:
- grad_out: bfloat16 [256, 53248], P('row', 'col'), may hold values from -6 to 6
- acts: bfloat16 [256, 16384], P('col', 'row'), may hold values from -6 to 6
- weight: bfloat16 [16384, 53248], P('row', 'col'), may hold values from -0.046875 to 0.046875
Outputs:
- grad_in: bfloat16 [256, 16384], P('col', 'row')
- grad_weight: bfloat16 [16384, 53248], P('row', 'col')
All inputs are finite; a program needn't handle non-finite values.
Results may differ from a plain program's by a relative error of at most 0.001.
Values may be sent and summed in bfloat16 or wider, within the bound.
No kernel may reach another device: no remote copies, remote signals or barrier semaphores. Data moves between devices by JAX's collectives and lax.ppermute only.
A program may use at most 32 MiB of HBM per device.

v0:
```python
import jax
import jax.numpy as jnp
from jax import lax
from jax.sharding import PartitionSpec as P

MXB = 32


code_limit = 448.0
peak_floor = 0.25


def block_scale(peaks):
    scale = jnp.full_like(peaks, 2.0 ** (-10))
    for power in range(-1, 8):
        scale = jnp.where(peaks >= 2.0**power, 2.0 ** (power - 8), scale)
    return scale


def grid_codes(scaled):
    clipped = jnp.clip(scaled, -code_limit, code_limit)
    magnitude = jnp.abs(clipped)
    spacing = jnp.full_like(magnitude, 2.0 ** (-9))
    for power in range(-5, 9):
        spacing = jnp.where(magnitude >= 2.0**power, 2.0 ** (power - 3), spacing)
    return jnp.sign(clipped) * jnp.floor(magnitude / spacing + 0.5) * spacing


def requant_along_cols(values):
    height, width = values.shape
    blocks = values.astype(jnp.float32).reshape(height, width // MXB, MXB)
    peaks = jnp.maximum(jnp.max(jnp.abs(blocks), axis=2, keepdims=True), peak_floor)
    scale = block_scale(peaks)
    codes = grid_codes(blocks / scale).astype(jnp.bfloat16)
    restored = (codes.astype(jnp.float32) * scale).astype(jnp.bfloat16)
    return restored.reshape(height, width)


def requant_along_rows(values):
    height, width = values.shape
    blocks = values.astype(jnp.float32).reshape(height // MXB, MXB, width)
    peaks = jnp.maximum(jnp.max(jnp.abs(blocks), axis=1, keepdims=True), peak_floor)
    scale = block_scale(peaks)
    codes = grid_codes(blocks / scale).astype(jnp.bfloat16)
    restored = (codes.astype(jnp.float32) * scale).astype(jnp.bfloat16)
    return restored.reshape(height, width)


def local(grad_out, acts, weight):
    gradient = lax.all_gather(grad_out, "row", axis=0, tiled=True)
    grad_cols = requant_along_cols(gradient)
    grad_toks = requant_along_rows(gradient)
    own_rows = acts.shape[0]
    feat_count = acts.shape[1]
    group = min(own_rows, MXB)
    acts_wide = acts.astype(jnp.float32)
    local_peaks = jnp.max(jnp.abs(acts_wide).reshape(own_rows // group, group, feat_count), axis=1)
    peaks_all = lax.all_gather(local_peaks, "col", axis=0, tiled=True)
    total_rows = peaks_all.shape[0] * group
    block_peaks = jnp.maximum(
        jnp.max(peaks_all.reshape(total_rows // MXB, MXB // group, feat_count), axis=1), peak_floor
    )
    block_scales = block_scale(block_peaks)
    row_scales = jnp.broadcast_to(
        block_scales[:, None, :], (total_rows // MXB, MXB, feat_count)
    ).reshape(total_rows, feat_count)
    own_scales = lax.dynamic_slice_in_dim(row_scales, lax.axis_index("col") * own_rows, own_rows, 0)
    codes = grid_codes(acts_wide / own_scales).astype(jnp.bfloat16)
    all_codes = lax.all_gather(codes, "col", axis=0, tiled=True)
    act_toks = (all_codes.astype(jnp.float32) * row_scales).astype(jnp.bfloat16)
    grad_weight = lax.dot_general(
        act_toks, grad_toks, (((0,), (0,)), ((), ())), preferred_element_type=jnp.float32
    ).astype(jnp.bfloat16)
    grad_in = lax.psum_scatter(
        lax.dot_general(
            grad_cols, weight, (((1,), (1,)), ((), ())), preferred_element_type=jnp.float32
        ),
        "col",
        scatter_dimension=0,
        tiled=True,
    ).astype(jnp.bfloat16)
    return (grad_in, grad_weight)


def solution(mesh):
    return jax.shard_map(
        local,
        mesh=mesh,
        in_specs=(P("row", "col"), P("col", "row"), P("row", "col")),
        out_specs=(P("col", "row"), P("row", "col")),
        check_vma=False,
    )
```

profile of v0, /device:TPU:4, one launch (start us, length us, event | category | flops | bytes accessed | tf_op | source)
XLA Modules:
  0.0 866.5 jit_solution(6127781724332231383)
XLA Ops:
  7.2 0.0 copy-start
  7.2 0.0 all-gather.5.cloned.1.call-start
  7.2 1.4 fusion.23
  8.7 0.0 all-gather.5.cloned.1.call-update
  8.7 0.0 all-gather.7.cloned.1.call-start
  8.7 24.1 %all_gather.9 = bf16[256,416]{1,0:T(8,128)(2,1)S(1)} all-gather(bf16[32,416]{1,0:T(8,128)(2,1)} %param.3), channel_id=1, replica_groups=mesh['row'=8,'col'=128] {'row'}, dimensions={0}, use_global_device_ids=true | all-gather | bytes 239616 | tf_op jit(solution)/shard_map/all_gather | solution.py:50
  32.9 0.1 copy.14
  33.1 0.2 copy.15
  33.3 0.7 reduce_max.38
  33.9 239.4 %all-gather.5.cloned.1.call-done = f32[262144]{0:T(1024)} async-done(((f32[2048]{0:T(1024)}), f32[262144]{0:T(1024)}) %all-gather.5.cloned.1.call-update) | async-done | bytes 1048592 | tf_op jit(solution)/shard_map/all_gather | solution.py:58
  273.3 1.4 reshape.123
  274.7 0.2 reduce_max.41
  274.9 0.0 copy-start.3
  274.9 0.0 copy-start.2
  274.9 0.2 broadcast_in_dim.236
  275.2 0.0 copy-start.1
  275.2 1.3 copy-done.1
  276.5 0.0 copy-done.3
  276.5 0.7 fusion.25
  277.3 0.0 all-gather.7.cloned.1.call-update
  277.3 0.0 copy-done.2
  277.3 0.7 fusion.2
  278.0 0.1 bitcast_reduce_fusion
  278.1 0.1 div.42
  278.1 0.2 copy.16
  278.3 0.0 copy-done
  278.3 2.0 fusion.46
  280.3 1.3 dynamic-slice
  282.3 569.6 %all-reduce.2 = bf16[256,2048]{1,0:T(8,128)(2,1)S(1)} all-reduce(f32[256,2048]{1,0:T(8,128)} %fusion.46), channel_id=3, replica_groups=mesh['row'=8,'col'=128] {'col'}, use_global_device_ids=true, to_apply=%region_1.2.clone | all-reduce | flops 524288 | bytes 3145728
  851.9 0.6 dynamic-slice_convert_fusion
  852.5 2.5 reshape.129
  855.0 4.6 convolution_convert_fusion
  (5 shorter events, 0.1 us)
Async XLA Ops:
  7.2 271.1 %copy-start = (bf16[2048,416]{0,1:T(8,128)(2,1)S(1)}, bf16[2048,416]{0,1:T(8,128)(2,1)}, u32[]{:S(2)}) copy-start(bf16[2048,416]{0,1:T(8,128)(2,1)} %param.5) | copy-start | bytes 5111812
  7.2 266.1 %all-gather.5.cloned.1.call-start = ((), (), s32[]{:S(2)}) async-start(), calls=%async_computation | async-start | bytes 1056768 | tf_op jit(solution)/shard_map/all_gather | solution.py:58
  8.7 843.8 %all-gather.7.cloned.1.call-start = ((), (), s32[]{:S(2)}) async-start(), calls=%async_computation.1 | async-start | bytes 1056768 | tf_op jit(solution)/shard_map/all_gather | solution.py:69
  274.9 1.7 copy-start.3
  274.9 2.4 copy-start.2
  275.2 1.4 copy-start.1
Sparse Core Ops, SparseCore 0:
  12.7 260.6 all-gather.4
  277.4 243.4 all-gather.6
where the time goes:
time: 867 us; the launch traced here: 866 us
  blocking collectives  594 us (69%)
  waiting for transfers between devices  239 us (28%)
  between operations  14.8 us (2%)
    unnamed x1, blocking collectives  570 us
    all_gather x1, waiting for transfers between devices, local(): peaks_all = lax.all_gather(local_peaks, 'col', axis=0, tiled=True)  239 us
    all_gather x1, blocking collectives, local(): gradient = lax.all_gather(grad_out, 'row', axis=0, tiled=True)  24.1 us
  transfers between devices with their start and end apart: 2, of which 1 were waited for; matrix products, arithmetic and copies ran while one was open for 1% of the time, Pallas kernels for 0%

commit v1 on v0

v1 whole, which is shorter than its diff:
```python
import functools

import jax
import jax.numpy as jnp
from jax import lax
from jax.experimental import pallas as pl
from jax.experimental.pallas import tpu as pltpu
from jax.sharding import Mesh
from jax.sharding import PartitionSpec as P

MXB = 32
CODE_LIMIT = 448.0
PEAK_FLOOR = 0.25
Y, ZH, ZL = 4, 8, 4
F32 = jnp.float32
BF16 = jnp.bfloat16


def block_scale(peaks):
    scale = jnp.full_like(peaks, 2.0 ** (-10))
    for power in range(-1, 8):
        scale = jnp.where(peaks >= 2.0**power, 2.0 ** (power - 8), scale)
    return scale


def requant(blocks, axis):
    peaks = jnp.maximum(jnp.max(jnp.abs(blocks), axis=axis, keepdims=True), PEAK_FLOOR)
    scale = block_scale(peaks)
    limit = CODE_LIMIT * scale
    held = jnp.minimum(jnp.maximum(blocks, -limit), limit) * (1.0 + 2.0**-12)
    wide = held * (2.0**20 + 1.0)
    normal = wide - (wide - held)
    anchor = (1.5 * 2.0**14) * scale
    small = (held + anchor) - anchor
    return jnp.where(jnp.abs(blocks) < 2.0**-6 * scale, small, normal)


def dot(a, b, dims):
    return lax.dot_general(a, b, (dims, ((), ())), preferred_element_type=F32)


def partial_kernel(y_ref, g_ref, w_ref, *out_refs):
    tok, ff = g_ref.shape
    g_t = g_ref[...].astype(F32).T
    codes_t = requant(g_t.reshape(ff // MXB, MXB, tok), 1).reshape(ff, tok).astype(BF16)
    chunk = tok // Y
    row = lax.broadcasted_iota(jnp.int32, (tok, tok), 0)
    col = lax.broadcasted_iota(jnp.int32, (tok, tok), 1)
    far, rest = row // chunk, row % chunk
    zl, zh, pair = rest // (2 * ZH), rest % (2 * ZH) // 2, rest % 2
    source = (far + y_ref[0]) % Y * chunk + (zh * ZL + zl) * 2 + pair
    order = jnp.where(col == source, 1.0, 0.0).astype(BF16)
    codes = dot(order, codes_t, ((1,), (1,))).astype(BF16)
    for d, out_ref in enumerate(out_refs):
        out_ref[...] = dot(codes[d * chunk : (d + 1) * chunk], w_ref[...], ((1,), (0,)))


def partial_sums(y, g, w_t):
    tok, ff = g.shape
    feat = w_t.shape[1]
    return pl.pallas_call(
        partial_kernel,
        out_shape=[jax.ShapeDtypeStruct((tok // Y, feat), F32)] * Y,
        in_specs=[
            pl.BlockSpec(memory_space=pltpu.SMEM),
            pl.BlockSpec(memory_space=pltpu.VMEM),
            pl.BlockSpec(memory_space=pltpu.VMEM),
        ],
        out_specs=[pl.BlockSpec(memory_space=pltpu.VMEM)] * Y,
        compiler_params=pltpu.CompilerParams(vmem_limit_bytes=32 * 2**20),
        cost_estimate=pl.CostEstimate(
            flops=2 * tok * ff * feat, bytes_accessed=2 * ff * feat + 4 * tok * feat, transcendentals=0
        ),
    )(y, g, w_t)


def weight_kernel(y_ref, g_ref, *refs):
    act_refs, out_ref, toks_ref, ahead_ref = refs[:Y], refs[Y], refs[Y + 1], refs[Y + 2]
    tok, ff = g_ref.shape
    chunk = tok // Y

    @pl.when(pl.program_id(0) == 0)
    def _():
        g = g_ref[...].astype(F32).reshape(tok // MXB, MXB, ff)
        ahead_ref[...] = requant(g, 1).reshape(tok, ff)
        parts = []
        for d in range(Y):
            start = pl.multiple_of((y_ref[0] + (Y - d)) % Y * chunk, chunk)
            parts.append(ahead_ref[pl.ds(start, chunk), :].T)
        toks_ref[...] = jnp.concatenate(parts, axis=1).astype(BF16)

    acts = []
    for act_ref in act_refs:
        a = act_ref[...].astype(F32)
        width = a.shape[1]
        acts.append(requant(a.reshape(chunk // MXB, MXB, width), 1).reshape(chunk, width).astype(BF16))
    out_ref[...] = dot(toks_ref[...], jnp.concatenate(acts, axis=0), ((1,), (0,))).astype(BF16)


def weight_grad(y, g, acts):
    tok, ff = g.shape
    feat = acts[0].shape[1]
    tile = feat // 4
    return pl.pallas_call(
        weight_kernel,
        out_shape=jax.ShapeDtypeStruct((ff, feat), BF16),
        grid=(feat // tile,),
        in_specs=[
            pl.BlockSpec(memory_space=pltpu.SMEM),
            pl.BlockSpec((tok, ff), lambda i: (0, 0)),
        ]
        + [pl.BlockSpec((tok // Y, tile), lambda i: (0, i))] * Y,
        out_specs=pl.BlockSpec((ff, tile), lambda i: (0, i)),
        scratch_shapes=[pltpu.VMEM((ff, tok), BF16), pltpu.VMEM((tok, ff), F32)],
        compiler_params=pltpu.CompilerParams(vmem_limit_bytes=32 * 2**20),
        cost_estimate=pl.CostEstimate(
            flops=2 * tok * ff * feat + 20 * tok * feat,
            bytes_accessed=2 * ff * feat + 2 * tok * feat,
            transcendentals=0,
        ),
    )(y, g, *acts)


def along_y(x, distance):
    return lax.ppermute(x, "y", [(k, (k + distance) % Y) for k in range(Y)])


def local(grad_out, acts, weight):
    y = lax.axis_index("y").astype(jnp.int32).reshape(1)
    z = ZH * ZL
    rows, feat = acts.shape

    copies = jnp.broadcast_to(acts[None], (z, rows, feat))
    z_acts = lax.all_to_all(copies, ("zh", "zl"), 0, 0).reshape(z * rows, feat)
    g = lax.all_gather(grad_out, ("x", "core"), axis=0, tiled=True)

    sums = partial_sums(y, g, weight.T)
    arrived = [along_y(sums[d], d) for d in (2, 1, 3)]
    total = sums[0] + arrived[0] + arrived[1] + arrived[2]
    total = lax.psum_scatter(total, "zl", scatter_dimension=0, tiled=True)

    all_acts = [z_acts] + [along_y(z_acts, d) for d in (1, 2, 3)]

    parts = lax.all_to_all(total.reshape(ZH, rows, feat), "zh", 0, 0)
    grad_weight = weight_grad(y, g, all_acts).T
    grad_in = jnp.sum(parts, axis=0).astype(BF16)
    return grad_in, grad_weight


def solution(mesh):
    fine = Mesh(mesh.devices.reshape(4, 2, Y, ZH, ZL), ("x", "core", "y", "zh", "zl"))
    row, col = ("x", "core"), ("y", "zh", "zl")
    return jax.shard_map(
        local,
        mesh=fine,
        in_specs=(P(row, col), P(col, row), P(row, col)),
        out_specs=(P(col, row), P(row, col)),
        check_vma=False,
    )
```

time: 867 us -> 168 us (0.19)
  the two profiles are of different devices: /device:TPU:4 before, /device:TPU:8 now
where the time goes in v1:
time: 168 us; the launch traced here: 167 us
  starting transfers between devices  69.1 us (41%)
  waiting for transfers between devices  57.8 us (34%)
  between operations  14.1 us (8%)
  blocking collectives  13.4 us (8%)
  Pallas kernels  6.24 us (4%)
  local copies, waits for them, and re-layouts  4.02 us (2%)
  other arithmetic  2.74 us (2%)
    reduce_scatter x1, waiting for transfers between devices, local(): total = lax.psum_scatter(total, 'zl', scatter_dimension=0, tiled=True)  43.9 us
    ppermute x6, starting transfers between devices, along_y(): return lax.ppermute(x, 'y', [(k, (k + distance) % Y) for k in range(Y)])  30.4 us
    all_to_all x1, starting transfers between devices, local(): parts = lax.all_to_all(total.reshape(ZH, rows, feat), 'zh', 0, 0)  19.7 us
    all_to_all x1, starting transfers between devices, local(): z_acts = lax.all_to_all(copies, ('zh', 'zl'), 0, 0).reshape(z * rows, feat)  18.8 us
    all_gather x1, blocking collectives, local(): g = lax.all_gather(grad_out, ('x', 'core'), axis=0, tiled=True)  13.4 us
    ppermute x6, waiting for transfers between devices, along_y(): return lax.ppermute(x, 'y', [(k, (k + distance) % Y) for k in range(Y)])  8.35 us
    all_to_all x1, waiting for transfers between devices, local(): parts = lax.all_to_all(total.reshape(ZH, rows, feat), 'zh', 0, 0)  5.46 us
    pallas_call x1, Pallas kernels, weight_grad(): pl.pallas_call(weight_kernel, out_shape=jax.ShapeDtypeStruct((ff, feat),...  4.37 us
  transfers between devices with their start and end apart: 9, of which 4 were waited for; matrix products, arithmetic and copies ran while one was open for 3% of the time, Pallas kernels for 3%

profile of v1, /device:TPU:8, one launch (start us, length us, event | category | flops | bytes accessed | tf_op | source)
XLA Modules:
  0.0 167.4 jit_solution(12705253687919642251)
XLA Ops:
  7.2 0.0 copy-start.1
  7.2 13.4 %all_gather.3.g_ref = bf16[256,416]{1,0:T(8,128)(2,1)S(1)} all-gather(bf16[32,416]{1,0:T(8,128)(2,1)} %param.3), channel_id=1, replica_groups=mesh['x'=4,'core'=2,'y'=4,'zh'=8,'zl'=4] {'x','core'}, dimensions={0}, use_global_device_ids=true | all-gather | bytes 239616 | tf_op jit(solution)/shard_map/all_gather | solution.py:135
  20.6 0.0 copy-start
  20.6 1.5 copy-done
  22.0 1.9 %shard_map.50 = (f32[64,2048]{1,0:T(8,128)S(1)}, f32[64,2048]{1,0:T(8,128)S(1)}, f32[64,2048]{1,0:T(8,128)S(1)}, f32[64,2048]{1,0:T(8,128)S(1)}) custom-call(s32[1]{0:T(128)} %bitcast.y_ref, bf16[256,416]{1,0:T(8,128)(2,1)S(1)} %all_gather.3.g_ref, bf16[416,2048]{1,0:T(8,128)(2,1)S(1)} %bitcast.3), custom_call_target="tpu_custom_call" | custom-call | flops 436207616 | bytes 3801088 | tf_op jit(solution)/shard_map/pallas_call | solution.py:61
  23.9 4.2 %collective-permute-start = (f32[64,2048]{1,0:T(8,128)S(1)}, f32[64,2048]{1,0:T(8,128)S(1)}, u32[]{:S(2)}, u32[]{:S(2)}) collective-permute-start(f32[64,2048]{1,0:T(8,128)S(1)} %get-tuple-element.7), channel_id=1, source_target_pairs={{0,64},{32,96},{64,0},{96,32},{1,65},{33,97},{65,1},{97,33},{2,66}... | collective-permute-start | bytes 1572872 | tf_op jit(solution)/shard_map/ppermute | solution.py:125
  28.1 13.8 %collective-permute-start.1 = (f32[64,2048]{1,0:T(8,128)S(1)}, f32[64,2048]{1,0:T(8,128)}, u32[]{:S(2)}, u32[]{:S(2)}) collective-permute-start(f32[64,2048]{1,0:T(8,128)S(1)} %get-tuple-element.8), channel_id=1, source_target_pairs={{0,32},{32,64},{64,96},{96,0},{1,33},{33,65},{65,97},{97,1},{2,34}... | collective-permute-start | bytes 1572872 | tf_op jit(solution)/shard_map/ppermute | solution.py:125
  42.0 1.9 %collective-permute-start.2 = (f32[64,2048]{1,0:T(8,128)S(1)}, f32[64,2048]{1,0:T(8,128)}, u32[]{:S(2)}, u32[]{:S(2)}) collective-permute-start(f32[64,2048]{1,0:T(8,128)S(1)} %get-tuple-element.9), channel_id=1, source_target_pairs={{0,96},{32,0},{64,32},{96,64},{1,97},{33,1},{65,33},{97,65},{2,98}... | collective-permute-start | bytes 1572872 | tf_op jit(solution)/shard_map/ppermute | solution.py:125
  43.9 0.0 copy-done.1
  43.9 0.8 broadcast_in_dim.2
  44.8 18.8 %all-to-all-start.1 = ((bf16[32,2,2048]{2,1,0:T(2,128)(2,1)}), bf16[32,2,2048]{2,1,0:T(2,128)(2,1)S(1)}, u32[]{:S(2)}, u32[]{:S(2)}) async-start(bf16[32,2,2048]{2,1,0:T(2,128)(2,1)} %broadcast_in_dim.2), calls=%async_computation.2 | async-start | bytes 524288 | tf_op jit(solution)/shard_map/all_to_all | solution.py:134
  63.6 0.0 reduce-scatter.2.cloned.1.call-start
  63.6 0.0 collective-permute-done
  63.7 0.0 collective-permute-done.1
  63.7 0.0 collective-permute-done.2
  63.7 2.1 %add_add_fusion = f32[64,2048]{1,0:T(8,128)} fusion(f32[64,2048]{1,0:T(8,128)} %collective-permute-done.2, f32[64,2048]{1,0:T(8,128)} %collective-permute-done.1, f32[64,2048]{1,0:T(8,128)S(1)} %get-tuple-element.6, f32[64,2048]{1,0:T(8,128)S(1)} %collective-permute-done), kind=kLoop, calls=%fused_computation | loop fusion | flops 393216 | bytes 2621440 | tf_op jit(solution)/shard_map/add | solution.py:139
  65.8 0.0 reduce-scatter.2.cloned.1.call-update
  65.8 43.9 %reduce-scatter.2.cloned.1.call-done = f32[16,2048]{1,0:T(8,128)} async-done(((f32[64,2048]{1,0:T(8,128)}), f32[16,2048]{1,0:T(8,128)}) %reduce-scatter.2.cloned.1.call-update) | async-done | bytes 131088 | tf_op jit(solution)/shard_map/reduce_scatter | solution.py:140
  109.7 1.6 reshape.15
  111.3 0.0 all-to-all-done.1
  111.3 19.7 %all-to-all-start = ((f32[8,2,2048]{2,1,0:T(2,128)}), f32[8,2,2048]{2,1,0:T(2,128)S(1)}, u32[]{:S(2)}, u32[]{:S(2)}) async-start(f32[8,2,2048]{2,1,0:T(2,128)} %reshape.15), calls=%async_computation.1 | async-start | bytes 262144 | tf_op jit(solution)/shard_map/all_to_all | solution.py:144
  131.1 0.1 reshape.16.refs_0_
  131.2 3.4 %collective-permute-start.3 = (bf16[64,2048]{1,0:T(8,128)(2,1)S(1)}, bf16[64,2048]{1,0:T(8,128)(2,1)S(1)}, u32[]{:S(2)}, u32[]{:S(2)}) collective-permute-start(bf16[64,2048]{1,0:T(8,128)(2,1)S(1)} %reshape.16.refs_0_), channel_id=1, source_target_pairs={{0,32},{32,64},{64,96},{96,0},{1,33},{33,65},{65,97},{97,1},{2,34}... | collective-permute-start | bytes 786440 | tf_op jit(solution)/shard_map/ppermute | solution.py:125
  134.6 3.1 %collective-permute-start.4 = (bf16[64,2048]{1,0:T(8,128)(2,1)S(1)}, bf16[64,2048]{1,0:T(8,128)(2,1)S(1)}, u32[]{:S(2)}, u32[]{:S(2)}) collective-permute-start(bf16[64,2048]{1,0:T(8,128)(2,1)S(1)} %reshape.16.refs_0_), channel_id=1, source_target_pairs={{0,64},{32,96},{64,0},{96,32},{1,65},{33,97},{65,1},{97,33},{2,66}... | collective-permute-start | bytes 786440 | tf_op jit(solution)/shard_map/ppermute | solution.py:125
  137.6 4.0 %collective-permute-start.5 = (bf16[64,2048]{1,0:T(8,128)(2,1)S(1)}, bf16[64,2048]{1,0:T(8,128)(2,1)S(1)}, u32[]{:S(2)}, u32[]{:S(2)}) collective-permute-start(bf16[64,2048]{1,0:T(8,128)(2,1)S(1)} %reshape.16.refs_0_), channel_id=1, source_target_pairs={{0,96},{32,0},{64,32},{96,64},{1,97},{33,1},{65,33},{97,65},{2,98}... | collective-permute-start | bytes 786440 | tf_op jit(solution)/shard_map/ppermute | solution.py:125
  141.7 0.0 collective-permute-done.3.refs_1_
  141.7 5.5 %collective-permute-done.4.refs_2_ = bf16[64,2048]{1,0:T(8,128)(2,1)S(1)} collective-permute-done((bf16[64,2048]{1,0:T(8,128)(2,1)S(1)}, bf16[64,2048]{1,0:T(8,128)(2,1)S(1)}, u32[]{:S(2)}, u32[]{:S(2)}) %collective-permute-start.4) | collective-permute-done | bytes 262176 | tf_op jit(solution)/shard_map/ppermute | solution.py:125
  147.2 2.8 %collective-permute-done.5.refs_3_ = bf16[64,2048]{1,0:T(8,128)(2,1)S(1)} collective-permute-done((bf16[64,2048]{1,0:T(8,128)(2,1)S(1)}, bf16[64,2048]{1,0:T(8,128)(2,1)S(1)}, u32[]{:S(2)}, u32[]{:S(2)}) %collective-permute-start.5) | collective-permute-done | bytes 262176 | tf_op jit(solution)/shard_map/ppermute | solution.py:125
  150.0 4.4 %shard_map.51 = bf16[416,2048]{1,0:T(8,128)(2,1)} custom-call(s32[1]{0:T(128)} %bitcast.y_ref, bf16[256,416]{1,0:T(8,128)(2,1)S(1)} %all_gather.3.g_ref, bf16[64,2048]{1,0:T(8,128)(2,1)S(1)} %reshape.16.refs_0_, bf16[64,2048]{1,0:T(8,128)(2,1)S(1)} %collective-permute-done.3.refs_1_, bf16[64,2048]{1,0:T(8,128)(2,1)S(1)} %collective-permute-done.4.refs_2_, ...), custom_call_target="tpu_custom_call" | custom-call | flops 446693376 | bytes 2752512 | tf_op jit(solution)/shard_map/pallas_call | solution.py:104
  154.4 5.5 %all-to-all-done = f32[8,2,2048]{2,1,0:T(2,128)S(1)} async-done(((f32[8,2,2048]{2,1,0:T(2,128)}), f32[8,2,2048]{2,1,0:T(2,128)S(1)}, u32[]{:S(2)}, u32[]{:S(2)}) %all-to-all-start) | async-done | bytes 131104 | tf_op jit(solution)/shard_map/all_to_all | solution.py:144
  159.9 0.6 reduce_sum.9
Async XLA Ops:
  7.2 36.7 %copy-start.1 = (bf16[2,2048]{1,0:T(2,128)(2,1)S(1)}, bf16[2,2048]{1,0:T(2,128)(2,1)}, u32[]{:S(2)}) copy-start(bf16[2,2048]{1,0:T(2,128)(2,1)} %param.4) | copy-start | bytes 24580
  20.6 1.5 copy-start
  23.9 39.7 %collective-permute-start = (f32[64,2048]{1,0:T(8,128)S(1)}, f32[64,2048]{1,0:T(8,128)S(1)}, u32[]{:S(2)}, u32[]{:S(2)}) collective-permute-start(f32[64,2048]{1,0:T(8,128)S(1)} %get-tuple-element.7), channel_id=1, source_target_pairs={{0,64},{32,96},{64,0},{96,32},{1,65},{33,97},{65,1},{97,33},{2,66}... | collective-permute-start | bytes 1572872 | tf_op jit(solution)/shard_map/ppermute | solution.py:125
  28.1 35.5 %collective-permute-start.1 = (f32[64,2048]{1,0:T(8,128)S(1)}, f32[64,2048]{1,0:T(8,128)}, u32[]{:S(2)}, u32[]{:S(2)}) collective-permute-start(f32[64,2048]{1,0:T(8,128)S(1)} %get-tuple-element.8), channel_id=1, source_target_pairs={{0,32},{32,64},{64,96},{96,0},{1,33},{33,65},{65,97},{97,1},{2,34}... | collective-permute-start | bytes 1572872 | tf_op jit(solution)/shard_map/ppermute | solution.py:125
  42.0 21.7 %collective-permute-start.2 = (f32[64,2048]{1,0:T(8,128)S(1)}, f32[64,2048]{1,0:T(8,128)}, u32[]{:S(2)}, u32[]{:S(2)}) collective-permute-start(f32[64,2048]{1,0:T(8,128)S(1)} %get-tuple-element.9), channel_id=1, source_target_pairs={{0,96},{32,0},{64,32},{96,64},{1,97},{33,1},{65,33},{97,65},{2,98}... | collective-permute-start | bytes 1572872 | tf_op jit(solution)/shard_map/ppermute | solution.py:125
  44.8 66.6 %all-to-all-start.1 = ((bf16[32,2,2048]{2,1,0:T(2,128)(2,1)}), bf16[32,2,2048]{2,1,0:T(2,128)(2,1)S(1)}, u32[]{:S(2)}, u32[]{:S(2)}) async-start(bf16[32,2,2048]{2,1,0:T(2,128)(2,1)} %broadcast_in_dim.2), calls=%async_computation.2 | async-start | bytes 524288 | tf_op jit(solution)/shard_map/all_to_all | solution.py:134
  63.6 46.1 %reduce-scatter.2.cloned.1.call-start = ((), (), s32[]{:S(2)}) async-start(), calls=%async_computation.3 | async-start | bytes 655360 | tf_op jit(solution)/shard_map/reduce_scatter | solution.py:140
  111.3 48.5 %all-to-all-start = ((f32[8,2,2048]{2,1,0:T(2,128)}), f32[8,2,2048]{2,1,0:T(2,128)S(1)}, u32[]{:S(2)}, u32[]{:S(2)}) async-start(f32[8,2,2048]{2,1,0:T(2,128)} %reshape.15), calls=%async_computation.1 | async-start | bytes 262144 | tf_op jit(solution)/shard_map/all_to_all | solution.py:144
  131.2 10.5 %collective-permute-start.3 = (bf16[64,2048]{1,0:T(8,128)(2,1)S(1)}, bf16[64,2048]{1,0:T(8,128)(2,1)S(1)}, u32[]{:S(2)}, u32[]{:S(2)}) collective-permute-start(bf16[64,2048]{1,0:T(8,128)(2,1)S(1)} %reshape.16.refs_0_), channel_id=1, source_target_pairs={{0,32},{32,64},{64,96},{96,0},{1,33},{33,65},{65,97},{97,1},{2,34}... | collective-permute-start | bytes 786440 | tf_op jit(solution)/shard_map/ppermute | solution.py:125
  134.6 12.6 %collective-permute-start.4 = (bf16[64,2048]{1,0:T(8,128)(2,1)S(1)}, bf16[64,2048]{1,0:T(8,128)(2,1)S(1)}, u32[]{:S(2)}, u32[]{:S(2)}) collective-permute-start(bf16[64,2048]{1,0:T(8,128)(2,1)S(1)} %reshape.16.refs_0_), channel_id=1, source_target_pairs={{0,64},{32,96},{64,0},{96,32},{1,65},{33,97},{65,1},{97,33},{2,66}... | collective-permute-start | bytes 786440 | tf_op jit(solution)/shard_map/ppermute | solution.py:125
  137.6 12.4 %collective-permute-start.5 = (bf16[64,2048]{1,0:T(8,128)(2,1)S(1)}, bf16[64,2048]{1,0:T(8,128)(2,1)S(1)}, u32[]{:S(2)}, u32[]{:S(2)}) collective-permute-start(bf16[64,2048]{1,0:T(8,128)(2,1)S(1)} %reshape.16.refs_0_), channel_id=1, source_target_pairs={{0,96},{32,0},{64,32},{96,64},{1,97},{33,1},{65,33},{97,65},{2,98}... | collective-permute-start | bytes 786440 | tf_op jit(solution)/shard_map/ppermute | solution.py:125
Sparse Core Ops, SparseCore 0:
  68.4 41.2 reduce-scatter.1

commit v2 on v1

--- a/solution.py
+++ b/solution.py
@@ -39,7 +39,7 @@
     return lax.dot_general(a, b, (dims, ((), ())), preferred_element_type=F32)
 
 
-def partial_kernel(y_ref, g_ref, w_ref, *out_refs):
+def partial_kernel(at_ref, g_ref, w_ref, *out_refs):
     tok, ff = g_ref.shape
     g_t = g_ref[...].astype(F32).T
     codes_t = requant(g_t.reshape(ff // MXB, MXB, tok), 1).reshape(ff, tok).astype(BF16)
@@ -47,15 +47,15 @@
     row = lax.broadcasted_iota(jnp.int32, (tok, tok), 0)
     col = lax.broadcasted_iota(jnp.int32, (tok, tok), 1)
     far, rest = row // chunk, row % chunk
-    zl, zh, pair = rest // (2 * ZH), rest % (2 * ZH) // 2, rest % 2
-    source = (far + y_ref[0]) % Y * chunk + (zh * ZL + zl) * 2 + pair
+    near, zh, pair = rest // (2 * ZH), rest % (2 * ZH) // 2, rest % 2
+    source = (far + at_ref[0]) % Y * chunk + (zh * ZL + (near + at_ref[1]) % ZL) * 2 + pair
     order = jnp.where(col == source, 1.0, 0.0).astype(BF16)
     codes = dot(order, codes_t, ((1,), (1,))).astype(BF16)
     for d, out_ref in enumerate(out_refs):
         out_ref[...] = dot(codes[d * chunk : (d + 1) * chunk], w_ref[...], ((1,), (0,)))
 
 
-def partial_sums(y, g, w_t):
+def partial_sums(at, g, w_t):
     tok, ff = g.shape
     feat = w_t.shape[1]
     return pl.pallas_call(
@@ -71,10 +71,10 @@
         cost_estimate=pl.CostEstimate(
             flops=2 * tok * ff * feat, bytes_accessed=2 * ff * feat + 4 * tok * feat, transcendentals=0
         ),
-    )(y, g, w_t)
+    )(at, g, w_t)
 
 
-def weight_kernel(y_ref, g_ref, *refs):
+def weight_kernel(at_ref, g_ref, *refs):
     act_refs, out_ref, toks_ref, ahead_ref = refs[:Y], refs[Y], refs[Y + 1], refs[Y + 2]
     tok, ff = g_ref.shape
     chunk = tok // Y
@@ -85,7 +85,7 @@
         ahead_ref[...] = requant(g, 1).reshape(tok, ff)
         parts = []
         for d in range(Y):
-            start = pl.multiple_of((y_ref[0] + (Y - d)) % Y * chunk, chunk)
+            start = pl.multiple_of((at_ref[0] + (Y - d)) % Y * chunk, chunk)
             parts.append(ahead_ref[pl.ds(start, chunk), :].T)
         toks_ref[...] = jnp.concatenate(parts, axis=1).astype(BF16)
 
@@ -97,7 +97,7 @@
     out_ref[...] = dot(toks_ref[...], jnp.concatenate(acts, axis=0), ((1,), (0,))).astype(BF16)
 
 
-def weight_grad(y, g, acts):
+def weight_grad(at, g, acts):
     tok, ff = g.shape
     feat = acts[0].shape[1]
     tile = feat // 4
@@ -118,15 +118,50 @@
             bytes_accessed=2 * ff * feat + 2 * tok * feat,
             transcendentals=0,
         ),
-    )(y, g, *acts)
+    )(at, g, *acts)
 
 
-def along_y(x, distance):
-    return lax.ppermute(x, "y", [(k, (k + distance) % Y) for k in range(Y)])
+def add_y_kernel(*refs):
+    ins, outs = refs[:Y], refs[Y:]
+    total = (ins[0][...] + ins[1][...]) + (ins[2][...] + ins[3][...])
+    rows = total.shape[0] // ZL
+    for e, out_ref in enumerate(outs):
+        out_ref[...] = total[e * rows : (e + 1) * rows]
+
+
+def add_y(parts):
+    rows, feat = parts[0].shape
+    return pl.pallas_call(
+        add_y_kernel,
+        out_shape=[jax.ShapeDtypeStruct((rows // ZL, feat), F32)] * ZL,
+        compiler_params=pltpu.CompilerParams(vmem_limit_bytes=16 * 2**20),
+        cost_estimate=pl.CostEstimate(flops=4 * rows * feat, bytes_accessed=20 * rows * feat, transcendentals=0),
+    )(*parts)
+
+
+def add_zl_kernel(*refs):
+    ins, out_ref = refs[:ZL], refs[ZL]
+    total = (ins[0][...] + ins[1][...]) + (ins[2][...] + ins[3][...])
+    for h in range(ZH):
+        out_ref[h] = total[2 * h : 2 * h + 2]
+
+
+def add_zl(parts):
+    rows, feat = parts[0].shape
+    return pl.pallas_call(
+        add_zl_kernel,
+        out_shape=jax.ShapeDtypeStruct((ZH, rows // ZH, feat), F32),
+        compiler_params=pltpu.CompilerParams(vmem_limit_bytes=16 * 2**20),
+        cost_estimate=pl.CostEstimate(flops=4 * rows * feat, bytes_accessed=20 * rows * feat, transcendentals=0),
+    )(*parts)
+
+
+def along(x, axis, distance, size):
+    return lax.ppermute(x, axis, [(k, (k + distance) % size) for k in range(size)])
 
 
 def local(grad_out, acts, weight):
-    y = lax.axis_index("y").astype(jnp.int32).reshape(1)
+    at = jnp.stack([lax.axis_index("y"), lax.axis_index("zl")]).astype(jnp.int32)
     z = ZH * ZL
     rows, feat = acts.shape
 
@@ -134,15 +169,14 @@
     z_acts = lax.all_to_all(copies, ("zh", "zl"), 0, 0).reshape(z * rows, feat)
     g = lax.all_gather(grad_out, ("x", "core"), axis=0, tiled=True)
 
-    sums = partial_sums(y, g, weight.T)
-    arrived = [along_y(sums[d], d) for d in (2, 1, 3)]
-    total = sums[0] + arrived[0] + arrived[1] + arrived[2]
-    total = lax.psum_scatter(total, "zl", scatter_dimension=0, tiled=True)
+    sums = partial_sums(at, g, weight.T)
+    pieces = add_y([sums[0]] + [along(sums[d], "y", d, Y) for d in (2, 1, 3)])
+    total = add_zl([pieces[0]] + [along(pieces[e], "zl", e, ZL) for e in (1, 2, 3)])
 
-    all_acts = [z_acts] + [along_y(z_acts, d) for d in (1, 2, 3)]
+    all_acts = [z_acts] + [along(z_acts, "y", d, Y) for d in (1, 2, 3)]
 
-    parts = lax.all_to_all(total.reshape(ZH, rows, feat), "zh", 0, 0)
-    grad_weight = weight_grad(y, g, all_acts).T
+    parts = lax.all_to_all(total, "zh", 0, 0)
+    grad_weight = weight_grad(at, g, all_acts).T
     grad_in = jnp.sum(parts, axis=0).astype(BF16)
     return grad_in, grad_weight
 

time: 168 us -> 151 us (0.90)
  the two profiles are of different devices: /device:TPU:8 before, /device:TPU:88 now
where the time goes in v2:
time: 151 us; the launch traced here: 150 us
  starting transfers between devices  76.2 us (50%)
  waiting for transfers between devices  48 us (32%)
  blocking collectives  13.4 us (9%)
  Pallas kernels  8.17 us (5%)
  local copies, waits for them, and re-layouts  3.09 us (2%)
    all_to_all x1, starting transfers between devices, local(): z_acts = lax.all_to_all(copies, ('zh', 'zl'), 0, 0).reshape(z * rows, feat)  28.1 us
    ppermute x9, starting transfers between devices, along(): lax.ppermute(x, axis, [(k, (k + distance) % size) for k in range(size)])  26.7 us
    ppermute x9, waiting for transfers between devices, along(): lax.ppermute(x, axis, [(k, (k + distance) % size) for k in range(size)])  25.1 us
    all_to_all x1, waiting for transfers between devices, local(): parts = lax.all_to_all(total, 'zh', 0, 0)  22.8 us
    all_to_all x1, starting transfers between devices, local(): parts = lax.all_to_all(total, 'zh', 0, 0)  21.4 us
    all_gather x1, blocking collectives, local(): g = lax.all_gather(grad_out, ('x', 'core'), axis=0, tiled=True)  13.4 us
    pallas_call x1, Pallas kernels, weight_grad(): pl.pallas_call(weight_kernel, out_shape=jax.ShapeDtypeStruct((ff, feat),...  4.92 us
  transfers between devices with their start and end apart: 11, of which 6 were waited for; matrix products, arithmetic and copies ran while one was open for 1% of the time, Pallas kernels for 2%

profile of v2, /device:TPU:88, one launch (start us, length us, event | category | flops | bytes accessed | tf_op | source)
XLA Modules:
  0.0 150.3 jit_solution(5248841800803591459)
XLA Ops:
  0.6 1.5 %broadcast_in_dim.2 = bf16[32,2,2048]{2,1,0:T(2,128)(2,1)} broadcast(bf16[2,2048]{1,0:T(2,128)(2,1)} %param.4), dimensions={1,2} | broadcast | bytes 270336 | tf_op jit(solution)/shard_map/broadcast_in_dim | solution.py:168
  2.2 28.1 %all-to-all-start.1 = ((bf16[32,2,2048]{2,1,0:T(2,128)(2,1)}), bf16[32,2,2048]{2,1,0:T(2,128)(2,1)S(1)}, u32[]{:S(2)}, u32[]{:S(2)}) async-start(bf16[32,2,2048]{2,1,0:T(2,128)(2,1)} %broadcast_in_dim.2), calls=%async_computation.1 | async-start | bytes 524288 | tf_op jit(solution)/shard_map/all_to_all | solution.py:169
  30.3 13.4 %all_gather.3.g_ref = bf16[256,416]{1,0:T(8,128)(2,1)S(1)} all-gather(bf16[32,416]{1,0:T(8,128)(2,1)} %param.3), channel_id=1, replica_groups=mesh['x'=4,'core'=2,'y'=4,'zh'=8,'zl'=4] {'x','core'}, dimensions={0}, use_global_device_ids=true | all-gather | bytes 239616 | tf_op jit(solution)/shard_map/all_gather | solution.py:170
  43.7 0.1 pad_add_fusion.at_ref
  43.8 1.5 copy-done
  45.3 2.5 %shard_map.50 = (f32[64,2048]{1,0:T(8,128)S(1)}, f32[64,2048]{1,0:T(8,128)S(1)}, f32[64,2048]{1,0:T(8,128)S(1)}, f32[64,2048]{1,0:T(8,128)S(1)}) custom-call(s32[2]{0:T(128)S(1)} %pad_add_fusion.at_ref, bf16[256,416]{1,0:T(8,128)(2,1)S(1)} %all_gather.3.g_ref, bf16[416,2048]{1,0:T(8,128)(2,1)S(1)} %bitcast.4), custom_call_target="tpu_custom_call" | custom-call | flops 436207616 | bytes 3801088 | tf_op jit(solution)/shard_map/pallas_call | solution.py:61
  47.7 3.2 %collective-permute-start = (f32[64,2048]{1,0:T(8,128)S(1)}, f32[64,2048]{1,0:T(8,128)S(1)}, u32[]{:S(2)}, u32[]{:S(2)}) collective-permute-start(f32[64,2048]{1,0:T(8,128)S(1)} %get-tuple-element.11), channel_id=1, source_target_pairs={{0,64},{32,96},{64,0},{96,32},{1,65},{33,97},{65,1},{97,33},{2,66}... | collective-permute-start | bytes 1572872 | tf_op jit(solution)/shard_map/ppermute | solution.py:160
  50.9 4.1 %collective-permute-start.1 = (f32[64,2048]{1,0:T(8,128)S(1)}, f32[64,2048]{1,0:T(8,128)S(1)}, u32[]{:S(2)}, u32[]{:S(2)}) collective-permute-start(f32[64,2048]{1,0:T(8,128)S(1)} %get-tuple-element.12), channel_id=1, source_target_pairs={{0,32},{32,64},{64,96},{96,0},{1,33},{33,65},{65,97},{97,1},{2,34}... | collective-permute-start | bytes 1572872 | tf_op jit(solution)/shard_map/ppermute | solution.py:160
  55.0 1.9 %collective-permute-start.2 = (f32[64,2048]{1,0:T(8,128)S(1)}, f32[64,2048]{1,0:T(8,128)S(1)}, u32[]{:S(2)}, u32[]{:S(2)}) collective-permute-start(f32[64,2048]{1,0:T(8,128)S(1)} %get-tuple-element.13), channel_id=1, source_target_pairs={{0,96},{32,0},{64,32},{96,64},{1,97},{33,1},{65,33},{97,65},{2,98}... | collective-permute-start | bytes 1572872 | tf_op jit(solution)/shard_map/ppermute | solution.py:160
  56.9 9.0 %collective-permute-done.refs_1_ = f32[64,2048]{1,0:T(8,128)S(1)} collective-permute-done((f32[64,2048]{1,0:T(8,128)S(1)}, f32[64,2048]{1,0:T(8,128)S(1)}, u32[]{:S(2)}, u32[]{:S(2)}) %collective-permute-start) | collective-permute-done | bytes 524320 | tf_op jit(solution)/shard_map/ppermute | solution.py:160
  65.9 8.2 %collective-permute-done.1.refs_2_ = f32[64,2048]{1,0:T(8,128)S(1)} collective-permute-done((f32[64,2048]{1,0:T(8,128)S(1)}, f32[64,2048]{1,0:T(8,128)S(1)}, u32[]{:S(2)}, u32[]{:S(2)}) %collective-permute-start.1) | collective-permute-done | bytes 524320 | tf_op jit(solution)/shard_map/ppermute | solution.py:160
  74.1 2.4 %collective-permute-done.2.refs_3_ = f32[64,2048]{1,0:T(8,128)S(1)} collective-permute-done((f32[64,2048]{1,0:T(8,128)S(1)}, f32[64,2048]{1,0:T(8,128)S(1)}, u32[]{:S(2)}, u32[]{:S(2)}) %collective-permute-start.2) | collective-permute-done | bytes 524320 | tf_op jit(solution)/shard_map/ppermute | solution.py:160
  76.5 0.1 shard_map.51
  76.6 3.4 %collective-permute-start.3 = (f32[16,2048]{1,0:T(8,128)S(1)}, f32[16,2048]{1,0:T(8,128)S(1)}, u32[]{:S(2)}, u32[]{:S(2)}) collective-permute-start(f32[16,2048]{1,0:T(8,128)S(1)} %get-tuple-element.15), channel_id=1, source_target_pairs={{0,1},{1,2},{2,3},{3,0},{4,5},{5,6},{6,7},{7,4},{8,9},{9,10},{10,1... | collective-permute-start | bytes 393224 | tf_op jit(solution)/shard_map/ppermute | solution.py:160
  80.0 2.5 %collective-permute-start.4 = (f32[16,2048]{1,0:T(8,128)S(1)}, f32[16,2048]{1,0:T(8,128)S(1)}, u32[]{:S(2)}, u32[]{:S(2)}) collective-permute-start(f32[16,2048]{1,0:T(8,128)S(1)} %get-tuple-element.16), channel_id=1, source_target_pairs={{0,2},{1,3},{2,0},{3,1},{4,6},{5,7},{6,4},{7,5},{8,10},{9,11},{10,... | collective-permute-start | bytes 393224 | tf_op jit(solution)/shard_map/ppermute | solution.py:160
  82.5 3.0 %collective-permute-start.5 = (f32[16,2048]{1,0:T(8,128)S(1)}, f32[16,2048]{1,0:T(8,128)S(1)}, u32[]{:S(2)}, u32[]{:S(2)}) collective-permute-start(f32[16,2048]{1,0:T(8,128)S(1)} %get-tuple-element.17), channel_id=1, source_target_pairs={{0,3},{1,0},{2,1},{3,2},{4,7},{5,4},{6,5},{7,6},{8,11},{9,8},{10,9... | collective-permute-start | bytes 393224 | tf_op jit(solution)/shard_map/ppermute | solution.py:160
  85.6 0.0 collective-permute-done.3.refs_1_
  85.6 3.4 %collective-permute-done.4.refs_2_ = f32[16,2048]{1,0:T(8,128)S(1)} collective-permute-done((f32[16,2048]{1,0:T(8,128)S(1)}, f32[16,2048]{1,0:T(8,128)S(1)}, u32[]{:S(2)}, u32[]{:S(2)}) %collective-permute-start.4) | collective-permute-done | bytes 131104 | tf_op jit(solution)/shard_map/ppermute | solution.py:160
  89.0 2.1 %collective-permute-done.5.refs_3_ = f32[16,2048]{1,0:T(8,128)S(1)} collective-permute-done((f32[16,2048]{1,0:T(8,128)S(1)}, f32[16,2048]{1,0:T(8,128)S(1)}, u32[]{:S(2)}, u32[]{:S(2)}) %collective-permute-start.5) | collective-permute-done | bytes 131104 | tf_op jit(solution)/shard_map/ppermute | solution.py:160
  91.1 0.7 shard_map.52
  91.8 0.0 all-to-all-done.1
  91.8 21.4 %all-to-all-start = ((f32[8,2,2048]{2,1,0:T(2,128)}), f32[8,2,2048]{2,1,0:T(2,128)S(1)}, u32[]{:S(2)}, u32[]{:S(2)}) async-start(f32[8,2,2048]{2,1,0:T(2,128)} %shard_map.52), calls=%async_computation | async-start | bytes 262144 | tf_op jit(solution)/shard_map/all_to_all | solution.py:178
  113.2 0.1 reshape.8.refs_0_
  113.3 2.1 %collective-permute-start.6 = (bf16[64,2048]{1,0:T(8,128)(2,1)S(1)}, bf16[64,2048]{1,0:T(8,128)(2,1)S(1)}, u32[]{:S(2)}, u32[]{:S(2)}) collective-permute-start(bf16[64,2048]{1,0:T(8,128)(2,1)S(1)} %reshape.8.refs_0_), channel_id=1, source_target_pairs={{0,32},{32,64},{64,96},{96,0},{1,33},{33,65},{65,97},{97,1},{2,34}... | collective-permute-start | bytes 786440 | tf_op jit(solution)/shard_map/ppermute | solution.py:160
  115.4 4.5 %collective-permute-start.7 = (bf16[64,2048]{1,0:T(8,128)(2,1)S(1)}, bf16[64,2048]{1,0:T(8,128)(2,1)S(1)}, u32[]{:S(2)}, u32[]{:S(2)}) collective-permute-start(bf16[64,2048]{1,0:T(8,128)(2,1)S(1)} %reshape.8.refs_0_), channel_id=1, source_target_pairs={{0,64},{32,96},{64,0},{96,32},{1,65},{33,97},{65,1},{97,33},{2,66}... | collective-permute-start | bytes 786440 | tf_op jit(solution)/shard_map/ppermute | solution.py:160
  120.0 1.9 %collective-permute-start.8 = (bf16[64,2048]{1,0:T(8,128)(2,1)S(1)}, bf16[64,2048]{1,0:T(8,128)(2,1)S(1)}, u32[]{:S(2)}, u32[]{:S(2)}) collective-permute-start(bf16[64,2048]{1,0:T(8,128)(2,1)S(1)} %reshape.8.refs_0_), channel_id=1, source_target_pairs={{0,96},{32,0},{64,32},{96,64},{1,97},{33,1},{65,33},{97,65},{2,98}... | collective-permute-start | bytes 786440 | tf_op jit(solution)/shard_map/ppermute | solution.py:160
  121.9 22.8 %all-to-all-done = f32[8,2,2048]{2,1,0:T(2,128)S(1)} async-done(((f32[8,2,2048]{2,1,0:T(2,128)}), f32[8,2,2048]{2,1,0:T(2,128)S(1)}, u32[]{:S(2)}, u32[]{:S(2)}) %all-to-all-start) | async-done | bytes 131104 | tf_op jit(solution)/shard_map/all_to_all | solution.py:178
  144.7 0.6 reduce_sum.9
  145.4 0.0 collective-permute-done.6.refs_1_
  145.4 0.0 collective-permute-done.7.refs_2_
  145.4 0.0 collective-permute-done.8.refs_3_
  145.4 4.9 %shard_map.53 = bf16[416,2048]{1,0:T(8,128)(2,1)} custom-call(s32[2]{0:T(128)S(1)} %pad_add_fusion.at_ref, bf16[256,416]{1,0:T(8,128)(2,1)S(1)} %all_gather.3.g_ref, bf16[64,2048]{1,0:T(8,128)(2,1)S(1)} %reshape.8.refs_0_, bf16[64,2048]{1,0:T(8,128)(2,1)S(1)} %collective-permute-done.6.refs_1_, bf16[64,2048]{1,0:T(8,128)(2,1)S(1)} %collective-permute-done.7.refs_2_, ...), custom_call_target="tpu_custom_call" | custom-call | flops 446693376 | bytes 2752512 | tf_op jit(solution)/shard_map/pallas_call | solution.py:104
  (1 shorter events, 0.0 us)
Async XLA Ops:
  2.2 89.6 %all-to-all-start.1 = ((bf16[32,2,2048]{2,1,0:T(2,128)(2,1)}), bf16[32,2,2048]{2,1,0:T(2,128)(2,1)S(1)}, u32[]{:S(2)}, u32[]{:S(2)}) async-start(bf16[32,2,2048]{2,1,0:T(2,128)(2,1)} %broadcast_in_dim.2), calls=%async_computation.1 | async-start | bytes 524288 | tf_op jit(solution)/shard_map/all_to_all | solution.py:169
  43.8 1.5 copy-start
  47.7 18.2 %collective-permute-start = (f32[64,2048]{1,0:T(8,128)S(1)}, f32[64,2048]{1,0:T(8,128)S(1)}, u32[]{:S(2)}, u32[]{:S(2)}) collective-permute-start(f32[64,2048]{1,0:T(8,128)S(1)} %get-tuple-element.11), channel_id=1, source_target_pairs={{0,64},{32,96},{64,0},{96,32},{1,65},{33,97},{65,1},{97,33},{2,66}... | collective-permute-start | bytes 1572872 | tf_op jit(solution)/shard_map/ppermute | solution.py:160
  50.9 23.2 %collective-permute-start.1 = (f32[64,2048]{1,0:T(8,128)S(1)}, f32[64,2048]{1,0:T(8,128)S(1)}, u32[]{:S(2)}, u32[]{:S(2)}) collective-permute-start(f32[64,2048]{1,0:T(8,128)S(1)} %get-tuple-element.12), channel_id=1, source_target_pairs={{0,32},{32,64},{64,96},{96,0},{1,33},{33,65},{65,97},{97,1},{2,34}... | collective-permute-start | bytes 1572872 | tf_op jit(solution)/shard_map/ppermute | solution.py:160
  55.0 21.5 %collective-permute-start.2 = (f32[64,2048]{1,0:T(8,128)S(1)}, f32[64,2048]{1,0:T(8,128)S(1)}, u32[]{:S(2)}, u32[]{:S(2)}) collective-permute-start(f32[64,2048]{1,0:T(8,128)S(1)} %get-tuple-element.13), channel_id=1, source_target_pairs={{0,96},{32,0},{64,32},{96,64},{1,97},{33,1},{65,33},{97,65},{2,98}... | collective-permute-start | bytes 1572872 | tf_op jit(solution)/shard_map/ppermute | solution.py:160
  76.6 8.9 %collective-permute-start.3 = (f32[16,2048]{1,0:T(8,128)S(1)}, f32[16,2048]{1,0:T(8,128)S(1)}, u32[]{:S(2)}, u32[]{:S(2)}) collective-permute-start(f32[16,2048]{1,0:T(8,128)S(1)} %get-tuple-element.15), channel_id=1, source_target_pairs={{0,1},{1,2},{2,3},{3,0},{4,5},{5,6},{6,7},{7,4},{8,9},{9,10},{10,1... | collective-permute-start | bytes 393224 | tf_op jit(solution)/shard_map/ppermute | solution.py:160
  80.0 8.9 %collective-permute-start.4 = (f32[16,2048]{1,0:T(8,128)S(1)}, f32[16,2048]{1,0:T(8,128)S(1)}, u32[]{:S(2)}, u32[]{:S(2)}) collective-permute-start(f32[16,2048]{1,0:T(8,128)S(1)} %get-tuple-element.16), channel_id=1, source_target_pairs={{0,2},{1,3},{2,0},{3,1},{4,6},{5,7},{6,4},{7,5},{8,10},{9,11},{10,... | collective-permute-start | bytes 393224 | tf_op jit(solution)/shard_map/ppermute | solution.py:160
  82.5 8.6 %collective-permute-start.5 = (f32[16,2048]{1,0:T(8,128)S(1)}, f32[16,2048]{1,0:T(8,128)S(1)}, u32[]{:S(2)}, u32[]{:S(2)}) collective-permute-start(f32[16,2048]{1,0:T(8,128)S(1)} %get-tuple-element.17), channel_id=1, source_target_pairs={{0,3},{1,0},{2,1},{3,2},{4,7},{5,4},{6,5},{7,6},{8,11},{9,8},{10,9... | collective-permute-start | bytes 393224 | tf_op jit(solution)/shard_map/ppermute | solution.py:160
  91.8 52.9 %all-to-all-start = ((f32[8,2,2048]{2,1,0:T(2,128)}), f32[8,2,2048]{2,1,0:T(2,128)S(1)}, u32[]{:S(2)}, u32[]{:S(2)}) async-start(f32[8,2,2048]{2,1,0:T(2,128)} %shard_map.52), calls=%async_computation | async-start | bytes 262144 | tf_op jit(solution)/shard_map/all_to_all | solution.py:178
  113.3 32.1 %collective-permute-start.6 = (bf16[64,2048]{1,0:T(8,128)(2,1)S(1)}, bf16[64,2048]{1,0:T(8,128)(2,1)S(1)}, u32[]{:S(2)}, u32[]{:S(2)}) collective-permute-start(bf16[64,2048]{1,0:T(8,128)(2,1)S(1)} %reshape.8.refs_0_), channel_id=1, source_target_pairs={{0,32},{32,64},{64,96},{96,0},{1,33},{33,65},{65,97},{97,1},{2,34}... | collective-permute-start | bytes 786440 | tf_op jit(solution)/shard_map/ppermute | solution.py:160
  115.4 29.9 %collective-permute-start.7 = (bf16[64,2048]{1,0:T(8,128)(2,1)S(1)}, bf16[64,2048]{1,0:T(8,128)(2,1)S(1)}, u32[]{:S(2)}, u32[]{:S(2)}) collective-permute-start(bf16[64,2048]{1,0:T(8,128)(2,1)S(1)} %reshape.8.refs_0_), channel_id=1, source_target_pairs={{0,64},{32,96},{64,0},{96,32},{1,65},{33,97},{65,1},{97,33},{2,66}... | collective-permute-start | bytes 786440 | tf_op jit(solution)/shard_map/ppermute | solution.py:160
  120.0 25.4 %collective-permute-start.8 = (bf16[64,2048]{1,0:T(8,128)(2,1)S(1)}, bf16[64,2048]{1,0:T(8,128)(2,1)S(1)}, u32[]{:S(2)}, u32[]{:S(2)}) collective-permute-start(bf16[64,2048]{1,0:T(8,128)(2,1)S(1)} %reshape.8.refs_0_), channel_id=1, source_target_pairs={{0,96},{32,0},{64,32},{96,64},{1,97},{33,1},{65,33},{97,65},{2,98}... | collective-permute-start | bytes 786440 | tf_op jit(solution)/shard_map/ppermute | solution.py:160

commit v3 on v2

v3 whole, which is shorter than its diff:
```python
import jax
import jax.numpy as jnp
from jax import lax
from jax.experimental import pallas as pl
from jax.experimental.pallas import tpu as pltpu
from jax.sharding import Mesh
from jax.sharding import PartitionSpec as P

MXB = 32
CODE_LIMIT = 448.0
PEAK_FLOOR = 0.25
Y, ZH, ZL = 4, 8, 4
LANES = 128
SPAN = 125.0
F32 = jnp.float32
BF16 = jnp.bfloat16


def block_scale(peaks):
    scale = jnp.full_like(peaks, 2.0 ** (-10))
    for power in range(-1, 8):
        scale = jnp.where(peaks >= 2.0**power, 2.0 ** (power - 8), scale)
    return scale


def requant(blocks, axis):
    peaks = jnp.maximum(jnp.max(jnp.abs(blocks), axis=axis, keepdims=True), PEAK_FLOOR)
    scale = block_scale(peaks)
    limit = CODE_LIMIT * scale
    held = jnp.minimum(jnp.maximum(blocks, -limit), limit) * (1.0 + 2.0**-12)
    wide = held * (2.0**20 + 1.0)
    normal = wide - (wide - held)
    anchor = (1.5 * 2.0**14) * scale
    small = (held + anchor) - anchor
    return jnp.where(jnp.abs(blocks) < 2.0**-6 * scale, small, normal)


def dot(a, b, dims):
    return lax.dot_general(a, b, (dims, ((), ())), preferred_element_type=F32)


def encode(values):
    top = jnp.max(jnp.abs(values), axis=1, keepdims=True)
    top = (jnp.maximum(top, 2.0**-90) * (1.0 + 2.0**-7)).astype(BF16)
    step = (2.0 * SPAN) / top.astype(F32)
    level = jnp.exp2(jnp.abs(values) * step - SPAN)
    codes = jnp.where(values < 0.0, -level, level).astype(BF16)
    return codes, jnp.broadcast_to(top, (values.shape[0], LANES))


def decode(codes, top):
    code = codes.astype(F32)
    step = top[:, :1].astype(F32) * (1.0 / (2.0 * SPAN))
    magnitude = (jnp.log2(jnp.abs(code)) + SPAN) * step
    return jnp.where(code < 0.0, -magnitude, magnitude)


def decoded_sum(in_refs):
    feat = in_refs[0].shape[1] - LANES
    parts = [decode(in_ref[:, :feat], in_ref[:, feat:]) for in_ref in in_refs]
    return (parts[0] + parts[1]) + (parts[2] + parts[3])


def partial_kernel(at_ref, g_ref, w_hbm, *refs):
    out_refs, w_ref, sem = refs[:Y], refs[Y], refs[Y + 1]
    copy = pltpu.make_async_copy(w_hbm, w_ref, sem)
    copy.start()
    tok, ff = g_ref.shape
    feat = w_ref.shape[1]
    g_t = g_ref[...].astype(F32).T
    codes_t = requant(g_t.reshape(ff // MXB, MXB, tok), 1).reshape(ff, tok).astype(BF16)
    chunk = tok // Y
    row = lax.broadcasted_iota(jnp.int32, (tok, tok), 0)
    col = lax.broadcasted_iota(jnp.int32, (tok, tok), 1)
    far, rest = row // chunk, row % chunk
    near, zh, pair = rest // (2 * ZH), rest % (2 * ZH) // 2, rest % 2
    source = (far + at_ref[0]) % Y * chunk + (zh * ZL + (near + at_ref[1]) % ZL) * 2 + pair
    order = jnp.where(col == source, 1.0, 0.0).astype(BF16)
    held = dot(order, codes_t, ((1,), (1,))).astype(BF16)
    copy.wait()
    for d, out_ref in enumerate(out_refs):
        codes, top = encode(dot(held[d * chunk : (d + 1) * chunk], w_ref[...], ((1,), (0,))))
        out_ref[:, :feat] = codes
        out_ref[:, feat:] = top


def partial_sums(at, g, w_t):
    tok, ff = g.shape
    feat = w_t.shape[1]
    return pl.pallas_call(
        partial_kernel,
        out_shape=[jax.ShapeDtypeStruct((tok // Y, feat + LANES), BF16)] * Y,
        in_specs=[
            pl.BlockSpec(memory_space=pltpu.SMEM),
            pl.BlockSpec(memory_space=pltpu.VMEM),
            pl.BlockSpec(memory_space=pltpu.HBM),
        ],
        out_specs=[pl.BlockSpec(memory_space=pltpu.VMEM)] * Y,
        scratch_shapes=[pltpu.VMEM((ff, feat), BF16), pltpu.SemaphoreType.DMA],
        compiler_params=pltpu.CompilerParams(vmem_limit_bytes=58 * 2**20),
        cost_estimate=pl.CostEstimate(
            flops=2 * tok * ff * feat, bytes_accessed=2 * ff * feat + 2 * tok * feat, transcendentals=tok * feat
        ),
    )(at, g, w_t)


def add_y_kernel(*refs):
    feat = refs[0].shape[1] - LANES
    rows = refs[Y].shape[0]
    codes, top = encode(decoded_sum(refs[:Y]))
    for e, out_ref in enumerate(refs[Y:]):
        out_ref[:, :feat] = codes[e * rows : (e + 1) * rows]
        out_ref[:, feat:] = top[e * rows : (e + 1) * rows]


def add_zl_kernel(*refs):
    total = decoded_sum(refs[:ZL])
    for k in range(ZH):
        refs[ZL][k] = total[2 * k : 2 * k + 2]


def add_call(kernel, parts, out_shape):
    size = len(parts) * parts[0].size
    return pl.pallas_call(
        kernel,
        out_shape=out_shape,
        compiler_params=pltpu.CompilerParams(vmem_limit_bytes=16 * 2**20),
        cost_estimate=pl.CostEstimate(flops=10 * size, bytes_accessed=4 * size, transcendentals=size),
    )(*parts)


def weight_kernel(at_ref, g_ref, *refs):
    act_refs, (out_ref, done_ref, toks_ref, ahead_ref) = refs[:Y], refs[Y:]
    tok, ff = g_ref.shape
    chunk = tok // Y

    @pl.when(pl.program_id(0) == 0)
    def _():
        g = g_ref[...].astype(F32).reshape(tok // MXB, MXB, ff)
        ahead_ref[...] = requant(g, 1).reshape(tok, ff)
        parts = []
        for d in range(Y):
            start = pl.multiple_of((at_ref[0] + (Y - d)) % Y * chunk, chunk)
            parts.append(ahead_ref[pl.ds(start, chunk), :].T)
        toks_ref[...] = jnp.concatenate(parts, axis=1).astype(BF16)
        done_ref[...] = jnp.zeros_like(done_ref)

    acts = []
    for act_ref in act_refs:
        a = act_ref[...].astype(F32)
        width = a.shape[1]
        acts.append(requant(a.reshape(chunk // MXB, MXB, width), 1).reshape(chunk, width).astype(BF16))
    out_ref[...] = dot(toks_ref[...], jnp.concatenate(acts, axis=0), ((1,), (0,))).astype(BF16)


def weight_grad(at, g, acts):
    tok, ff = g.shape
    feat = acts[0].shape[1]
    tile = feat // 4
    return pl.pallas_call(
        weight_kernel,
        out_shape=[jax.ShapeDtypeStruct((ff, feat), BF16), jax.ShapeDtypeStruct((8, LANES), F32)],
        grid=(feat // tile,),
        in_specs=[
            pl.BlockSpec(memory_space=pltpu.SMEM),
            pl.BlockSpec((tok, ff), lambda i: (0, 0)),
        ]
        + [pl.BlockSpec((tok // Y, tile), lambda i: (0, i))] * Y,
        out_specs=[pl.BlockSpec((ff, tile), lambda i: (0, i)), pl.BlockSpec((8, LANES), lambda i: (0, 0))],
        scratch_shapes=[pltpu.VMEM((ff, tok), BF16), pltpu.VMEM((tok, ff), F32)],
        compiler_params=pltpu.CompilerParams(vmem_limit_bytes=32 * 2**20),
        cost_estimate=pl.CostEstimate(
            flops=2 * tok * ff * feat + 20 * tok * feat,
            bytes_accessed=2 * ff * feat + 2 * tok * feat,
            transcendentals=0,
        ),
    )(at, g, *acts)


def add_zh_kernel(in_ref, done_ref, out_ref):
    total = in_ref[0]
    for k in range(1, ZH):
        total = total + in_ref[k]
    out_ref[...] = total.astype(BF16)


def add_zh(parts, done):
    return pl.pallas_call(
        add_zh_kernel,
        out_shape=jax.ShapeDtypeStruct(parts.shape[1:], BF16),
        compiler_params=pltpu.CompilerParams(vmem_limit_bytes=16 * 2**20),
        cost_estimate=pl.CostEstimate(flops=parts.size, bytes_accessed=4 * parts.size, transcendentals=0),
    )(parts, done)


def along(x, axis, distance, size):
    return lax.ppermute(x, axis, [(k, (k + distance) % size) for k in range(size)])


def local(grad_out, acts, weight):
    at = jnp.stack([lax.axis_index("y"), lax.axis_index("zl")]).astype(jnp.int32)
    rows, feat = acts.shape
    z = ZH * ZL

    copies = jnp.broadcast_to(acts[None], (z, rows, feat))
    z_acts = lax.all_to_all(copies, ("zh", "zl"), 0, 0).reshape(z * rows, feat)
    g = lax.all_gather(grad_out, ("x", "core"), axis=0, tiled=True)

    sums = partial_sums(at, g, weight.T)
    sums = [sums[0]] + [along(sums[d], "y", d, Y) for d in (2, 1, 3)]
    sums = add_call(add_y_kernel, sums, [jax.ShapeDtypeStruct((ZH * rows, feat + LANES), BF16)] * ZL)
    sums = [sums[0]] + [along(sums[e], "zl", e, ZL) for e in (1, 2, 3)]
    sums = add_call(add_zl_kernel, sums, jax.ShapeDtypeStruct((ZH, rows, feat), F32))

    all_acts = [z_acts] + [along(z_acts, "y", d, Y) for d in (1, 2, 3)]
    sums = lax.all_to_all(sums, "zh", 0, 0)
    grad_weight_t, done = weight_grad(at, g, all_acts)
    return add_zh(sums, done), grad_weight_t.T


def solution(mesh):
    fine = Mesh(mesh.devices.reshape(4, 2, Y, ZH, ZL), ("x", "core", "y", "zh", "zl"))
    row, col = ("x", "core"), ("y", "zh", "zl")
    return jax.shard_map(
        local,
        mesh=fine,
        in_specs=(P(row, col), P(col, row), P(row, col)),
        out_specs=(P(col, row), P(row, col)),
        check_vma=False,
    )
```

time: 151 us -> 136 us (0.901)
  the two profiles are of different devices: /device:TPU:88 before, /device:TPU:8 now
where the time goes in v3:
time: 136 us
  starting transfers between devices  80.7 us (59%)
  waiting for transfers between devices  24.1 us (18%)
  blocking collectives  14.5 us (11%)
  Pallas kernels  12.3 us (9%)
  local copies, waits for them, and re-layouts  2.6 us (2%)
    ppermute x9, starting transfers between devices, along(): lax.ppermute(x, axis, [(k, (k + distance) % size) for k in range(size)])  32.3 us
    all_to_all x1, starting transfers between devices, local(): z_acts = lax.all_to_all(copies, ('zh', 'zl'), 0, 0).reshape(z * rows, feat)  28.7 us
    all_to_all x1, starting transfers between devices, local(): sums = lax.all_to_all(sums, 'zh', 0, 0)  19.7 us
    ppermute x9, waiting for transfers between devices, along(): lax.ppermute(x, axis, [(k, (k + distance) % size) for k in range(size)])  19 us
    all_gather x1, blocking collectives, local(): g = lax.all_gather(grad_out, ('x', 'core'), axis=0, tiled=True)  14.5 us
    all_to_all x1, waiting for transfers between devices, local(): sums = lax.all_to_all(sums, 'zh', 0, 0)  5.16 us
    pallas_call x1, Pallas kernels, partial_sums(): pl.pallas_call(partial_kernel, out_shape=[jax.ShapeDtypeStruct((tok // Y,...  4.96 us
    pallas_call x1, Pallas kernels, weight_grad(): pl.pallas_call(weight_kernel, out_shape=[jax.ShapeDtypeStruct((ff, feat),...  4.9 us
  transfers between devices with their start and end apart: 11, of which 6 were waited for; matrix products, arithmetic and copies ran while one was open for 1% of the time, Pallas kernels for 9%

profile of v3, /device:TPU:8, one launch (start us, length us, event | category | flops | bytes accessed | tf_op | source)
XLA Modules:
  0.0 135.6 jit_solution(12850764964094174568)
XLA Ops:
  0.6 1.5 %broadcast_in_dim.2 = bf16[32,2,2048]{2,1,0:T(2,128)(2,1)} broadcast(bf16[2,2048]{1,0:T(2,128)(2,1)} %param.4), dimensions={1,2} | broadcast | bytes 270336 | tf_op jit(solution)/shard_map/broadcast_in_dim | solution.py:205
  2.2 28.7 %all-to-all-start.1 = ((bf16[32,2,2048]{2,1,0:T(2,128)(2,1)}), bf16[32,2,2048]{2,1,0:T(2,128)(2,1)S(1)}, u32[]{:S(2)}, u32[]{:S(2)}) async-start(bf16[32,2,2048]{2,1,0:T(2,128)(2,1)} %broadcast_in_dim.2), calls=%async_computation.1 | async-start | bytes 524288 | tf_op jit(solution)/shard_map/all_to_all | solution.py:206
  30.9 14.5 %all_gather.3.g_ref = bf16[256,416]{1,0:T(8,128)(2,1)} all-gather(bf16[32,416]{1,0:T(8,128)(2,1)} %param.3), channel_id=1, replica_groups=mesh['x'=4,'core'=2,'y'=4,'zh'=8,'zl'=4] {'x','core'}, dimensions={0}, use_global_device_ids=true | all-gather | bytes 239616 | tf_op jit(solution)/shard_map/all_gather | solution.py:207
  45.4 0.6 pad_add_fusion.at_ref
  46.0 5.0 %shard_map.50 = (bf16[64,2176]{1,0:T(8,128)(2,1)}, bf16[64,2176]{1,0:T(8,128)(2,1)}, bf16[64,2176]{1,0:T(8,128)(2,1)}, bf16[64,2176]{1,0:T(8,128)(2,1)}) custom-call(s32[2]{0:T(128)} %pad_add_fusion.at_ref, bf16[256,416]{1,0:T(8,128)(2,1)} %all_gather.3.g_ref, bf16[416,2048]{1,0:T(8,128)(2,1)} %bitcast.4), custom_call_target="tpu_custom_call" | custom-call | flops 436207616 | bytes 2752512 | tf_op jit(solution)/shard_map/pallas_call | solution.py:90
  51.0 4.2 %collective-permute-start = (bf16[64,2176]{1,0:T(8,128)(2,1)}, bf16[64,2176]{1,0:T(8,128)(2,1)S(1)}, u32[]{:S(2)}, u32[]{:S(2)}) collective-permute-start(bf16[64,2176]{1,0:T(8,128)(2,1)} %get-tuple-element.13), channel_id=1, source_target_pairs={{0,64},{32,96},{64,0},{96,32},{1,65},{33,97},{65,1},{97,33},{2,66}... | collective-permute-start | bytes 835592 | tf_op jit(solution)/shard_map/ppermute | solution.py:197
  55.2 1.9 %collective-permute-start.1 = (bf16[64,2176]{1,0:T(8,128)(2,1)}, bf16[64,2176]{1,0:T(8,128)(2,1)S(1)}, u32[]{:S(2)}, u32[]{:S(2)}) collective-permute-start(bf16[64,2176]{1,0:T(8,128)(2,1)} %get-tuple-element.14), channel_id=1, source_target_pairs={{0,32},{32,64},{64,96},{96,0},{1,33},{33,65},{65,97},{97,1},{2,34}... | collective-permute-start | bytes 835592 | tf_op jit(solution)/shard_map/ppermute | solution.py:197
  57.1 3.9 %collective-permute-start.2 = (bf16[64,2176]{1,0:T(8,128)(2,1)}, bf16[64,2176]{1,0:T(8,128)(2,1)S(1)}, u32[]{:S(2)}, u32[]{:S(2)}) collective-permute-start(bf16[64,2176]{1,0:T(8,128)(2,1)} %get-tuple-element.15), channel_id=1, source_target_pairs={{0,96},{32,0},{64,32},{96,64},{1,97},{33,1},{65,33},{97,65},{2,98}... | collective-permute-start | bytes 835592 | tf_op jit(solution)/shard_map/ppermute | solution.py:197
  61.0 2.6 %collective-permute-done.refs_1_ = bf16[64,2176]{1,0:T(8,128)(2,1)S(1)} collective-permute-done((bf16[64,2176]{1,0:T(8,128)(2,1)}, bf16[64,2176]{1,0:T(8,128)(2,1)S(1)}, u32[]{:S(2)}, u32[]{:S(2)}) %collective-permute-start) | collective-permute-done | bytes 278560 | tf_op jit(solution)/shard_map/ppermute | solution.py:197
  63.6 6.0 %collective-permute-done.1.refs_2_ = bf16[64,2176]{1,0:T(8,128)(2,1)S(1)} collective-permute-done((bf16[64,2176]{1,0:T(8,128)(2,1)}, bf16[64,2176]{1,0:T(8,128)(2,1)S(1)}, u32[]{:S(2)}, u32[]{:S(2)}) %collective-permute-start.1) | collective-permute-done | bytes 278560 | tf_op jit(solution)/shard_map/ppermute | solution.py:197
  69.6 0.0 collective-permute-done.2.refs_3_
  69.6 1.0 copy-done.1
  70.6 0.9 shard_map.51
  71.4 3.7 %collective-permute-start.3 = (bf16[16,2176]{1,0:T(8,128)(2,1)S(1)}, bf16[16,2176]{1,0:T(8,128)(2,1)S(1)}, u32[]{:S(2)}, u32[]{:S(2)}) collective-permute-start(bf16[16,2176]{1,0:T(8,128)(2,1)S(1)} %get-tuple-element.17), channel_id=1, source_target_pairs={{0,1},{1,2},{2,3},{3,0},{4,5},{5,6},{6,7},{7,4},{8,9},{9,10},{10,1... | collective-permute-start | bytes 208904 | tf_op jit(solution)/shard_map/ppermute | solution.py:197
  75.1 4.3 %collective-permute-start.4 = (bf16[16,2176]{1,0:T(8,128)(2,1)S(1)}, bf16[16,2176]{1,0:T(8,128)(2,1)S(1)}, u32[]{:S(2)}, u32[]{:S(2)}) collective-permute-start(bf16[16,2176]{1,0:T(8,128)(2,1)S(1)} %get-tuple-element.18), channel_id=1, source_target_pairs={{0,2},{1,3},{2,0},{3,1},{4,6},{5,7},{6,4},{7,5},{8,10},{9,11},{10,... | collective-permute-start | bytes 208904 | tf_op jit(solution)/shard_map/ppermute | solution.py:197
  79.4 3.4 %collective-permute-start.5 = (bf16[16,2176]{1,0:T(8,128)(2,1)S(1)}, bf16[16,2176]{1,0:T(8,128)(2,1)S(1)}, u32[]{:S(2)}, u32[]{:S(2)}) collective-permute-start(bf16[16,2176]{1,0:T(8,128)(2,1)S(1)} %get-tuple-element.19), channel_id=1, source_target_pairs={{0,3},{1,0},{2,1},{3,2},{4,7},{5,4},{6,5},{7,6},{8,11},{9,8},{10,9... | collective-permute-start | bytes 208904 | tf_op jit(solution)/shard_map/ppermute | solution.py:197
  82.8 0.0 collective-permute-done.3.refs_1_
  82.8 0.0 collective-permute-done.4.refs_2_
  82.8 2.8 %collective-permute-done.5.refs_3_ = bf16[16,2176]{1,0:T(8,128)(2,1)S(1)} collective-permute-done((bf16[16,2176]{1,0:T(8,128)(2,1)S(1)}, bf16[16,2176]{1,0:T(8,128)(2,1)S(1)}, u32[]{:S(2)}, u32[]{:S(2)}) %collective-permute-start.5) | collective-permute-done | bytes 69664 | tf_op jit(solution)/shard_map/ppermute | solution.py:197
  85.6 0.9 shard_map.52
  86.6 0.0 all-to-all-done.1
  86.6 19.7 %all-to-all-start = ((f32[8,2,2048]{2,1,0:T(2,128)}), f32[8,2,2048]{2,1,0:T(2,128)S(1)}, u32[]{:S(2)}, u32[]{:S(2)}) async-start(f32[8,2,2048]{2,1,0:T(2,128)} %shard_map.52), calls=%async_computation | async-start | bytes 262144 | tf_op jit(solution)/shard_map/all_to_all | solution.py:216
  106.2 0.1 reshape.8.refs_0_
  106.3 2.5 %collective-permute-start.8 = (bf16[64,2048]{1,0:T(8,128)(2,1)S(1)}, bf16[64,2048]{1,0:T(8,128)(2,1)S(1)}, u32[]{:S(2)}, u32[]{:S(2)}) collective-permute-start(bf16[64,2048]{1,0:T(8,128)(2,1)S(1)} %reshape.8.refs_0_), channel_id=1, source_target_pairs={{0,96},{32,0},{64,32},{96,64},{1,97},{33,1},{65,33},{97,65},{2,98}... | collective-permute-start | bytes 786440 | tf_op jit(solution)/shard_map/ppermute | solution.py:197
  108.9 4.2 %collective-permute-start.7 = (bf16[64,2048]{1,0:T(8,128)(2,1)S(1)}, bf16[64,2048]{1,0:T(8,128)(2,1)S(1)}, u32[]{:S(2)}, u32[]{:S(2)}) collective-permute-start(bf16[64,2048]{1,0:T(8,128)(2,1)S(1)} %reshape.8.refs_0_), channel_id=1, source_target_pairs={{0,64},{32,96},{64,0},{96,32},{1,65},{33,97},{65,1},{97,33},{2,66}... | collective-permute-start | bytes 786440 | tf_op jit(solution)/shard_map/ppermute | solution.py:197
  113.1 4.2 %collective-permute-start.6 = (bf16[64,2048]{1,0:T(8,128)(2,1)S(1)}, bf16[64,2048]{1,0:T(8,128)(2,1)S(1)}, u32[]{:S(2)}, u32[]{:S(2)}) collective-permute-start(bf16[64,2048]{1,0:T(8,128)(2,1)S(1)} %reshape.8.refs_0_), channel_id=1, source_target_pairs={{0,32},{32,64},{64,96},{96,0},{1,33},{33,65},{65,97},{97,1},{2,34}... | collective-permute-start | bytes 786440 | tf_op jit(solution)/shard_map/ppermute | solution.py:197
  117.3 0.0 collective-permute-done.8.refs_3_
  117.3 4.7 %collective-permute-done.7.refs_2_ = bf16[64,2048]{1,0:T(8,128)(2,1)S(1)} collective-permute-done((bf16[64,2048]{1,0:T(8,128)(2,1)S(1)}, bf16[64,2048]{1,0:T(8,128)(2,1)S(1)}, u32[]{:S(2)}, u32[]{:S(2)}) %collective-permute-start.7) | collective-permute-done | bytes 262176 | tf_op jit(solution)/shard_map/ppermute | solution.py:197
  122.0 2.8 %collective-permute-done.6.refs_1_ = bf16[64,2048]{1,0:T(8,128)(2,1)S(1)} collective-permute-done((bf16[64,2048]{1,0:T(8,128)(2,1)S(1)}, bf16[64,2048]{1,0:T(8,128)(2,1)S(1)}, u32[]{:S(2)}, u32[]{:S(2)}) %collective-permute-start.6) | collective-permute-done | bytes 262176 | tf_op jit(solution)/shard_map/ppermute | solution.py:197
  124.9 4.9 %shard_map.53 = (bf16[416,2048]{1,0:T(8,128)(2,1)}, f32[8,128]{1,0:T(8,128)S(1)}) custom-call(s32[2]{0:T(128)S(1)} %copy-done.2, bf16[256,416]{1,0:T(8,128)(2,1)S(1)} %copy-done, bf16[64,2048]{1,0:T(8,128)(2,1)S(1)} %reshape.8.refs_0_, bf16[64,2048]{1,0:T(8,128)(2,1)S(1)} %collective-permute-done.6.refs_1_, ...), custom_call_target="tpu_custom_call" | custom-call | flops 446693376 | bytes 2752512 | tf_op jit(solution)/shard_map/pallas_call | solution.py:160
  129.8 5.2 %all-to-all-done.in_ref = f32[8,2,2048]{2,1,0:T(2,128)S(1)} async-done(((f32[8,2,2048]{2,1,0:T(2,128)}), f32[8,2,2048]{2,1,0:T(2,128)S(1)}, u32[]{:S(2)}, u32[]{:S(2)}) %all-to-all-start) | async-done | bytes 131104 | tf_op jit(solution)/shard_map/all_to_all | solution.py:216
  134.9 0.6 shard_map.54
  (5 shorter events, 0.0 us)
Async XLA Ops:
  2.2 84.4 %all-to-all-start.1 = ((bf16[32,2,2048]{2,1,0:T(2,128)(2,1)}), bf16[32,2,2048]{2,1,0:T(2,128)(2,1)S(1)}, u32[]{:S(2)}, u32[]{:S(2)}) async-start(bf16[32,2,2048]{2,1,0:T(2,128)(2,1)} %broadcast_in_dim.2), calls=%async_computation.1 | async-start | bytes 524288 | tf_op jit(solution)/shard_map/all_to_all | solution.py:206
  46.0 78.9 %copy-start = (bf16[256,416]{1,0:T(8,128)(2,1)S(1)}, bf16[256,416]{1,0:T(8,128)(2,1)}, u32[]{:S(2)}) copy-start(bf16[256,416]{1,0:T(8,128)(2,1)} %all_gather.3.g_ref) | copy-start | bytes 638980
  46.0 78.9 %copy-start.2 = (s32[2]{0:T(128)S(1)}, s32[2]{0:T(128)}, u32[]{:S(2)}) copy-start(s32[2]{0:T(128)} %pad_add_fusion.at_ref) | copy-start | bytes 28
  51.0 12.7 %collective-permute-start = (bf16[64,2176]{1,0:T(8,128)(2,1)}, bf16[64,2176]{1,0:T(8,128)(2,1)S(1)}, u32[]{:S(2)}, u32[]{:S(2)}) collective-permute-start(bf16[64,2176]{1,0:T(8,128)(2,1)} %get-tuple-element.13), channel_id=1, source_target_pairs={{0,64},{32,96},{64,0},{96,32},{1,65},{33,97},{65,1},{97,33},{2,66}... | collective-permute-start | bytes 835592 | tf_op jit(solution)/shard_map/ppermute | solution.py:197
  55.2 14.4 %collective-permute-start.1 = (bf16[64,2176]{1,0:T(8,128)(2,1)}, bf16[64,2176]{1,0:T(8,128)(2,1)S(1)}, u32[]{:S(2)}, u32[]{:S(2)}) collective-permute-start(bf16[64,2176]{1,0:T(8,128)(2,1)} %get-tuple-element.14), channel_id=1, source_target_pairs={{0,32},{32,64},{64,96},{96,0},{1,33},{33,65},{65,97},{97,1},{2,34}... | collective-permute-start | bytes 835592 | tf_op jit(solution)/shard_map/ppermute | solution.py:197
  57.1 12.5 %collective-permute-start.2 = (bf16[64,2176]{1,0:T(8,128)(2,1)}, bf16[64,2176]{1,0:T(8,128)(2,1)S(1)}, u32[]{:S(2)}, u32[]{:S(2)}) collective-permute-start(bf16[64,2176]{1,0:T(8,128)(2,1)} %get-tuple-element.15), channel_id=1, source_target_pairs={{0,96},{32,0},{64,32},{96,64},{1,97},{33,1},{65,33},{97,65},{2,98}... | collective-permute-start | bytes 835592 | tf_op jit(solution)/shard_map/ppermute | solution.py:197
  69.6 1.0 copy-start.1
  71.4 11.4 %collective-permute-start.3 = (bf16[16,2176]{1,0:T(8,128)(2,1)S(1)}, bf16[16,2176]{1,0:T(8,128)(2,1)S(1)}, u32[]{:S(2)}, u32[]{:S(2)}) collective-permute-start(bf16[16,2176]{1,0:T(8,128)(2,1)S(1)} %get-tuple-element.17), channel_id=1, source_target_pairs={{0,1},{1,2},{2,3},{3,0},{4,5},{5,6},{6,7},{7,4},{8,9},{9,10},{10,1... | collective-permute-start | bytes 208904 | tf_op jit(solution)/shard_map/ppermute | solution.py:197
  75.1 7.7 %collective-permute-start.4 = (bf16[16,2176]{1,0:T(8,128)(2,1)S(1)}, bf16[16,2176]{1,0:T(8,128)(2,1)S(1)}, u32[]{:S(2)}, u32[]{:S(2)}) collective-permute-start(bf16[16,2176]{1,0:T(8,128)(2,1)S(1)} %get-tuple-element.18), channel_id=1, source_target_pairs={{0,2},{1,3},{2,0},{3,1},{4,6},{5,7},{6,4},{7,5},{8,10},{9,11},{10,... | collective-permute-start | bytes 208904 | tf_op jit(solution)/shard_map/ppermute | solution.py:197
  79.4 6.2 %collective-permute-start.5 = (bf16[16,2176]{1,0:T(8,128)(2,1)S(1)}, bf16[16,2176]{1,0:T(8,128)(2,1)S(1)}, u32[]{:S(2)}, u32[]{:S(2)}) collective-permute-start(bf16[16,2176]{1,0:T(8,128)(2,1)S(1)} %get-tuple-element.19), channel_id=1, source_target_pairs={{0,3},{1,0},{2,1},{3,2},{4,7},{5,4},{6,5},{7,6},{8,11},{9,8},{10,9... | collective-permute-start | bytes 208904 | tf_op jit(solution)/shard_map/ppermute | solution.py:197
  86.6 48.4 %all-to-all-start = ((f32[8,2,2048]{2,1,0:T(2,128)}), f32[8,2,2048]{2,1,0:T(2,128)S(1)}, u32[]{:S(2)}, u32[]{:S(2)}) async-start(f32[8,2,2048]{2,1,0:T(2,128)} %shard_map.52), calls=%async_computation | async-start | bytes 262144 | tf_op jit(solution)/shard_map/all_to_all | solution.py:216
  106.3 11.0 %collective-permute-start.8 = (bf16[64,2048]{1,0:T(8,128)(2,1)S(1)}, bf16[64,2048]{1,0:T(8,128)(2,1)S(1)}, u32[]{:S(2)}, u32[]{:S(2)}) collective-permute-start(bf16[64,2048]{1,0:T(8,128)(2,1)S(1)} %reshape.8.refs_0_), channel_id=1, source_target_pairs={{0,96},{32,0},{64,32},{96,64},{1,97},{33,1},{65,33},{97,65},{2,98}... | collective-permute-start | bytes 786440 | tf_op jit(solution)/shard_map/ppermute | solution.py:197
  108.9 13.2 %collective-permute-start.7 = (bf16[64,2048]{1,0:T(8,128)(2,1)S(1)}, bf16[64,2048]{1,0:T(8,128)(2,1)S(1)}, u32[]{:S(2)}, u32[]{:S(2)}) collective-permute-start(bf16[64,2048]{1,0:T(8,128)(2,1)S(1)} %reshape.8.refs_0_), channel_id=1, source_target_pairs={{0,64},{32,96},{64,0},{96,32},{1,65},{33,97},{65,1},{97,33},{2,66}... | collective-permute-start | bytes 786440 | tf_op jit(solution)/shard_map/ppermute | solution.py:197
  113.1 11.8 %collective-permute-start.6 = (bf16[64,2048]{1,0:T(8,128)(2,1)S(1)}, bf16[64,2048]{1,0:T(8,128)(2,1)S(1)}, u32[]{:S(2)}, u32[]{:S(2)}) collective-permute-start(bf16[64,2048]{1,0:T(8,128)(2,1)S(1)} %reshape.8.refs_0_), channel_id=1, source_target_pairs={{0,32},{32,64},{64,96},{96,0},{1,33},{33,65},{65,97},{97,1},{2,34}... | collective-permute-start | bytes 786440 | tf_op jit(solution)/shard_map/ppermute | solution.py:197

commit v4 on v3

v4 whole, which is shorter than its diff:
```python
import jax
import jax.numpy as jnp
from jax import lax
from jax.experimental import pallas as pl
from jax.experimental.pallas import tpu as pltpu
from jax.sharding import Mesh
from jax.sharding import PartitionSpec as P

MXB = 32
CODE_LIMIT = 448.0
PEAK_FLOOR = 0.25
Y, ZH, ZM, Z0 = 4, 8, 2, 2
ZL = ZM * Z0
Z16 = ZH * ZM
LANES = 128
SPAN = 125.0
F32 = jnp.float32
BF16 = jnp.bfloat16


def block_scale(peaks):
    scale = jnp.full_like(peaks, 2.0 ** (-10))
    for power in range(-1, 8):
        scale = jnp.where(peaks >= 2.0**power, 2.0 ** (power - 8), scale)
    return scale


def requant(blocks, axis):
    peaks = jnp.maximum(jnp.max(jnp.abs(blocks), axis=axis, keepdims=True), PEAK_FLOOR)
    scale = block_scale(peaks)
    limit = CODE_LIMIT * scale
    held = jnp.minimum(jnp.maximum(blocks, -limit), limit) * (1.0 + 2.0**-12)
    wide = held * (2.0**20 + 1.0)
    normal = wide - (wide - held)
    anchor = (1.5 * 2.0**14) * scale
    small = (held + anchor) - anchor
    return jnp.where(jnp.abs(blocks) < 2.0**-6 * scale, small, normal)


def dot(a, b, dims):
    return lax.dot_general(a, b, (dims, ((), ())), preferred_element_type=F32)


def encode(values):
    top = jnp.max(jnp.abs(values), axis=1, keepdims=True)
    top = (jnp.maximum(top, 2.0**-90) * (1.0 + 2.0**-7)).astype(BF16)
    step = (2.0 * SPAN) / top.astype(F32)
    level = jnp.exp2(jnp.abs(values) * step - SPAN)
    codes = jnp.where(values < 0.0, -level, level).astype(BF16)
    return codes, jnp.broadcast_to(top, (values.shape[0], LANES))


def decode(codes, top):
    code = codes.astype(F32)
    step = top[:, :1].astype(F32) * (1.0 / (2.0 * SPAN))
    magnitude = (jnp.log2(jnp.abs(code)) + SPAN) * step
    return jnp.where(code < 0.0, -magnitude, magnitude)


def decoded_sum(in_ref):
    feat = in_ref.shape[2] - LANES
    total = decode(in_ref[0, :, :feat], in_ref[0, :, feat:])
    for k in range(1, in_ref.shape[0]):
        total = total + decode(in_ref[k, :, :feat], in_ref[k, :, feat:])
    return total


def partial_kernel(g_ref, w_hbm, out_ref, w_ref, sem):
    copy = pltpu.make_async_copy(w_hbm, w_ref, sem)
    copy.start()
    tok, ff = g_ref.shape
    feat = w_ref.shape[1]
    g_t = g_ref[...].astype(F32).T
    codes_t = requant(g_t.reshape(ff // MXB, MXB, tok), 1).reshape(ff, tok).astype(BF16)
    row = lax.broadcasted_iota(jnp.int32, (tok, tok), 0)
    col = lax.broadcasted_iota(jnp.int32, (tok, tok), 1)
    rows = tok // (Y * Z0)
    place, rest = row // rows, row % rows
    source = place // Z0 * (rows * Z0) + (rest // 2 * Z0 + place % Z0) * 2 + rest % 2
    order = jnp.where(col == source, 1.0, 0.0).astype(BF16)
    held = dot(order, codes_t, ((1,), (1,))).astype(BF16)
    copy.wait()
    for k in range(Y * Z0):
        codes, top = encode(dot(held[k * rows : (k + 1) * rows], w_ref[...], ((1,), (0,))))
        out_ref[k, :, :feat] = codes
        out_ref[k, :, feat:] = top


def partial_sums(g, w_t):
    tok, ff = g.shape
    feat = w_t.shape[1]
    return pl.pallas_call(
        partial_kernel,
        out_shape=jax.ShapeDtypeStruct((Y * Z0, tok // (Y * Z0), feat + LANES), BF16),
        in_specs=[pl.BlockSpec(memory_space=pltpu.VMEM), pl.BlockSpec(memory_space=pltpu.HBM)],
        out_specs=pl.BlockSpec(memory_space=pltpu.VMEM),
        scratch_shapes=[pltpu.VMEM((ff, feat), BF16), pltpu.SemaphoreType.DMA],
        compiler_params=pltpu.CompilerParams(vmem_limit_bytes=58 * 2**20),
        cost_estimate=pl.CostEstimate(
            flops=2 * tok * ff * feat, bytes_accessed=2 * ff * feat + 2 * tok * feat, transcendentals=tok * feat
        ),
    )(g, w_t)


def add_near_kernel(in_ref, *refs):
    act_refs, (out_ref, acts_ref) = refs[:ZL], refs[ZL:]
    feat = in_ref.shape[2] - LANES
    codes, top = encode(decoded_sum(in_ref))
    for k in range(Z16):
        out_ref[k, :, :feat] = codes[2 * k : 2 * k + 2]
        out_ref[k, :, feat:] = top[2 * k : 2 * k + 2]
    acts_ref[...] = jnp.concatenate([act_ref[...] for act_ref in act_refs], axis=0)


def add_near(parts, acts):
    places, rows, wide = parts.shape
    return pl.pallas_call(
        add_near_kernel,
        out_shape=[
            jax.ShapeDtypeStruct((Z16, rows // Z16, wide), BF16),
            jax.ShapeDtypeStruct((ZL * acts[0].shape[0], acts[0].shape[1]), BF16),
        ],
        compiler_params=pltpu.CompilerParams(vmem_limit_bytes=16 * 2**20),
        cost_estimate=pl.CostEstimate(flops=10 * parts.size, bytes_accessed=2 * parts.size, transcendentals=parts.size),
    )(parts, *acts)


def add_far_kernel(in_ref, done_ref, out_ref):
    out_ref[...] = decoded_sum(in_ref).astype(BF16)


def add_far(parts, done):
    places, rows, wide = parts.shape
    return pl.pallas_call(
        add_far_kernel,
        out_shape=jax.ShapeDtypeStruct((rows, wide - LANES), BF16),
        compiler_params=pltpu.CompilerParams(vmem_limit_bytes=16 * 2**20),
        cost_estimate=pl.CostEstimate(flops=10 * parts.size, bytes_accessed=2 * parts.size, transcendentals=parts.size),
    )(parts, done)


def weight_kernel(at_ref, g_ref, *refs):
    act_refs, (out_ref, done_ref, toks_ref) = refs[:Y], refs[Y:]
    tok, ff = g_ref.shape
    chunk = tok // Y

    @pl.when(pl.program_id(0) == 0)
    def _():
        g = requant(g_ref[...].astype(F32).reshape(tok // MXB, MXB, ff), 1).reshape(tok, ff).astype(BF16)
        row = lax.broadcasted_iota(jnp.int32, (tok, tok), 0)
        col = lax.broadcasted_iota(jnp.int32, (tok, tok), 1)
        far, rest = col // chunk, col % chunk
        near, zh, pair = rest // (2 * ZH), rest % (2 * ZH) // 2, rest % 2
        y, zl = (at_ref[0] + Y - far) % Y, (at_ref[1] + ZL - near) % ZL
        order = jnp.where(row == y * chunk + (zh * ZL + zl) * 2 + pair, 1.0, 0.0).astype(BF16)
        toks_ref[...] = dot(g, order, ((0,), (0,))).astype(BF16)
        done_ref[...] = jnp.zeros_like(done_ref)

    acts = []
    for act_ref in act_refs:
        a = act_ref[...].astype(F32)
        width = a.shape[1]
        blocks = a.reshape(ZL, 2 * ZH // 8, 8, width)
        for_blocks = [requant(blocks[:, b].reshape(MXB, width), 0).reshape(ZL, 8, width) for b in range(2 * ZH // 8)]
        acts.append(jnp.stack(for_blocks, axis=1).reshape(chunk, width).astype(BF16))
    out_ref[...] = dot(toks_ref[...], jnp.concatenate(acts, axis=0), ((1,), (0,))).astype(BF16)


def weight_grad(at, g, acts):
    tok, ff = g.shape
    feat = acts[0].shape[1]
    tile = feat // 4
    return pl.pallas_call(
        weight_kernel,
        out_shape=[jax.ShapeDtypeStruct((ff, feat), BF16), jax.ShapeDtypeStruct((8, LANES), F32)],
        grid=(feat // tile,),
        in_specs=[
            pl.BlockSpec(memory_space=pltpu.SMEM),
            pl.BlockSpec((tok, ff), lambda i: (0, 0)),
        ]
        + [pl.BlockSpec((tok // Y, tile), lambda i: (0, i))] * Y,
        out_specs=[pl.BlockSpec((ff, tile), lambda i: (0, i)), pl.BlockSpec((8, LANES), lambda i: (0, 0))],
        scratch_shapes=[pltpu.VMEM((ff, tok), BF16)],
        compiler_params=pltpu.CompilerParams(vmem_limit_bytes=32 * 2**20),
        cost_estimate=pl.CostEstimate(
            flops=2 * tok * ff * feat + 20 * tok * feat,
            bytes_accessed=2 * ff * feat + 2 * tok * feat,
            transcendentals=0,
        ),
    )(at, g, *acts)


def along(x, axis, distance, size):
    return lax.ppermute(x, axis, [(k, (k + distance) % size) for k in range(size)])


def local(grad_out, acts, weight):
    rows, feat = acts.shape
    near = lax.axis_index("zm") * Z0 + lax.axis_index("z0")
    at = jnp.stack([lax.axis_index("y"), near]).astype(jnp.int32)

    copies = jnp.broadcast_to(acts[None], (ZH, rows, feat))
    zh_acts = lax.all_to_all(copies, "zh", 0, 0).reshape(ZH * rows, feat)
    g = lax.all_gather(grad_out, ("x", "core"), axis=0, tiled=True)

    sums = lax.all_to_all(partial_sums(g, weight.T), ("y", "z0"), 0, 0)
    near_acts = [zh_acts] + [along(zh_acts, ("zm", "z0"), e, ZL) for e in (1, 2, 3)]
    sums, z_acts = add_near(sums, near_acts)
    sums = lax.all_to_all(sums, ("zh", "zm"), 0, 0)
    all_acts = [z_acts] + [along(z_acts, "y", d, Y) for d in (1, 2, 3)]
    grad_weight_t, done = weight_grad(at, g, all_acts)
    return add_far(sums, done), grad_weight_t.T


def solution(mesh):
    fine = Mesh(mesh.devices.reshape(4, 2, Y, ZH, ZM, Z0), ("x", "core", "y", "zh", "zm", "z0"))
    row, col = ("x", "core"), ("y", "zh", "zm", "z0")
    return jax.shard_map(
        local,
        mesh=fine,
        in_specs=(P(row, col), P(col, row), P(row, col)),
        out_specs=(P(col, row), P(row, col)),
        check_vma=False,
    )
```

time: 136 us -> 129 us (0.949)
  the two profiles are of different devices: /device:TPU:8 before, /device:TPU:1 now
where the time goes in v4:
time: 129 us
  starting transfers between devices  74.7 us (58%)
  waiting for transfers between devices  24.2 us (19%)
  blocking collectives  15.2 us (12%)
  Pallas kernels  12.6 us (10%)
  local copies, waits for them, and re-layouts  1.39 us (1%)
    all_to_all x1, starting transfers between devices, local(): zh_acts = lax.all_to_all(copies, 'zh', 0, 0).reshape(ZH * rows, feat)  28.9 us
    all_to_all x1, starting transfers between devices, local(): sums = lax.all_to_all(sums, ('zh', 'zm'), 0, 0)  23.6 us
    ppermute x6, waiting for transfers between devices, along(): lax.ppermute(x, axis, [(k, (k + distance) % size) for k in range(size)])  18.3 us
    ppermute x6, starting transfers between devices, along(): lax.ppermute(x, axis, [(k, (k + distance) % size) for k in range(size)])  17.6 us
    all_gather x1, blocking collectives, local(): g = lax.all_gather(grad_out, ('x', 'core'), axis=0, tiled=True)  15.2 us
    pallas_call x1, Pallas kernels, partial_sums(): pl.pallas_call(partial_kernel, out_shape=jax.ShapeDtypeStruct((Y * Z0, to...  5.64 us
    pallas_call x1, Pallas kernels, weight_grad(): pl.pallas_call(weight_kernel, out_shape=[jax.ShapeDtypeStruct((ff, feat),...  4.69 us
    all_to_all x1, waiting for transfers between devices, local(): sums = lax.all_to_all(sums, ('zh', 'zm'), 0, 0)  4.56 us
  transfers between devices with their start and end apart: 9, of which 6 were waited for; matrix products, arithmetic and copies ran while one was open for 0% of the time, Pallas kernels for 8%

profile of v4, /device:TPU:1, one launch (start us, length us, event | category | flops | bytes accessed | tf_op | source)
XLA Modules:
  0.0 128.9 jit_solution(11343423833304411138)
XLA Ops:
  0.6 1.4 %broadcast_in_dim.2 = bf16[8,2,2048]{2,1,0:T(2,128)(2,1)} broadcast(bf16[2,2048]{1,0:T(2,128)(2,1)} %param.4), dimensions={1,2} | broadcast | bytes 73728 | tf_op jit(solution)/shard_map/broadcast_in_dim | solution.py:202
  2.0 28.9 %all-to-all-start.1 = ((bf16[8,2,2048]{2,1,0:T(2,128)(2,1)}), bf16[8,2,2048]{2,1,0:T(2,128)(2,1)S(1)}, u32[]{:S(2)}, u32[]{:S(2)}) async-start(bf16[8,2,2048]{2,1,0:T(2,128)(2,1)} %broadcast_in_dim.2), calls=%async_computation.1 | async-start | bytes 131072 | tf_op jit(solution)/shard_map/all_to_all | solution.py:203
  30.9 15.2 %all_gather.3.g_ref = bf16[256,416]{1,0:T(8,128)(2,1)} all-gather(bf16[32,416]{1,0:T(8,128)(2,1)} %param.3), channel_id=1, replica_groups=mesh['x'=4,'core'=2,'y'=4,'zh'=8,'zm'=2,'z0'=2] {'x','core'}, dimensions={0}, use_global_device_ids=true | all-gather | bytes 239616 | tf_op jit(solution)/shard_map/all_gather | solution.py:204
  46.1 5.6 %shard_map.50 = bf16[8,32,2176]{2,1,0:T(8,128)(2,1)} custom-call(bf16[256,416]{1,0:T(8,128)(2,1)} %all_gather.3.g_ref, bf16[416,2048]{1,0:T(8,128)(2,1)} %bitcast.4), custom_call_target="tpu_custom_call" | custom-call | flops 436207616 | bytes 2752512 | tf_op jit(solution)/shard_map/pallas_call | solution.py:92
  51.8 0.0 copy-start
  51.8 1.3 %all-to-all-done.1 = bf16[8,2,2048]{2,1,0:T(2,128)(2,1)S(1)} async-done(((bf16[8,2,2048]{2,1,0:T(2,128)(2,1)}), bf16[8,2,2048]{2,1,0:T(2,128)(2,1)S(1)}, u32[]{:S(2)}, u32[]{:S(2)}) %all-to-all-start.1) | async-done | bytes 65568 | tf_op jit(solution)/shard_map/all_to_all | solution.py:203
  53.1 4.5 %all-to-all-start = ((bf16[8,32,2176]{2,1,0:T(8,128)(2,1)}), bf16[8,32,2176]{2,1,0:T(8,128)(2,1)S(1)}, u32[]{:S(2)}, u32[]{:S(2)}) async-start(bf16[8,32,2176]{2,1,0:T(8,128)(2,1)} %shard_map.50), calls=%async_computation | async-start | bytes 2228224 | tf_op jit(solution)/shard_map/all_to_all | solution.py:206
  57.7 4.4 %collective-permute-start.2 = (bf16[16,2048]{1,0:T(8,128)(2,1)S(1)}, bf16[16,2048]{1,0:T(8,128)(2,1)S(1)}, u32[]{:S(2)}, u32[]{:S(2)}) collective-permute-start(bf16[16,2048]{1,0:T(8,128)(2,1)S(1)} %reshape.8.refs_0_), channel_id=1, source_target_pairs={{0,3},{1,0},{2,1},{3,2},{4,7},{5,4},{6,5},{7,6},{8,11},{9,8},{10,9... | collective-permute-start | bytes 196616 | tf_op jit(solution)/shard_map/ppermute | solution.py:194
  62.1 2.1 %collective-permute-start.1 = (bf16[16,2048]{1,0:T(8,128)(2,1)S(1)}, bf16[16,2048]{1,0:T(8,128)(2,1)S(1)}, u32[]{:S(2)}, u32[]{:S(2)}) collective-permute-start(bf16[16,2048]{1,0:T(8,128)(2,1)S(1)} %reshape.8.refs_0_), channel_id=1, source_target_pairs={{0,2},{1,3},{2,0},{3,1},{4,6},{5,7},{6,4},{7,5},{8,10},{9,11},{10,... | collective-permute-start | bytes 196616 | tf_op jit(solution)/shard_map/ppermute | solution.py:194
  64.2 2.1 %collective-permute-start = (bf16[16,2048]{1,0:T(8,128)(2,1)S(1)}, bf16[16,2048]{1,0:T(8,128)(2,1)S(1)}, u32[]{:S(2)}, u32[]{:S(2)}) collective-permute-start(bf16[16,2048]{1,0:T(8,128)(2,1)S(1)} %reshape.8.refs_0_), channel_id=1, source_target_pairs={{0,1},{1,2},{2,3},{3,0},{4,5},{5,6},{6,7},{7,4},{8,9},{9,10},{10,1... | collective-permute-start | bytes 196616 | tf_op jit(solution)/shard_map/ppermute | solution.py:194
  66.2 4.6 %collective-permute-done.2.refs_3_ = bf16[16,2048]{1,0:T(8,128)(2,1)S(1)} collective-permute-done((bf16[16,2048]{1,0:T(8,128)(2,1)S(1)}, bf16[16,2048]{1,0:T(8,128)(2,1)S(1)}, u32[]{:S(2)}, u32[]{:S(2)}) %collective-permute-start.2) | collective-permute-done | bytes 65568 | tf_op jit(solution)/shard_map/ppermute | solution.py:194
  70.8 0.0 collective-permute-done.1.refs_2_
  70.8 3.0 %collective-permute-done.refs_1_ = bf16[16,2048]{1,0:T(8,128)(2,1)S(1)} collective-permute-done((bf16[16,2048]{1,0:T(8,128)(2,1)S(1)}, bf16[16,2048]{1,0:T(8,128)(2,1)S(1)}, u32[]{:S(2)}, u32[]{:S(2)}) %collective-permute-start) | collective-permute-done | bytes 65568 | tf_op jit(solution)/shard_map/ppermute | solution.py:194
  73.8 0.0 all-to-all-done.in_ref
  73.8 1.5 %shard_map.51 = (bf16[16,2,2176]{2,1,0:T(2,128)(2,1)}, bf16[64,2048]{1,0:T(8,128)(2,1)S(1)}) custom-call(bf16[8,32,2176]{2,1,0:T(8,128)(2,1)S(1)} %all-to-all-done.in_ref, bf16[16,2048]{1,0:T(8,128)(2,1)S(1)} %reshape.8.refs_0_, bf16[16,2048]{1,0:T(8,128)(2,1)S(1)} %collective-permute-done.refs_1_, bf16[16,2048]{1,0:T(8,128)(2,1)S(1)} %collective-permute-done.1.refs_2_, ...), custom_call_target="tpu_custom_call" | custom-call | flops 5570560 | bytes 1114112 | tf_op jit(solution)/shard_map/pallas_call | solution.py:117
  75.3 23.6 %all-to-all-start.2 = ((bf16[16,2,2176]{2,1,0:T(2,128)(2,1)}), bf16[16,2,2176]{2,1,0:T(2,128)(2,1)S(1)}, u32[]{:S(2)}, u32[]{:S(2)}) async-start(bf16[16,2,2176]{2,1,0:T(2,128)(2,1)} %get-tuple-element.6), calls=%async_computation.2 | async-start | bytes 278528 | tf_op jit(solution)/shard_map/all_to_all | solution.py:209
  98.9 3.7 %collective-permute-start.5 = (bf16[64,2048]{1,0:T(8,128)(2,1)S(1)}, bf16[64,2048]{1,0:T(8,128)(2,1)S(1)}, u32[]{:S(2)}, u32[]{:S(2)}) collective-permute-start(bf16[64,2048]{1,0:T(8,128)(2,1)S(1)} %get-tuple-element.7.refs_0_), channel_id=1, source_target_pairs={{0,96},{32,0},{64,32},{96,64},{1,97},{33,1},{65,33},{97,65},{2,98}... | collective-permute-start | bytes 786440 | tf_op jit(solution)/shard_map/ppermute | solution.py:194
  102.7 2.6 %collective-permute-start.4 = (bf16[64,2048]{1,0:T(8,128)(2,1)S(1)}, bf16[64,2048]{1,0:T(8,128)(2,1)S(1)}, u32[]{:S(2)}, u32[]{:S(2)}) collective-permute-start(bf16[64,2048]{1,0:T(8,128)(2,1)S(1)} %get-tuple-element.7.refs_0_), channel_id=1, source_target_pairs={{0,64},{32,96},{64,0},{96,32},{1,65},{33,97},{65,1},{97,33},{2,66}... | collective-permute-start | bytes 786440 | tf_op jit(solution)/shard_map/ppermute | solution.py:194
  105.3 2.8 %collective-permute-start.3 = (bf16[64,2048]{1,0:T(8,128)(2,1)S(1)}, bf16[64,2048]{1,0:T(8,128)(2,1)S(1)}, u32[]{:S(2)}, u32[]{:S(2)}) collective-permute-start(bf16[64,2048]{1,0:T(8,128)(2,1)S(1)} %get-tuple-element.7.refs_0_), channel_id=1, source_target_pairs={{0,32},{32,64},{64,96},{96,0},{1,33},{33,65},{65,97},{97,1},{2,34}... | collective-permute-start | bytes 786440 | tf_op jit(solution)/shard_map/ppermute | solution.py:194
  108.1 0.1 pad_add_fusion.at_ref
  108.2 0.0 collective-permute-done.5.refs_3_
  108.2 3.6 %collective-permute-done.4.refs_2_ = bf16[64,2048]{1,0:T(8,128)(2,1)S(1)} collective-permute-done((bf16[64,2048]{1,0:T(8,128)(2,1)S(1)}, bf16[64,2048]{1,0:T(8,128)(2,1)S(1)}, u32[]{:S(2)}, u32[]{:S(2)}) %collective-permute-start.4) | collective-permute-done | bytes 262176 | tf_op jit(solution)/shard_map/ppermute | solution.py:194
  111.7 7.2 %collective-permute-done.3.refs_1_ = bf16[64,2048]{1,0:T(8,128)(2,1)S(1)} collective-permute-done((bf16[64,2048]{1,0:T(8,128)(2,1)S(1)}, bf16[64,2048]{1,0:T(8,128)(2,1)S(1)}, u32[]{:S(2)}, u32[]{:S(2)}) %collective-permute-start.3) | collective-permute-done | bytes 262176 | tf_op jit(solution)/shard_map/ppermute | solution.py:194
  118.9 0.0 copy-done
  118.9 4.7 %shard_map.52 = (bf16[416,2048]{1,0:T(8,128)(2,1)}, f32[8,128]{1,0:T(8,128)S(1)}) custom-call(s32[2]{0:T(128)S(1)} %pad_add_fusion.at_ref, bf16[256,416]{1,0:T(8,128)(2,1)S(1)} %copy-done, bf16[64,2048]{1,0:T(8,128)(2,1)S(1)} %get-tuple-element.7.refs_0_, bf16[64,2048]{1,0:T(8,128)(2,1)S(1)} %collective-permute-done.3.refs_1_, ...), custom_call_target="tpu_custom_call" | custom-call | flops 446693376 | bytes 2752512 | tf_op jit(solution)/shard_map/pallas_call | solution.py:173
  123.6 4.6 %all-to-all-done.2.in_ref = bf16[16,2,2176]{2,1,0:T(2,128)(2,1)S(1)} async-done(((bf16[16,2,2176]{2,1,0:T(2,128)(2,1)}), bf16[16,2,2176]{2,1,0:T(2,128)(2,1)S(1)}, u32[]{:S(2)}, u32[]{:S(2)}) %all-to-all-start.2) | async-done | bytes 139296 | tf_op jit(solution)/shard_map/all_to_all | solution.py:209
  128.1 0.7 shard_map.53
  (1 shorter events, 0.0 us)
Async XLA Ops:
  2.0 51.1 %all-to-all-start.1 = ((bf16[8,2,2048]{2,1,0:T(2,128)(2,1)}), bf16[8,2,2048]{2,1,0:T(2,128)(2,1)S(1)}, u32[]{:S(2)}, u32[]{:S(2)}) async-start(bf16[8,2,2048]{2,1,0:T(2,128)(2,1)} %broadcast_in_dim.2), calls=%async_computation.1 | async-start | bytes 131072 | tf_op jit(solution)/shard_map/all_to_all | solution.py:203
  51.8 67.1 %copy-start = (bf16[256,416]{1,0:T(8,128)(2,1)S(1)}, bf16[256,416]{1,0:T(8,128)(2,1)}, u32[]{:S(2)}) copy-start(bf16[256,416]{1,0:T(8,128)(2,1)} %all_gather.3.g_ref) | copy-start | bytes 638980
  53.1 20.7 %all-to-all-start = ((bf16[8,32,2176]{2,1,0:T(8,128)(2,1)}), bf16[8,32,2176]{2,1,0:T(8,128)(2,1)S(1)}, u32[]{:S(2)}, u32[]{:S(2)}) async-start(bf16[8,32,2176]{2,1,0:T(8,128)(2,1)} %shard_map.50), calls=%async_computation | async-start | bytes 2228224 | tf_op jit(solution)/shard_map/all_to_all | solution.py:206
  57.7 13.1 %collective-permute-start.2 = (bf16[16,2048]{1,0:T(8,128)(2,1)S(1)}, bf16[16,2048]{1,0:T(8,128)(2,1)S(1)}, u32[]{:S(2)}, u32[]{:S(2)}) collective-permute-start(bf16[16,2048]{1,0:T(8,128)(2,1)S(1)} %reshape.8.refs_0_), channel_id=1, source_target_pairs={{0,3},{1,0},{2,1},{3,2},{4,7},{5,4},{6,5},{7,6},{8,11},{9,8},{10,9... | collective-permute-start | bytes 196616 | tf_op jit(solution)/shard_map/ppermute | solution.py:194
  62.1 8.7 %collective-permute-start.1 = (bf16[16,2048]{1,0:T(8,128)(2,1)S(1)}, bf16[16,2048]{1,0:T(8,128)(2,1)S(1)}, u32[]{:S(2)}, u32[]{:S(2)}) collective-permute-start(bf16[16,2048]{1,0:T(8,128)(2,1)S(1)} %reshape.8.refs_0_), channel_id=1, source_target_pairs={{0,2},{1,3},{2,0},{3,1},{4,6},{5,7},{6,4},{7,5},{8,10},{9,11},{10,... | collective-permute-start | bytes 196616 | tf_op jit(solution)/shard_map/ppermute | solution.py:194
  64.2 9.6 %collective-permute-start = (bf16[16,2048]{1,0:T(8,128)(2,1)S(1)}, bf16[16,2048]{1,0:T(8,128)(2,1)S(1)}, u32[]{:S(2)}, u32[]{:S(2)}) collective-permute-start(bf16[16,2048]{1,0:T(8,128)(2,1)S(1)} %reshape.8.refs_0_), channel_id=1, source_target_pairs={{0,1},{1,2},{2,3},{3,0},{4,5},{5,6},{6,7},{7,4},{8,9},{9,10},{10,1... | collective-permute-start | bytes 196616 | tf_op jit(solution)/shard_map/ppermute | solution.py:194
  75.3 52.8 %all-to-all-start.2 = ((bf16[16,2,2176]{2,1,0:T(2,128)(2,1)}), bf16[16,2,2176]{2,1,0:T(2,128)(2,1)S(1)}, u32[]{:S(2)}, u32[]{:S(2)}) async-start(bf16[16,2,2176]{2,1,0:T(2,128)(2,1)} %get-tuple-element.6), calls=%async_computation.2 | async-start | bytes 278528 | tf_op jit(solution)/shard_map/all_to_all | solution.py:209
  98.9 9.2 %collective-permute-start.5 = (bf16[64,2048]{1,0:T(8,128)(2,1)S(1)}, bf16[64,2048]{1,0:T(8,128)(2,1)S(1)}, u32[]{:S(2)}, u32[]{:S(2)}) collective-permute-start(bf16[64,2048]{1,0:T(8,128)(2,1)S(1)} %get-tuple-element.7.refs_0_), channel_id=1, source_target_pairs={{0,96},{32,0},{64,32},{96,64},{1,97},{33,1},{65,33},{97,65},{2,98}... | collective-permute-start | bytes 786440 | tf_op jit(solution)/shard_map/ppermute | solution.py:194
  102.7 9.1 %collective-permute-start.4 = (bf16[64,2048]{1,0:T(8,128)(2,1)S(1)}, bf16[64,2048]{1,0:T(8,128)(2,1)S(1)}, u32[]{:S(2)}, u32[]{:S(2)}) collective-permute-start(bf16[64,2048]{1,0:T(8,128)(2,1)S(1)} %get-tuple-element.7.refs_0_), channel_id=1, source_target_pairs={{0,64},{32,96},{64,0},{96,32},{1,65},{33,97},{65,1},{97,33},{2,66}... | collective-permute-start | bytes 786440 | tf_op jit(solution)/shard_map/ppermute | solution.py:194
  105.3 13.6 %collective-permute-start.3 = (bf16[64,2048]{1,0:T(8,128)(2,1)S(1)}, bf16[64,2048]{1,0:T(8,128)(2,1)S(1)}, u32[]{:S(2)}, u32[]{:S(2)}) collective-permute-start(bf16[64,2048]{1,0:T(8,128)(2,1)S(1)} %get-tuple-element.7.refs_0_), channel_id=1, source_target_pairs={{0,32},{32,64},{64,96},{96,0},{1,33},{33,65},{65,97},{97,1},{2,34}... | collective-permute-start | bytes 786440 | tf_op jit(solution)/shard_map/ppermute | solution.py:194

commit v5 on v4

--- a/solution.py
+++ b/solution.py
@@ -13,6 +13,7 @@
 ZL = ZM * Z0
 Z16 = ZH * ZM
 LANES = 128
+TILES = 4
 SPAN = 125.0
 F32 = jnp.float32
 BF16 = jnp.bfloat16
@@ -41,13 +42,18 @@
     return lax.dot_general(a, b, (dims, ((), ())), preferred_element_type=F32)
 
 
+def top_of(magnitude):
+    return (jnp.maximum(magnitude, 2.0**-90) * (1.0 + 2.0**-7)).astype(BF16)
+
+
+def encode_with(values, top):
+    level = jnp.exp2(jnp.abs(values) * ((2.0 * SPAN) / top.astype(F32)) - SPAN)
+    return jnp.where(values < 0.0, -level, level).astype(BF16)
+
+
 def encode(values):
-    top = jnp.max(jnp.abs(values), axis=1, keepdims=True)
-    top = (jnp.maximum(top, 2.0**-90) * (1.0 + 2.0**-7)).astype(BF16)
-    step = (2.0 * SPAN) / top.astype(F32)
-    level = jnp.exp2(jnp.abs(values) * step - SPAN)
-    codes = jnp.where(values < 0.0, -level, level).astype(BF16)
-    return codes, jnp.broadcast_to(top, (values.shape[0], LANES))
+    top = top_of(jnp.max(jnp.abs(values), axis=1, keepdims=True))
+    return encode_with(values, top), jnp.broadcast_to(top, (values.shape[0], LANES))
 
 
 def decode(codes, top):
@@ -65,11 +71,14 @@
     return total
 
 
-def partial_kernel(g_ref, w_hbm, out_ref, w_ref, sem):
-    copy = pltpu.make_async_copy(w_hbm, w_ref, sem)
-    copy.start()
+def partial_kernel(g_ref, w_hbm, out_ref, w_ref, sums_ref, sems):
     tok, ff = g_ref.shape
     feat = w_ref.shape[1]
+    tile = feat // TILES
+    tiles = [slice(t * tile, (t + 1) * tile) for t in range(TILES)]
+    copies = [pltpu.make_async_copy(w_hbm.at[:, c], w_ref.at[:, c], sems.at[t]) for t, c in enumerate(tiles)]
+    for copy in copies:
+        copy.start()
     g_t = g_ref[...].astype(F32).T
     codes_t = requant(g_t.reshape(ff // MXB, MXB, tok), 1).reshape(ff, tok).astype(BF16)
     row = lax.broadcasted_iota(jnp.int32, (tok, tok), 0)
@@ -79,11 +88,19 @@
     source = place // Z0 * (rows * Z0) + (rest // 2 * Z0 + place % Z0) * 2 + rest % 2
     order = jnp.where(col == source, 1.0, 0.0).astype(BF16)
     held = dot(order, codes_t, ((1,), (1,))).astype(BF16)
-    copy.wait()
+    most = jnp.zeros((tok, LANES), F32)
+    for copy, c in zip(copies, tiles):
+        copy.wait()
+        part = dot(held, w_ref[:, c], ((1,), (0,)))
+        sums_ref[:, c] = part
+        for k in range(tile // LANES):
+            most = jnp.maximum(most, jnp.abs(part[:, k * LANES : (k + 1) * LANES]))
+    top = top_of(jnp.max(most, axis=1, keepdims=True))
+    wide = jnp.broadcast_to(top, (tok, LANES))
     for k in range(Y * Z0):
-        codes, top = encode(dot(held[k * rows : (k + 1) * rows], w_ref[...], ((1,), (0,))))
-        out_ref[k, :, :feat] = codes
-        out_ref[k, :, feat:] = top
+        r = slice(k * rows, (k + 1) * rows)
+        out_ref[k, :, :feat] = encode_with(sums_ref[r, :], top[r])
+        out_ref[k, :, feat:] = wide[r]
 
 
 def partial_sums(g, w_t):
@@ -94,7 +111,11 @@
         out_shape=jax.ShapeDtypeStruct((Y * Z0, tok // (Y * Z0), feat + LANES), BF16),
         in_specs=[pl.BlockSpec(memory_space=pltpu.VMEM), pl.BlockSpec(memory_space=pltpu.HBM)],
         out_specs=pl.BlockSpec(memory_space=pltpu.VMEM),
-        scratch_shapes=[pltpu.VMEM((ff, feat), BF16), pltpu.SemaphoreType.DMA],
+        scratch_shapes=[
+            pltpu.VMEM((ff, feat), BF16),
+            pltpu.VMEM((tok, feat), F32),
+            pltpu.SemaphoreType.DMA((TILES,)),
+        ],
         compiler_params=pltpu.CompilerParams(vmem_limit_bytes=58 * 2**20),
         cost_estimate=pl.CostEstimate(
             flops=2 * tok * ff * feat, bytes_accessed=2 * ff * feat + 2 * tok * feat, transcendentals=tok * feat
@@ -102,27 +123,28 @@
     )(g, w_t)
 
 
-def add_near_kernel(in_ref, *refs):
-    act_refs, (out_ref, acts_ref) = refs[:ZL], refs[ZL:]
+def add_near_kernel(in_ref, acts_ref, out_ref):
     feat = in_ref.shape[2] - LANES
     codes, top = encode(decoded_sum(in_ref))
     for k in range(Z16):
         out_ref[k, :, :feat] = codes[2 * k : 2 * k + 2]
         out_ref[k, :, feat:] = top[2 * k : 2 * k + 2]
-    acts_ref[...] = jnp.concatenate([act_ref[...] for act_ref in act_refs], axis=0)
 
 
 def add_near(parts, acts):
     places, rows, wide = parts.shape
     return pl.pallas_call(
         add_near_kernel,
-        out_shape=[
-            jax.ShapeDtypeStruct((Z16, rows // Z16, wide), BF16),
-            jax.ShapeDtypeStruct((ZL * acts[0].shape[0], acts[0].shape[1]), BF16),
+        out_shape=jax.ShapeDtypeStruct((Z16, rows // Z16, wide), BF16),
+        grid=(1,),
+        in_specs=[
+            pl.BlockSpec(parts.shape, lambda i: (0, 0, 0)),
+            pl.BlockSpec((16, LANES), lambda i: (0, 0)),
         ],
+        out_specs=pl.BlockSpec((Z16, rows // Z16, wide), lambda i: (0, 0, 0)),
         compiler_params=pltpu.CompilerParams(vmem_limit_bytes=16 * 2**20),
         cost_estimate=pl.CostEstimate(flops=10 * parts.size, bytes_accessed=2 * parts.size, transcendentals=parts.size),
-    )(parts, *acts)
+    )(parts, acts)
 
 
 def add_far_kernel(in_ref, done_ref, out_ref):
@@ -151,8 +173,8 @@
         col = lax.broadcasted_iota(jnp.int32, (tok, tok), 1)
         far, rest = col // chunk, col % chunk
         near, zh, pair = rest // (2 * ZH), rest % (2 * ZH) // 2, rest % 2
-        y, zl = (at_ref[0] + Y - far) % Y, (at_ref[1] + ZL - near) % ZL
-        order = jnp.where(row == y * chunk + (zh * ZL + zl) * 2 + pair, 1.0, 0.0).astype(BF16)
+        y = (at_ref[0] + Y - far) % Y
+        order = jnp.where(row == y * chunk + (zh * ZL + near) * 2 + pair, 1.0, 0.0).astype(BF16)
         toks_ref[...] = dot(g, order, ((0,), (0,))).astype(BF16)
         done_ref[...] = jnp.zeros_like(done_ref)
 
@@ -196,17 +218,15 @@
 
 def local(grad_out, acts, weight):
     rows, feat = acts.shape
-    near = lax.axis_index("zm") * Z0 + lax.axis_index("z0")
-    at = jnp.stack([lax.axis_index("y"), near]).astype(jnp.int32)
+    at = lax.axis_index("y").astype(jnp.int32).reshape(1)
 
     copies = jnp.broadcast_to(acts[None], (ZH, rows, feat))
     zh_acts = lax.all_to_all(copies, "zh", 0, 0).reshape(ZH * rows, feat)
     g = lax.all_gather(grad_out, ("x", "core"), axis=0, tiled=True)
 
     sums = lax.all_to_all(partial_sums(g, weight.T), ("y", "z0"), 0, 0)
-    near_acts = [zh_acts] + [along(zh_acts, ("zm", "z0"), e, ZL) for e in (1, 2, 3)]
-    sums, z_acts = add_near(sums, near_acts)
-    sums = lax.all_to_all(sums, ("zh", "zm"), 0, 0)
+    z_acts = lax.all_gather(zh_acts, ("zm", "z0"), axis=0, tiled=True)
+    sums = lax.all_to_all(add_near(sums, z_acts), ("zh", "zm"), 0, 0)
     all_acts = [z_acts] + [along(z_acts, "y", d, Y) for d in (1, 2, 3)]
     grad_weight_t, done = weight_grad(at, g, all_acts)
     return add_far(sums, done), grad_weight_t.T

time: 129 us -> 131 us (1.016)
  the two profiles are of different devices: /device:TPU:1 before, /device:TPU:2 now
where the time goes in v5:
time: 131 us
  starting transfers between devices  64 us (49%)
  blocking collectives  36.2 us (28%)
  waiting for transfers between devices  17.3 us (13%)
  Pallas kernels  11.2 us (9%)
  local copies, waits for them, and re-layouts  1.4 us (1%)
    all_to_all x1, starting transfers between devices, local(): zh_acts = lax.all_to_all(copies, 'zh', 0, 0).reshape(ZH * rows, feat)  28.3 us
    all_gather x1, blocking collectives, local(): z_acts = lax.all_gather(zh_acts, ('zm', 'z0'), axis=0, tiled=True)  22.1 us
    all_to_all x1, starting transfers between devices, local(): sums = lax.all_to_all(add_near(sums, z_acts), ('zh', 'zm'), 0, 0)  19.3 us
    all_gather x1, blocking collectives, local(): g = lax.all_gather(grad_out, ('x', 'core'), axis=0, tiled=True)  14.2 us
    ppermute x3, starting transfers between devices, along(): lax.ppermute(x, axis, [(k, (k + distance) % size) for k in range(size)])  11.2 us
    all_to_all x1, waiting for transfers between devices, local(): sums = lax.all_to_all(add_near(sums, z_acts), ('zh', 'zm'), 0, 0)  6.84 us
    all_to_all x1, waiting for transfers between devices, local(): zh_acts = lax.all_to_all(copies, 'zh', 0, 0).reshape(ZH * rows, feat)  5.75 us
    all_to_all x1, starting transfers between devices, local(): sums = lax.all_to_all(partial_sums(g, weight.T), ('y', 'z0'), 0, 0)  5.11 us
  transfers between devices with their start and end apart: 6, of which 4 were waited for; matrix products, arithmetic and copies ran while one was open for 0% of the time, Pallas kernels for 7%

profile of v5, /device:TPU:2, one launch (start us, length us, event | category | flops | bytes accessed | tf_op | source)
XLA Modules:
  0.0 130.8 jit_solution(2368553547630138354)
XLA Ops:
  0.6 1.4 %broadcast_in_dim.2 = bf16[8,2,2048]{2,1,0:T(2,128)(2,1)} broadcast(bf16[2,2048]{1,0:T(2,128)(2,1)} %param.4), dimensions={1,2} | broadcast | bytes 73728 | tf_op jit(solution)/shard_map/broadcast_in_dim | solution.py:223
  2.0 28.3 %all-to-all-start.1 = ((bf16[8,2,2048]{2,1,0:T(2,128)(2,1)}), bf16[8,2,2048]{2,1,0:T(2,128)(2,1)S(1)}, u32[]{:S(2)}, u32[]{:S(2)}) async-start(bf16[8,2,2048]{2,1,0:T(2,128)(2,1)} %broadcast_in_dim.2), calls=%async_computation.1 | async-start | bytes 131072 | tf_op jit(solution)/shard_map/all_to_all | solution.py:224
  30.3 14.2 %all_gather.6.g_ref = bf16[256,416]{1,0:T(8,128)(2,1)} all-gather(bf16[32,416]{1,0:T(8,128)(2,1)} %param.3), channel_id=1, replica_groups=mesh['x'=4,'core'=2,'y'=4,'zh'=8,'zm'=2,'z0'=2] {'x','core'}, dimensions={0}, use_global_device_ids=true | all-gather | bytes 239616 | tf_op jit(solution)/shard_map/all_gather | solution.py:225
  44.5 4.8 %shard_map.50 = bf16[8,32,2176]{2,1,0:T(8,128)(2,1)} custom-call(bf16[256,416]{1,0:T(8,128)(2,1)} %all_gather.6.g_ref, bf16[416,2048]{1,0:T(8,128)(2,1)} %bitcast.3), custom_call_target="tpu_custom_call" | custom-call | flops 436207616 | bytes 2752512 | tf_op jit(solution)/shard_map/pallas_call | solution.py:109
  49.3 0.0 copy-start
  49.3 5.8 %all-to-all-done.1 = bf16[8,2,2048]{2,1,0:T(2,128)(2,1)S(1)} async-done(((bf16[8,2,2048]{2,1,0:T(2,128)(2,1)}), bf16[8,2,2048]{2,1,0:T(2,128)(2,1)S(1)}, u32[]{:S(2)}, u32[]{:S(2)}) %all-to-all-start.1) | async-done | bytes 65568 | tf_op jit(solution)/shard_map/all_to_all | solution.py:224
  55.0 5.1 %all-to-all-start = ((bf16[8,32,2176]{2,1,0:T(8,128)(2,1)}), bf16[8,32,2176]{2,1,0:T(8,128)(2,1)S(1)}, u32[]{:S(2)}, u32[]{:S(2)}) async-start(bf16[8,32,2176]{2,1,0:T(8,128)(2,1)} %shard_map.50), calls=%async_computation | async-start | bytes 2228224 | tf_op jit(solution)/shard_map/all_to_all | solution.py:227
  60.2 22.1 %all_gather.7.acts_ref.refs_0_ = bf16[64,2048]{1,0:T(8,128)(2,1)S(1)} all-gather(bf16[16,2048]{1,0:T(8,128)(2,1)S(1)} %reshape.11), channel_id=1, replica_groups=mesh['x'=4,'core'=2,'y'=4,'zh'=8,'zm'=2,'z0'=2] {'zm','z0'}, dimensions={0}, use_global_device_ids=true | all-gather | bytes 327680 | tf_op jit(solution)/shard_map/all_gather | solution.py:228
  82.2 0.0 all-to-all-done.in_ref
  82.2 1.5 %shard_map.51 = bf16[16,2,2176]{2,1,0:T(2,128)(2,1)} custom-call(bf16[8,32,2176]{2,1,0:T(8,128)(2,1)S(1)} %all-to-all-done.in_ref, bf16[64,2048]{1,0:T(8,128)(2,1)S(1)} %all_gather.7.acts_ref.refs_0_), custom_call_target="tpu_custom_call" | custom-call | flops 5570560 | bytes 1114112 | tf_op jit(solution)/shard_map/pallas_call | solution.py:136
  83.7 19.3 %all-to-all-start.2 = ((bf16[16,2,2176]{2,1,0:T(2,128)(2,1)}), bf16[16,2,2176]{2,1,0:T(2,128)(2,1)S(1)}, u32[]{:S(2)}, u32[]{:S(2)}) async-start(bf16[16,2,2176]{2,1,0:T(2,128)(2,1)} %shard_map.51), calls=%async_computation.2 | async-start | bytes 278528 | tf_op jit(solution)/shard_map/all_to_all | solution.py:229
  103.1 2.9 %collective-permute-start = (bf16[64,2048]{1,0:T(8,128)(2,1)S(1)}, bf16[64,2048]{1,0:T(8,128)(2,1)S(1)}, u32[]{:S(2)}, u32[]{:S(2)}) collective-permute-start(bf16[64,2048]{1,0:T(8,128)(2,1)S(1)} %all_gather.7.acts_ref.refs_0_), channel_id=1, source_target_pairs={{0,32},{32,64},{64,96},{96,0},{1,33},{33,65},{65,97},{97,1},{2,34}... | collective-permute-start | bytes 786440 | tf_op jit(solution)/shard_map/ppermute | solution.py:216
  105.9 4.3 %collective-permute-start.1 = (bf16[64,2048]{1,0:T(8,128)(2,1)S(1)}, bf16[64,2048]{1,0:T(8,128)(2,1)S(1)}, u32[]{:S(2)}, u32[]{:S(2)}) collective-permute-start(bf16[64,2048]{1,0:T(8,128)(2,1)S(1)} %all_gather.7.acts_ref.refs_0_), channel_id=1, source_target_pairs={{0,64},{32,96},{64,0},{96,32},{1,65},{33,97},{65,1},{97,33},{2,66}... | collective-permute-start | bytes 786440 | tf_op jit(solution)/shard_map/ppermute | solution.py:216
  110.3 4.0 %collective-permute-start.2 = (bf16[64,2048]{1,0:T(8,128)(2,1)S(1)}, bf16[64,2048]{1,0:T(8,128)(2,1)S(1)}, u32[]{:S(2)}, u32[]{:S(2)}) collective-permute-start(bf16[64,2048]{1,0:T(8,128)(2,1)S(1)} %all_gather.7.acts_ref.refs_0_), channel_id=1, source_target_pairs={{0,96},{32,0},{64,32},{96,64},{1,97},{33,1},{65,33},{97,65},{2,98}... | collective-permute-start | bytes 786440 | tf_op jit(solution)/shard_map/ppermute | solution.py:216
  114.3 0.0 collective-permute-done.refs_1_
  114.3 2.2 %collective-permute-done.1.refs_2_ = bf16[64,2048]{1,0:T(8,128)(2,1)S(1)} collective-permute-done((bf16[64,2048]{1,0:T(8,128)(2,1)S(1)}, bf16[64,2048]{1,0:T(8,128)(2,1)S(1)}, u32[]{:S(2)}, u32[]{:S(2)}) %collective-permute-start.1) | collective-permute-done | bytes 262176 | tf_op jit(solution)/shard_map/ppermute | solution.py:216
  116.5 2.5 %collective-permute-done.2.refs_3_ = bf16[64,2048]{1,0:T(8,128)(2,1)S(1)} collective-permute-done((bf16[64,2048]{1,0:T(8,128)(2,1)S(1)}, bf16[64,2048]{1,0:T(8,128)(2,1)S(1)}, u32[]{:S(2)}, u32[]{:S(2)}) %collective-permute-start.2) | collective-permute-done | bytes 262176 | tf_op jit(solution)/shard_map/ppermute | solution.py:216
  119.0 0.0 copy-done
  119.0 4.2 %shard_map.52 = (bf16[416,2048]{1,0:T(8,128)(2,1)}, f32[8,128]{1,0:T(8,128)S(1)}) custom-call(s32[1]{0:T(128)} %bitcast.1.at_ref, bf16[256,416]{1,0:T(8,128)(2,1)S(1)} %copy-done, bf16[64,2048]{1,0:T(8,128)(2,1)S(1)} %all_gather.7.acts_ref.refs_0_, bf16[64,2048]{1,0:T(8,128)(2,1)S(1)} %collective-permute-done.refs_1_, ...), custom_call_target="tpu_custom_call" | custom-call | flops 446693376 | bytes 2752512 | tf_op jit(solution)/shard_map/pallas_call | solution.py:195
  123.2 6.8 %all-to-all-done.2.in_ref = bf16[16,2,2176]{2,1,0:T(2,128)(2,1)S(1)} async-done(((bf16[16,2,2176]{2,1,0:T(2,128)(2,1)}), bf16[16,2,2176]{2,1,0:T(2,128)(2,1)S(1)}, u32[]{:S(2)}, u32[]{:S(2)}) %all-to-all-start.2) | async-done | bytes 139296 | tf_op jit(solution)/shard_map/all_to_all | solution.py:229
  130.0 0.7 shard_map.53
  (1 shorter events, 0.0 us)
Async XLA Ops:
  2.0 53.0 %all-to-all-start.1 = ((bf16[8,2,2048]{2,1,0:T(2,128)(2,1)}), bf16[8,2,2048]{2,1,0:T(2,128)(2,1)S(1)}, u32[]{:S(2)}, u32[]{:S(2)}) async-start(bf16[8,2,2048]{2,1,0:T(2,128)(2,1)} %broadcast_in_dim.2), calls=%async_computation.1 | async-start | bytes 131072 | tf_op jit(solution)/shard_map/all_to_all | solution.py:224
  49.3 69.8 %copy-start = (bf16[256,416]{1,0:T(8,128)(2,1)S(1)}, bf16[256,416]{1,0:T(8,128)(2,1)}, u32[]{:S(2)}) copy-start(bf16[256,416]{1,0:T(8,128)(2,1)} %all_gather.6.g_ref) | copy-start | bytes 638980
  55.0 27.2 %all-to-all-start = ((bf16[8,32,2176]{2,1,0:T(8,128)(2,1)}), bf16[8,32,2176]{2,1,0:T(8,128)(2,1)S(1)}, u32[]{:S(2)}, u32[]{:S(2)}) async-start(bf16[8,32,2176]{2,1,0:T(8,128)(2,1)} %shard_map.50), calls=%async_computation | async-start | bytes 2228224 | tf_op jit(solution)/shard_map/all_to_all | solution.py:227
  83.7 46.3 %all-to-all-start.2 = ((bf16[16,2,2176]{2,1,0:T(2,128)(2,1)}), bf16[16,2,2176]{2,1,0:T(2,128)(2,1)S(1)}, u32[]{:S(2)}, u32[]{:S(2)}) async-start(bf16[16,2,2176]{2,1,0:T(2,128)(2,1)} %shard_map.51), calls=%async_computation.2 | async-start | bytes 278528 | tf_op jit(solution)/shard_map/all_to_all | solution.py:229
  103.1 11.3 %collective-permute-start = (bf16[64,2048]{1,0:T(8,128)(2,1)S(1)}, bf16[64,2048]{1,0:T(8,128)(2,1)S(1)}, u32[]{:S(2)}, u32[]{:S(2)}) collective-permute-start(bf16[64,2048]{1,0:T(8,128)(2,1)S(1)} %all_gather.7.acts_ref.refs_0_), channel_id=1, source_target_pairs={{0,32},{32,64},{64,96},{96,0},{1,33},{33,65},{65,97},{97,1},{2,34}... | collective-permute-start | bytes 786440 | tf_op jit(solution)/shard_map/ppermute | solution.py:216
  105.9 10.6 %collective-permute-start.1 = (bf16[64,2048]{1,0:T(8,128)(2,1)S(1)}, bf16[64,2048]{1,0:T(8,128)(2,1)S(1)}, u32[]{:S(2)}, u32[]{:S(2)}) collective-permute-start(bf16[64,2048]{1,0:T(8,128)(2,1)S(1)} %all_gather.7.acts_ref.refs_0_), channel_id=1, source_target_pairs={{0,64},{32,96},{64,0},{96,32},{1,65},{33,97},{65,1},{97,33},{2,66}... | collective-permute-start | bytes 786440 | tf_op jit(solution)/shard_map/ppermute | solution.py:216
  110.3 8.8 %collective-permute-start.2 = (bf16[64,2048]{1,0:T(8,128)(2,1)S(1)}, bf16[64,2048]{1,0:T(8,128)(2,1)S(1)}, u32[]{:S(2)}, u32[]{:S(2)}) collective-permute-start(bf16[64,2048]{1,0:T(8,128)(2,1)S(1)} %all_gather.7.acts_ref.refs_0_), channel_id=1, source_target_pairs={{0,96},{32,0},{64,32},{96,64},{1,97},{33,1},{65,33},{97,65},{2,98}... | collective-permute-start | bytes 786440 | tf_op jit(solution)/shard_map/ppermute | solution.py:216

commit v6 on v5

--- a/solution.py
+++ b/solution.py
@@ -81,13 +81,8 @@
         copy.start()
     g_t = g_ref[...].astype(F32).T
     codes_t = requant(g_t.reshape(ff // MXB, MXB, tok), 1).reshape(ff, tok).astype(BF16)
-    row = lax.broadcasted_iota(jnp.int32, (tok, tok), 0)
-    col = lax.broadcasted_iota(jnp.int32, (tok, tok), 1)
     rows = tok // (Y * Z0)
-    place, rest = row // rows, row % rows
-    source = place // Z0 * (rows * Z0) + (rest // 2 * Z0 + place % Z0) * 2 + rest % 2
-    order = jnp.where(col == source, 1.0, 0.0).astype(BF16)
-    held = dot(order, codes_t, ((1,), (1,))).astype(BF16)
+    held = dot(ordered((tok, tok), 0), codes_t, ((1,), (1,))).astype(BF16)
     most = jnp.zeros((tok, LANES), F32)
     for copy, c in zip(copies, tiles):
         copy.wait()
@@ -124,84 +119,100 @@
 
 
 def add_near_kernel(in_ref, acts_ref, out_ref):
-    feat = in_ref.shape[2] - LANES
+    wide = in_ref.shape[2]
+    feat = wide - LANES
     codes, top = encode(decoded_sum(in_ref))
     for k in range(Z16):
         out_ref[k, :, :feat] = codes[2 * k : 2 * k + 2]
-        out_ref[k, :, feat:] = top[2 * k : 2 * k + 2]
+        out_ref[k, :, feat:wide] = top[2 * k : 2 * k + 2]
+        out_ref[k, :, wide:] = acts_ref[...]
 
 
 def add_near(parts, acts):
     places, rows, wide = parts.shape
     return pl.pallas_call(
         add_near_kernel,
-        out_shape=jax.ShapeDtypeStruct((Z16, rows // Z16, wide), BF16),
-        grid=(1,),
-        in_specs=[
-            pl.BlockSpec(parts.shape, lambda i: (0, 0, 0)),
-            pl.BlockSpec((16, LANES), lambda i: (0, 0)),
-        ],
-        out_specs=pl.BlockSpec((Z16, rows // Z16, wide), lambda i: (0, 0, 0)),
+        out_shape=jax.ShapeDtypeStruct((Z16, rows // Z16, wide + acts.shape[1]), BF16),
         compiler_params=pltpu.CompilerParams(vmem_limit_bytes=16 * 2**20),
         cost_estimate=pl.CostEstimate(flops=10 * parts.size, bytes_accessed=2 * parts.size, transcendentals=parts.size),
     )(parts, acts)
 
 
-def add_far_kernel(in_ref, done_ref, out_ref):
-    out_ref[...] = decoded_sum(in_ref).astype(BF16)
-
-
-def add_far(parts, done):
+def spread_kernel(in_ref, out_ref, held_ref):
+    feat = out_ref.shape[2]
+    for k in range(Z16):
+        held_ref[2 * k : 2 * k + 2, :] = in_ref[k, :, in_ref.shape[2] - feat :]
+    for j in range(Y * Z0):
+        out_ref[j] = held_ref[...]
+
+
+def spread(parts, feat):
+    places, rows, _ = parts.shape
+    return pl.pallas_call(
+        spread_kernel,
+        out_shape=jax.ShapeDtypeStruct((Y * Z0, places * rows, feat), BF16),
+        scratch_shapes=[pltpu.VMEM((places * rows, feat), BF16)],
+        compiler_params=pltpu.CompilerParams(vmem_limit_bytes=16 * 2**20),
+        cost_estimate=pl.CostEstimate(flops=0, bytes_accessed=20 * places * rows * feat, transcendentals=0),
+    )(parts)
+
+
+def add_far_kernel(in_ref, out_ref):
+    feat = out_ref.shape[1]
+    total = decode(in_ref[0, :, :feat], in_ref[0, :, feat : feat + LANES])
+    for k in range(1, Z16):
+        total = total + decode(in_ref[k, :, :feat], in_ref[k, :, feat : feat + LANES])
+    out_ref[...] = total.astype(BF16)
+
+
+def add_far(parts, feat):
     places, rows, wide = parts.shape
     return pl.pallas_call(
         add_far_kernel,
-        out_shape=jax.ShapeDtypeStruct((rows, wide - LANES), BF16),
+        out_shape=jax.ShapeDtypeStruct((rows, feat), BF16),
         compiler_params=pltpu.CompilerParams(vmem_limit_bytes=16 * 2**20),
         cost_estimate=pl.CostEstimate(flops=10 * parts.size, bytes_accessed=2 * parts.size, transcendentals=parts.size),
-    )(parts, done)
-
-
-def weight_kernel(at_ref, g_ref, *refs):
-    act_refs, (out_ref, done_ref, toks_ref) = refs[:Y], refs[Y:]
+    )(parts)
+
+
+def ordered(shape, axis):
+    tok = shape[0]
+    at = lax.broadcasted_iota(jnp.int32, shape, axis)
+    token = lax.broadcasted_iota(jnp.int32, shape, 1 - axis)
+    rows = tok // (Y * Z0)
+    place, rest = at // rows, at % rows
+    source = place // Z0 * (rows * Z0) + (rest // 2 * Z0 + place % Z0) * 2 + rest % 2
+    return jnp.where(token == source, 1.0, 0.0).astype(BF16)
+
+
+def weight_kernel(g_ref, act_ref, out_ref, toks_ref):
     tok, ff = g_ref.shape
     chunk = tok // Y
 
     @pl.when(pl.program_id(0) == 0)
     def _():
         g = requant(g_ref[...].astype(F32).reshape(tok // MXB, MXB, ff), 1).reshape(tok, ff).astype(BF16)
-        row = lax.broadcasted_iota(jnp.int32, (tok, tok), 0)
-        col = lax.broadcasted_iota(jnp.int32, (tok, tok), 1)
-        far, rest = col // chunk, col % chunk
-        near, zh, pair = rest // (2 * ZH), rest % (2 * ZH) // 2, rest % 2
-        y = (at_ref[0] + Y - far) % Y
-        order = jnp.where(row == y * chunk + (zh * ZL + near) * 2 + pair, 1.0, 0.0).astype(BF16)
-        toks_ref[...] = dot(g, order, ((0,), (0,))).astype(BF16)
-        done_ref[...] = jnp.zeros_like(done_ref)
-
+        toks_ref[...] = dot(g, ordered((tok, tok), 1), ((0,), (0,))).astype(BF16)
+
+    width = act_ref.shape[1]
     acts = []
-    for act_ref in act_refs:
-        a = act_ref[...].astype(F32)
-        width = a.shape[1]
-        blocks = a.reshape(ZL, 2 * ZH // 8, 8, width)
-        for_blocks = [requant(blocks[:, b].reshape(MXB, width), 0).reshape(ZL, 8, width) for b in range(2 * ZH // 8)]
-        acts.append(jnp.stack(for_blocks, axis=1).reshape(chunk, width).astype(BF16))
+    for y in range(Y):
+        a = act_ref[y * chunk : (y + 1) * chunk, :].astype(F32).reshape(Z0, chunk // MXB, MXB // Z0, width)
+        halves = [requant(a[:, b].reshape(MXB, width), 0).reshape(Z0, MXB // Z0, width) for b in range(chunk // MXB)]
+        acts.append(jnp.stack(halves, axis=1).reshape(chunk, width).astype(BF16))
     out_ref[...] = dot(toks_ref[...], jnp.concatenate(acts, axis=0), ((1,), (0,))).astype(BF16)
 
 
-def weight_grad(at, g, acts):
+def weight_grad(g, acts):
     tok, ff = g.shape
-    feat = acts[0].shape[1]
-    tile = feat // 4
+    feat = acts.shape[1]
+    tile = feat // TILES
     return pl.pallas_call(
         weight_kernel,
-        out_shape=[jax.ShapeDtypeStruct((ff, feat), BF16), jax.ShapeDtypeStruct((8, LANES), F32)],
-        grid=(feat // tile,),
-        in_specs=[
-            pl.BlockSpec(memory_space=pltpu.SMEM),
-            pl.BlockSpec((tok, ff), lambda i: (0, 0)),
-        ]
-        + [pl.BlockSpec((tok // Y, tile), lambda i: (0, i))] * Y,
-        out_specs=[pl.BlockSpec((ff, tile), lambda i: (0, i)), pl.BlockSpec((8, LANES), lambda i: (0, 0))],
+        out_shape=jax.ShapeDtypeStruct((ff, feat), BF16),
+        grid=(TILES,),
+        in_specs=[pl.BlockSpec((tok, ff), lambda i: (0, 0)), pl.BlockSpec((tok, tile), lambda i: (0, i))],
+        out_specs=pl.BlockSpec((ff, tile), lambda i: (0, i)),
         scratch_shapes=[pltpu.VMEM((ff, tok), BF16)],
         compiler_params=pltpu.CompilerParams(vmem_limit_bytes=32 * 2**20),
         cost_estimate=pl.CostEstimate(
@@ -209,27 +220,20 @@
             bytes_accessed=2 * ff * feat + 2 * tok * feat,
             transcendentals=0,
         ),
-    )(at, g, *acts)
-
-
-def along(x, axis, distance, size):
-    return lax.ppermute(x, axis, [(k, (k + distance) % size) for k in range(size)])
+    )(g, acts)
 
 
 def local(grad_out, acts, weight):
-    rows, feat = acts.shape
-    at = lax.axis_index("y").astype(jnp.int32).reshape(1)
-
-    copies = jnp.broadcast_to(acts[None], (ZH, rows, feat))
-    zh_acts = lax.all_to_all(copies, "zh", 0, 0).reshape(ZH * rows, feat)
-    g = lax.all_gather(grad_out, ("x", "core"), axis=0, tiled=True)
-
-    sums = lax.all_to_all(partial_sums(g, weight.T), ("y", "z0"), 0, 0)
-    z_acts = lax.all_gather(zh_acts, ("zm", "z0"), axis=0, tiled=True)
-    sums = lax.all_to_all(add_near(sums, z_acts), ("zh", "zm"), 0, 0)
-    all_acts = [z_acts] + [along(z_acts, "y", d, Y) for d in (1, 2, 3)]
-    grad_weight_t, done = weight_grad(at, g, all_acts)
-    return add_far(sums, done), grad_weight_t.T
+    own, ff = grad_out.shape
+    feat = acts.shape[1]
+    row, near, far = ("x", "core"), ("y", "z0"), ("zh", "zm")
+    copies = jnp.broadcast_to(grad_out[None], (8, own, ff))
+    g = lax.all_to_all(copies, row, 0, 0).reshape(8 * own, ff)
+    sums = lax.all_to_all(partial_sums(g, weight.T), near, 0, 0)
+    parts = lax.all_to_all(add_near(sums, acts), far, 0, 0)
+    all_acts = lax.all_to_all(spread(parts, feat), near, 0, 0)
+    grad_weight_t = weight_grad(g, all_acts.reshape(-1, feat))
+    return add_far(parts, feat), grad_weight_t.T
 
 
 def solution(mesh):

time: 131 us -> 126 us (0.962)
  the two profiles are of different devices: /device:TPU:2 before, /device:TPU:64 now
where the time goes in v6:
time: 126 us
  blocking collectives  96.1 us (76%)
  waiting for transfers between devices  12.9 us (10%)
  Pallas kernels  11.5 us (9%)
  starting transfers between devices  3.56 us (3%)
    all_to_all x1, blocking collectives, local(): parts = lax.all_to_all(add_near(sums, acts), far, 0, 0)  62.4 us
    all_to_all x1, blocking collectives, local(): sums = lax.all_to_all(partial_sums(g, weight.T), near, 0, 0)  22 us
    all_to_all x1, waiting for transfers between devices, local(): all_acts = lax.all_to_all(spread(parts, feat), near, 0, 0)  12.9 us
    all_to_all x1, blocking collectives, local(): g = lax.all_to_all(copies, row, 0, 0).reshape(8 * own, ff)  11.7 us
    pallas_call x1, Pallas kernels, partial_sums(): pl.pallas_call(partial_kernel, out_shape=jax.ShapeDtypeStruct((Y * Z0, to...  4.76 us
    pallas_call x1, Pallas kernels, weight_grad(): pl.pallas_call(weight_kernel, out_shape=jax.ShapeDtypeStruct((ff, feat),...  4.08 us
    all_to_all x1, starting transfers between devices, local(): all_acts = lax.all_to_all(spread(parts, feat), near, 0, 0)  3.56 us
  transfers between devices with their start and end apart: 1, of which 1 were waited for; matrix products, arithmetic and copies ran while one was open for 0% of the time, Pallas kernels for 1%

profile of v6, /device:TPU:64, one launch (start us, length us, event | category | flops | bytes accessed | tf_op | source)
XLA Modules:
  0.0 125.5 jit_solution(3192621002940167336)
XLA Ops:
  0.6 0.8 broadcast_in_dim.2
  1.4 11.7 %all_to_all.20 = bf16[8,32,416]{2,1,0:T(8,128)(2,1)} all-to-all(bf16[8,32,416]{2,1,0:T(8,128)(2,1)S(1)} %broadcast_in_dim.2), channel_id=1, replica_groups=mesh['x'=4,'core'=2,'y'=4,'zh'=8,'zm'=2,'z0'=2] {'x','core'}, dimensions={0} | all-to-all | bytes 425984 | tf_op jit(solution)/shard_map/all_to_all | solution.py:231
  13.2 4.8 %shard_map.50 = bf16[8,32,2176]{2,1,0:T(8,128)(2,1)} custom-call(bf16[256,416]{1,0:T(8,128)(2,1)} %bitcast.5, bf16[416,2048]{1,0:T(8,128)(2,1)} %bitcast.7), custom_call_target="tpu_custom_call" | custom-call | flops 436207616 | bytes 2752512 | tf_op jit(solution)/shard_map/pallas_call | solution.py:104
  17.9 0.0 copy-start.1
  17.9 22.0 %all_to_all.21.in_ref = bf16[8,32,2176]{2,1,0:T(8,128)(2,1)S(1)} all-to-all(bf16[8,32,2176]{2,1,0:T(8,128)(2,1)} %shard_map.50), channel_id=1, replica_groups=mesh['x'=4,'core'=2,'y'=4,'zh'=8,'zm'=2,'z0'=2] {'y','z0'}, dimensions={0} | all-to-all | bytes 2228224 | tf_op jit(solution)/shard_map/all_to_all | solution.py:232
  39.9 0.0 copy-done.1
  39.9 0.8 shard_map.51
  40.8 62.4 %all_to_all.22.in_ref = bf16[16,2,4224]{2,1,0:T(2,128)(2,1)S(1)} all-to-all(bf16[16,2,4224]{2,1,0:T(2,128)(2,1)S(1)} %shard_map.51), channel_id=1, replica_groups=mesh['x'=4,'core'=2,'y'=4,'zh'=8,'zm'=2,'z0'=2] {'zh','zm'}, dimensions={0} | all-to-all | bytes 540672 | tf_op jit(solution)/shard_map/all_to_all | solution.py:233
  103.2 0.0 copy-start
  103.2 1.1 shard_map.53
  104.3 3.6 %all-to-all-start.3 = ((bf16[8,32,2048]{2,1,0:T(8,128)(2,1)}), bf16[8,32,2048]{2,1,0:T(8,128)(2,1)S(1)}, u32[]{:S(2)}, u32[]{:S(2)}) async-start(bf16[8,32,2048]{2,1,0:T(8,128)(2,1)} %shard_map.53), calls=%async_computation.3 | async-start | bytes 2097152 | tf_op jit(solution)/shard_map/all_to_all | solution.py:234
  107.9 0.7 shard_map.52
  108.6 12.9 %all-to-all-done.3 = bf16[8,32,2048]{2,1,0:T(8,128)(2,1)S(1)} async-done(((bf16[8,32,2048]{2,1,0:T(8,128)(2,1)}), bf16[8,32,2048]{2,1,0:T(8,128)(2,1)S(1)}, u32[]{:S(2)}, u32[]{:S(2)}) %all-to-all-start.3) | async-done | bytes 1048608 | tf_op jit(solution)/shard_map/all_to_all | solution.py:234
  121.5 0.0 copy-done
  121.5 4.1 %shard_map.54 = bf16[416,2048]{1,0:T(8,128)(2,1)} custom-call(bf16[256,416]{1,0:T(8,128)(2,1)S(1)} %bitcast.6, bf16[256,2048]{1,0:T(8,128)(2,1)S(1)} %bitcast.4), custom_call_target="tpu_custom_call" | custom-call | flops 446693376 | bytes 2752512 | tf_op jit(solution)/shard_map/pallas_call | solution.py:210
Async XLA Ops:
  17.9 22.0 %copy-start.1 = (bf16[2,2048]{1,0:T(2,128)(2,1)S(1)}, bf16[2,2048]{1,0:T(2,128)(2,1)}, u32[]{:S(2)}) copy-start(bf16[2,2048]{1,0:T(2,128)(2,1)} %acts_ref.1) | copy-start | bytes 24580
  103.2 18.3 %copy-start = (bf16[8,32,416]{2,1,0:T(8,128)(2,1)S(1)}, bf16[8,32,416]{2,1,0:T(8,128)(2,1)}, u32[]{:S(2)}) copy-start(bf16[8,32,416]{2,1,0:T(8,128)(2,1)} %all_to_all.20) | copy-start | bytes 638980
  104.3 17.2 %all-to-all-start.3 = ((bf16[8,32,2048]{2,1,0:T(8,128)(2,1)}), bf16[8,32,2048]{2,1,0:T(8,128)(2,1)S(1)}, u32[]{:S(2)}, u32[]{:S(2)}) async-start(bf16[8,32,2048]{2,1,0:T(8,128)(2,1)} %shard_map.53), calls=%async_computation.3 | async-start | bytes 2097152 | tf_op jit(solution)/shard_map/all_to_all | solution.py:234

commit v7 on v6

--- a/solution.py
+++ b/solution.py
@@ -71,21 +71,17 @@
     return total
 
 
-def partial_kernel(g_ref, w_hbm, out_ref, w_ref, sums_ref, sems):
+def partial_kernel(g_ref, w_ref, out_ref, sums_ref):
     tok, ff = g_ref.shape
     feat = w_ref.shape[1]
     tile = feat // TILES
     tiles = [slice(t * tile, (t + 1) * tile) for t in range(TILES)]
-    copies = [pltpu.make_async_copy(w_hbm.at[:, c], w_ref.at[:, c], sems.at[t]) for t, c in enumerate(tiles)]
-    for copy in copies:
-        copy.start()
     g_t = g_ref[...].astype(F32).T
     codes_t = requant(g_t.reshape(ff // MXB, MXB, tok), 1).reshape(ff, tok).astype(BF16)
     rows = tok // (Y * Z0)
     held = dot(ordered((tok, tok), 0), codes_t, ((1,), (1,))).astype(BF16)
     most = jnp.zeros((tok, LANES), F32)
-    for copy, c in zip(copies, tiles):
-        copy.wait()
+    for c in tiles:
         part = dot(held, w_ref[:, c], ((1,), (0,)))
         sums_ref[:, c] = part
         for k in range(tile // LANES):
@@ -104,14 +100,8 @@
     return pl.pallas_call(
         partial_kernel,
         out_shape=jax.ShapeDtypeStruct((Y * Z0, tok // (Y * Z0), feat + LANES), BF16),
-        in_specs=[pl.BlockSpec(memory_space=pltpu.VMEM), pl.BlockSpec(memory_space=pltpu.HBM)],
-        out_specs=pl.BlockSpec(memory_space=pltpu.VMEM),
-        scratch_shapes=[
-            pltpu.VMEM((ff, feat), BF16),
-            pltpu.VMEM((tok, feat), F32),
-            pltpu.SemaphoreType.DMA((TILES,)),
-        ],
-        compiler_params=pltpu.CompilerParams(vmem_limit_bytes=58 * 2**20),
+        scratch_shapes=[pltpu.VMEM((tok, feat), F32)],
+        compiler_params=pltpu.CompilerParams(vmem_limit_bytes=16 * 2**20),
         cost_estimate=pl.CostEstimate(
             flops=2 * tok * ff * feat, bytes_accessed=2 * ff * feat + 2 * tok * feat, transcendentals=tok * feat
         ),
@@ -185,16 +175,25 @@
     return jnp.where(token == source, 1.0, 0.0).astype(BF16)
 
 
-def weight_kernel(g_ref, act_ref, out_ref, toks_ref):
+def toks_kernel(g_ref, out_ref):
     tok, ff = g_ref.shape
+    g = requant(g_ref[...].astype(F32).reshape(tok // MXB, MXB, ff), 1).reshape(tok, ff).astype(BF16)
+    out_ref[...] = dot(g, ordered((tok, tok), 1), ((0,), (0,))).astype(BF16)
+
+
+def grad_toks(g):
+    tok, ff = g.shape
+    return pl.pallas_call(
+        toks_kernel,
+        out_shape=jax.ShapeDtypeStruct((ff, tok), BF16),
+        compiler_params=pltpu.CompilerParams(vmem_limit_bytes=16 * 2**20),
+        cost_estimate=pl.CostEstimate(flops=2 * tok * tok * ff, bytes_accessed=4 * tok * ff, transcendentals=0),
+    )(g)
+
+
+def weight_kernel(toks_ref, act_ref, out_ref):
+    tok, width = act_ref.shape
     chunk = tok // Y
-
-    @pl.when(pl.program_id(0) == 0)
-    def _():
-        g = requant(g_ref[...].astype(F32).reshape(tok // MXB, MXB, ff), 1).reshape(tok, ff).astype(BF16)
-        toks_ref[...] = dot(g, ordered((tok, tok), 1), ((0,), (0,))).astype(BF16)
-
-    width = act_ref.shape[1]
     acts = []
     for y in range(Y):
         a = act_ref[y * chunk : (y + 1) * chunk, :].astype(F32).reshape(Z0, chunk // MXB, MXB // Z0, width)
@@ -203,24 +202,23 @@
     out_ref[...] = dot(toks_ref[...], jnp.concatenate(acts, axis=0), ((1,), (0,))).astype(BF16)
 
 
-def weight_grad(g, acts):
-    tok, ff = g.shape
+def weight_grad(toks, acts):
+    ff, tok = toks.shape
     feat = acts.shape[1]
     tile = feat // TILES
     return pl.pallas_call(
         weight_kernel,
         out_shape=jax.ShapeDtypeStruct((ff, feat), BF16),
         grid=(TILES,),
-        in_specs=[pl.BlockSpec((tok, ff), lambda i: (0, 0)), pl.BlockSpec((tok, tile), lambda i: (0, i))],
+        in_specs=[pl.BlockSpec((ff, tok), lambda i: (0, 0)), pl.BlockSpec((tok, tile), lambda i: (0, i))],
         out_specs=pl.BlockSpec((ff, tile), lambda i: (0, i)),
-        scratch_shapes=[pltpu.VMEM((ff, tok), BF16)],
         compiler_params=pltpu.CompilerParams(vmem_limit_bytes=32 * 2**20),
         cost_estimate=pl.CostEstimate(
             flops=2 * tok * ff * feat + 20 * tok * feat,
             bytes_accessed=2 * ff * feat + 2 * tok * feat,
             transcendentals=0,
         ),
-    )(g, acts)
+    )(toks, acts)
 
 
 def local(grad_out, acts, weight):
@@ -232,7 +230,7 @@
     sums = lax.all_to_all(partial_sums(g, weight.T), near, 0, 0)
     parts = lax.all_to_all(add_near(sums, acts), far, 0, 0)
     all_acts = lax.all_to_all(spread(parts, feat), near, 0, 0)
-    grad_weight_t = weight_grad(g, all_acts.reshape(-1, feat))
+    grad_weight_t = weight_grad(grad_toks(g), all_acts.reshape(-1, feat))
     return add_far(parts, feat), grad_weight_t.T
 
 

time: 126 us -> 124 us (0.984)
  Pallas kernels: 11.5 us -> 8.57 us
  local copies, waits for them, and re-layouts: 0.79 us -> 2.24 us
    pallas_call x1, Pallas kernels: 4.76 us -> 1.8 us  [partial_sums(): pl.pallas_call(partial_kernel, out_shape=jax.ShapeDtypeStruct((Y * Z0, to...]
    unnamed x4, local copies, waits for them, and re-layouts: 0.01 us -> 1.46 us
where the time goes in v7:
time: 124 us
  blocking collectives  95.8 us (77%)
  waiting for transfers between devices  12.7 us (10%)
  Pallas kernels  8.57 us (7%)
  starting transfers between devices  3.56 us (3%)
  local copies, waits for them, and re-layouts  2.24 us (2%)
    all_to_all x1, blocking collectives, local(): parts = lax.all_to_all(add_near(sums, acts), far, 0, 0)  62.4 us
    all_to_all x1, blocking collectives, local(): sums = lax.all_to_all(partial_sums(g, weight.T), near, 0, 0)  21.8 us
    all_to_all x1, waiting for transfers between devices, local(): all_acts = lax.all_to_all(spread(parts, feat), near, 0, 0)  12.7 us
    all_to_all x1, blocking collectives, local(): g = lax.all_to_all(copies, row, 0, 0).reshape(8 * own, ff)  11.6 us
    all_to_all x1, starting transfers between devices, local(): all_acts = lax.all_to_all(spread(parts, feat), near, 0, 0)  3.56 us
    pallas_call x1, Pallas kernels, weight_grad(): pl.pallas_call(weight_kernel, out_shape=jax.ShapeDtypeStruct((ff, feat),...  3.5 us
  transfers between devices with their start and end apart: 1, of which 1 were waited for; matrix products, arithmetic and copies ran while one was open for 0% of the time, Pallas kernels for 1%

profile of v7, /device:TPU:64, one launch (start us, length us, event | category | flops | bytes accessed | tf_op | source)
XLA Modules:
  0.0 123.5 jit_solution(16329322838695090390)
XLA Ops:
  0.6 0.8 broadcast_in_dim.2
  1.4 11.6 %all_to_all.20 = bf16[8,32,416]{2,1,0:T(8,128)(2,1)S(1)} all-to-all(bf16[8,32,416]{2,1,0:T(8,128)(2,1)S(1)} %broadcast_in_dim.2), channel_id=1, replica_groups=mesh['x'=4,'core'=2,'y'=4,'zh'=8,'zm'=2,'z0'=2] {'x','core'}, dimensions={0} | all-to-all | bytes 425984 | tf_op jit(solution)/shard_map/all_to_all | solution.py:229
  13.0 0.0 copy-start
  13.0 1.5 %copy-done = bf16[2048,416]{0,1:T(8,128)(2,1)S(1)} copy-done((bf16[2048,416]{0,1:T(8,128)(2,1)S(1)}, bf16[2048,416]{0,1:T(8,128)(2,1)}, u32[]{:S(2)}) %copy-start) | copy-done | bytes 1703960
  14.5 1.8 %shard_map.50 = bf16[8,32,2176]{2,1,0:T(8,128)(2,1)S(1)} custom-call(bf16[256,416]{1,0:T(8,128)(2,1)S(1)} %bitcast.5, bf16[416,2048]{1,0:T(8,128)(2,1)S(1)} %bitcast.7), custom_call_target="tpu_custom_call" | custom-call | flops 436207616 | bytes 2752512 | tf_op jit(solution)/shard_map/pallas_call | solution.py:100
  16.3 0.0 copy-start.1
  16.3 21.8 %all_to_all.21.in_ref = bf16[8,32,2176]{2,1,0:T(8,128)(2,1)S(1)} all-to-all(bf16[8,32,2176]{2,1,0:T(8,128)(2,1)S(1)} %shard_map.50), channel_id=1, replica_groups=mesh['x'=4,'core'=2,'y'=4,'zh'=8,'zm'=2,'z0'=2] {'y','z0'}, dimensions={0} | all-to-all | bytes 2228224 | tf_op jit(solution)/shard_map/all_to_all | solution.py:230
  38.1 0.0 copy-done.1
  38.1 0.8 shard_map.51
  38.9 62.4 %all_to_all.22.in_ref = bf16[16,2,4224]{2,1,0:T(2,128)(2,1)S(1)} all-to-all(bf16[16,2,4224]{2,1,0:T(2,128)(2,1)S(1)} %shard_map.51), channel_id=1, replica_groups=mesh['x'=4,'core'=2,'y'=4,'zh'=8,'zm'=2,'z0'=2] {'zh','zm'}, dimensions={0} | all-to-all | bytes 540672 | tf_op jit(solution)/shard_map/all_to_all | solution.py:231
  101.4 1.1 shard_map.54
  102.5 3.6 %all-to-all-start.3 = ((bf16[8,32,2048]{2,1,0:T(8,128)(2,1)}), bf16[8,32,2048]{2,1,0:T(8,128)(2,1)S(1)}, u32[]{:S(2)}, u32[]{:S(2)}) async-start(bf16[8,32,2048]{2,1,0:T(8,128)(2,1)} %shard_map.54), calls=%async_computation.3 | async-start | bytes 2097152 | tf_op jit(solution)/shard_map/all_to_all | solution.py:232
  106.0 0.6 shard_map.53.toks_ref
  106.6 0.7 shard_map.52
  107.3 12.7 %all-to-all-done.3 = bf16[8,32,2048]{2,1,0:T(8,128)(2,1)S(1)} async-done(((bf16[8,32,2048]{2,1,0:T(8,128)(2,1)}), bf16[8,32,2048]{2,1,0:T(8,128)(2,1)S(1)}, u32[]{:S(2)}, u32[]{:S(2)}) %all-to-all-start.3) | async-done | bytes 1048608 | tf_op jit(solution)/shard_map/all_to_all | solution.py:232
  120.0 3.5 %shard_map.55 = bf16[416,2048]{1,0:T(8,128)(2,1)} custom-call(bf16[416,256]{1,0:T(8,128)(2,1)S(1)} %shard_map.53.toks_ref, bf16[256,2048]{1,0:T(8,128)(2,1)S(1)} %bitcast.4), custom_call_target="tpu_custom_call" | custom-call | flops 446693376 | bytes 2752512 | tf_op jit(solution)/shard_map/pallas_call | solution.py:209
Async XLA Ops:
  13.0 1.5 %copy-start = (bf16[2048,416]{0,1:T(8,128)(2,1)S(1)}, bf16[2048,416]{0,1:T(8,128)(2,1)}, u32[]{:S(2)}) copy-start(bf16[2048,416]{0,1:T(8,128)(2,1)} %param.5) | copy-start | bytes 5111812
  16.3 21.8 %copy-start.1 = (bf16[2,2048]{1,0:T(2,128)(2,1)S(1)}, bf16[2,2048]{1,0:T(2,128)(2,1)}, u32[]{:S(2)}) copy-start(bf16[2,2048]{1,0:T(2,128)(2,1)} %acts_ref.1) | copy-start | bytes 24580
  102.5 17.6 %all-to-all-start.3 = ((bf16[8,32,2048]{2,1,0:T(8,128)(2,1)}), bf16[8,32,2048]{2,1,0:T(8,128)(2,1)S(1)}, u32[]{:S(2)}, u32[]{:S(2)}) async-start(bf16[8,32,2048]{2,1,0:T(8,128)(2,1)} %shard_map.54), calls=%async_computation.3 | async-start | bytes 2097152 | tf_op jit(solution)/shard_map/all_to_all | solution.py:232

commit v8 on v7

--- a/solution.py
+++ b/solution.py
@@ -94,6 +94,24 @@
         out_ref[k, :, feat:] = wide[r]
 
 
+def fetch_kernel(w_hbm, out_ref, sem):
+    copy = pltpu.make_async_copy(w_hbm, out_ref, sem)
+    copy.start()
+    copy.wait()
+
+
+def fetch(w_t):
+    return pl.pallas_call(
+        fetch_kernel,
+        out_shape=jax.ShapeDtypeStruct(w_t.shape, w_t.dtype),
+        in_specs=[pl.BlockSpec(memory_space=pltpu.HBM)],
+        out_specs=pl.BlockSpec(memory_space=pltpu.VMEM),
+        scratch_shapes=[pltpu.SemaphoreType.DMA],
+        compiler_params=pltpu.CompilerParams(vmem_limit_bytes=16 * 2**20),
+        cost_estimate=pl.CostEstimate(flops=0, bytes_accessed=4 * w_t.size, transcendentals=0),
+    )(w_t)
+
+
 def partial_sums(g, w_t):
     tok, ff = g.shape
     feat = w_t.shape[1]
@@ -205,11 +223,11 @@
 def weight_grad(toks, acts):
     ff, tok = toks.shape
     feat = acts.shape[1]
-    tile = feat // TILES
+    tile = feat // 2
     return pl.pallas_call(
         weight_kernel,
         out_shape=jax.ShapeDtypeStruct((ff, feat), BF16),
-        grid=(TILES,),
+        grid=(2,),
         in_specs=[pl.BlockSpec((ff, tok), lambda i: (0, 0)), pl.BlockSpec((tok, tile), lambda i: (0, i))],
         out_specs=pl.BlockSpec((ff, tile), lambda i: (0, i)),
         compiler_params=pltpu.CompilerParams(vmem_limit_bytes=32 * 2**20),
@@ -227,7 +245,7 @@
     row, near, far = ("x", "core"), ("y", "z0"), ("zh", "zm")
     copies = jnp.broadcast_to(grad_out[None], (8, own, ff))
     g = lax.all_to_all(copies, row, 0, 0).reshape(8 * own, ff)
-    sums = lax.all_to_all(partial_sums(g, weight.T), near, 0, 0)
+    sums = lax.all_to_all(partial_sums(g, fetch(weight.T)), near, 0, 0)
     parts = lax.all_to_all(add_near(sums, acts), far, 0, 0)
     all_acts = lax.all_to_all(spread(parts, feat), near, 0, 0)
     grad_weight_t = weight_grad(grad_toks(g), all_acts.reshape(-1, feat))

time: 124 us -> 123 us (level)
  blocking collectives: 95.8 us -> 84.2 us
  waiting for transfers between devices: 12.7 us -> 18.1 us
  starting transfers between devices: 3.56 us -> 7.86 us
    all_to_all x2 -> x1, blocking collectives: 33.4 us -> 21.8 us  [local(): sums = lax.all_to_all(partial_sums(g, fetch(weight.T)), near, 0, 0)]
    all_to_all x0 -> x1, waiting for transfers between devices: none -> 5.8 us  [local(): g = lax.all_to_all(copies, row, 0, 0).reshape(8 * own, ff)]
    all_to_all x0 -> x1, starting transfers between devices: none -> 4.3 us  [local(): g = lax.all_to_all(copies, row, 0, 0).reshape(8 * own, ff)]
  transfers between devices with their start and end apart: 1 -> 2, of which waited for: 1 -> 2; matrix products, arithmetic and copies ran while one was open for 0% -> 0% of each run, Pallas kernels for 1% -> 1%
where the time goes in v8:
time: 123 us; the launch traced here: 122 us
  blocking collectives  84.2 us (68%)
  waiting for transfers between devices  18.1 us (15%)
  Pallas kernels  8.54 us (7%)
  starting transfers between devices  7.86 us (6%)
  local copies, waits for them, and re-layouts  2.94 us (2%)
    all_to_all x1, blocking collectives, local(): parts = lax.all_to_all(add_near(sums, acts), far, 0, 0)  62.4 us
    all_to_all x1, blocking collectives, local(): sums = lax.all_to_all(partial_sums(g, fetch(weight.T)), near, 0, 0)  21.8 us
    all_to_all x1, waiting for transfers between devices, local(): all_acts = lax.all_to_all(spread(parts, feat), near, 0, 0)  12.3 us
    all_to_all x1, waiting for transfers between devices, local(): g = lax.all_to_all(copies, row, 0, 0).reshape(8 * own, ff)  5.8 us
    all_to_all x1, starting transfers between devices, local(): g = lax.all_to_all(copies, row, 0, 0).reshape(8 * own, ff)  4.3 us
    all_to_all x1, starting transfers between devices, local(): all_acts = lax.all_to_all(spread(parts, feat), near, 0, 0)  3.56 us
    pallas_call x1, Pallas kernels, weight_grad(): pl.pallas_call(weight_kernel, out_shape=jax.ShapeDtypeStruct((ff, feat),...  3.19 us
  transfers between devices with their start and end apart: 2, of which 2 were waited for; matrix products, arithmetic and copies ran while one was open for 0% of the time, Pallas kernels for 1%

profile of v8, /device:TPU:64, one launch (start us, length us, event | category | flops | bytes accessed | tf_op | source)
XLA Modules:
  0.0 122.3 jit_solution(11714008284552139503)
XLA Ops:
  0.6 1.5 %broadcast_in_dim.2 = bf16[8,32,416]{2,1,0:T(8,128)(2,1)} broadcast(bf16[32,416]{1,0:T(8,128)(2,1)} %param.3), dimensions={1,2} | broadcast | bytes 239616 | tf_op jit(solution)/shard_map/broadcast_in_dim | solution.py:246
  2.1 4.3 %all-to-all-start = ((bf16[8,32,416]{2,1,0:T(8,128)(2,1)}), bf16[8,32,416]{2,1,0:T(8,128)(2,1)S(1)}, u32[]{:S(2)}, u32[]{:S(2)}) async-start(bf16[8,32,416]{2,1,0:T(8,128)(2,1)} %broadcast_in_dim.2), calls=%async_computation | async-start | bytes 524288 | tf_op jit(solution)/shard_map/all_to_all | solution.py:247
  6.4 0.0 copy-start
  6.4 1.4 %copy-done = bf16[2048,416]{0,1:T(8,128)(2,1)S(1)} copy-done((bf16[2048,416]{0,1:T(8,128)(2,1)S(1)}, bf16[2048,416]{0,1:T(8,128)(2,1)}, u32[]{:S(2)}) %copy-start) | copy-done | bytes 1703960
  7.9 0.3 shard_map.50.w_ref
  8.2 5.8 %all-to-all-done = bf16[8,32,416]{2,1,0:T(8,128)(2,1)S(1)} async-done(((bf16[8,32,416]{2,1,0:T(8,128)(2,1)}), bf16[8,32,416]{2,1,0:T(8,128)(2,1)S(1)}, u32[]{:S(2)}, u32[]{:S(2)}) %all-to-all-start) | async-done | bytes 213024 | tf_op jit(solution)/shard_map/all_to_all | solution.py:247
  14.0 1.8 %shard_map.51 = bf16[8,32,2176]{2,1,0:T(8,128)(2,1)S(1)} custom-call(bf16[256,416]{1,0:T(8,128)(2,1)S(1)} %bitcast.5, bf16[416,2048]{1,0:T(8,128)(2,1)S(1)} %shard_map.50.w_ref), custom_call_target="tpu_custom_call" | custom-call | flops 436207616 | bytes 2752512 | tf_op jit(solution)/shard_map/pallas_call | solution.py:118
  15.8 0.0 copy-start.1
  15.8 21.8 %all_to_all.20.in_ref = bf16[8,32,2176]{2,1,0:T(8,128)(2,1)S(1)} all-to-all(bf16[8,32,2176]{2,1,0:T(8,128)(2,1)S(1)} %shard_map.51), channel_id=1, replica_groups=mesh['x'=4,'core'=2,'y'=4,'zh'=8,'zm'=2,'z0'=2] {'y','z0'}, dimensions={0} | all-to-all | bytes 2228224 | tf_op jit(solution)/shard_map/all_to_all | solution.py:248
  37.5 0.0 copy-done.1
  37.5 0.8 shard_map.52
  38.4 62.4 %all_to_all.21.in_ref = bf16[16,2,4224]{2,1,0:T(2,128)(2,1)S(1)} all-to-all(bf16[16,2,4224]{2,1,0:T(2,128)(2,1)S(1)} %shard_map.52), channel_id=1, replica_groups=mesh['x'=4,'core'=2,'y'=4,'zh'=8,'zm'=2,'z0'=2] {'zh','zm'}, dimensions={0} | all-to-all | bytes 540672 | tf_op jit(solution)/shard_map/all_to_all | solution.py:249
  100.8 1.1 shard_map.55
  101.9 3.6 %all-to-all-start.3 = ((bf16[8,32,2048]{2,1,0:T(8,128)(2,1)}), bf16[8,32,2048]{2,1,0:T(8,128)(2,1)S(1)}, u32[]{:S(2)}, u32[]{:S(2)}) async-start(bf16[8,32,2048]{2,1,0:T(8,128)(2,1)} %shard_map.55), calls=%async_computation.3 | async-start | bytes 2097152 | tf_op jit(solution)/shard_map/all_to_all | solution.py:250
  105.5 0.6 shard_map.54.toks_ref
  106.1 0.7 shard_map.53
  106.8 12.3 %all-to-all-done.3 = bf16[8,32,2048]{2,1,0:T(8,128)(2,1)S(1)} async-done(((bf16[8,32,2048]{2,1,0:T(8,128)(2,1)}), bf16[8,32,2048]{2,1,0:T(8,128)(2,1)S(1)}, u32[]{:S(2)}, u32[]{:S(2)}) %all-to-all-start.3) | async-done | bytes 1048608 | tf_op jit(solution)/shard_map/all_to_all | solution.py:250
  119.1 3.2 %shard_map.56 = bf16[416,2048]{1,0:T(8,128)(2,1)} custom-call(bf16[416,256]{1,0:T(8,128)(2,1)S(1)} %shard_map.54.toks_ref, bf16[256,2048]{1,0:T(8,128)(2,1)S(1)} %bitcast.4), custom_call_target="tpu_custom_call" | custom-call | flops 446693376 | bytes 2752512 | tf_op jit(solution)/shard_map/pallas_call | solution.py:227
Async XLA Ops:
  2.1 11.8 %all-to-all-start = ((bf16[8,32,416]{2,1,0:T(8,128)(2,1)}), bf16[8,32,416]{2,1,0:T(8,128)(2,1)S(1)}, u32[]{:S(2)}, u32[]{:S(2)}) async-start(bf16[8,32,416]{2,1,0:T(8,128)(2,1)} %broadcast_in_dim.2), calls=%async_computation | async-start | bytes 524288 | tf_op jit(solution)/shard_map/all_to_all | solution.py:247
  6.4 1.5 %copy-start = (bf16[2048,416]{0,1:T(8,128)(2,1)S(1)}, bf16[2048,416]{0,1:T(8,128)(2,1)}, u32[]{:S(2)}) copy-start(bf16[2048,416]{0,1:T(8,128)(2,1)} %param.5) | copy-start | bytes 5111812
  15.8 21.8 %copy-start.1 = (bf16[2,2048]{1,0:T(2,128)(2,1)S(1)}, bf16[2,2048]{1,0:T(2,128)(2,1)}, u32[]{:S(2)}) copy-start(bf16[2,2048]{1,0:T(2,128)(2,1)} %acts_ref.1) | copy-start | bytes 24580
  101.9 17.2 %all-to-all-start.3 = ((bf16[8,32,2048]{2,1,0:T(8,128)(2,1)}), bf16[8,32,2048]{2,1,0:T(8,128)(2,1)S(1)}, u32[]{:S(2)}, u32[]{:S(2)}) async-start(bf16[8,32,2048]{2,1,0:T(8,128)(2,1)} %shard_map.55), calls=%async_computation.3 | async-start | bytes 2097152 | tf_op jit(solution)/shard_map/all_to_all | solution.py:250

commit v9 on v8

--- a/solution.py
+++ b/solution.py
@@ -48,12 +48,12 @@
 
 def encode_with(values, top):
     level = jnp.exp2(jnp.abs(values) * ((2.0 * SPAN) / top.astype(F32)) - SPAN)
-    return jnp.where(values < 0.0, -level, level).astype(BF16)
+    return jnp.where(values < 0.0, -level, level)
 
 
 def encode(values):
     top = top_of(jnp.max(jnp.abs(values), axis=1, keepdims=True))
-    return encode_with(values, top), jnp.broadcast_to(top, (values.shape[0], LANES))
+    return encode_with(values, top), jnp.broadcast_to(top.astype(F32), (values.shape[0], LANES))
 
 
 def decode(codes, top):
@@ -90,7 +90,7 @@
     wide = jnp.broadcast_to(top, (tok, LANES))
     for k in range(Y * Z0):
         r = slice(k * rows, (k + 1) * rows)
-        out_ref[k, :, :feat] = encode_with(sums_ref[r, :], top[r])
+        out_ref[k, :, :feat] = encode_with(sums_ref[r, :], top[r]).astype(BF16)
         out_ref[k, :, feat:] = wide[r]
 
 
@@ -131,8 +131,8 @@
     feat = wide - LANES
     codes, top = encode(decoded_sum(in_ref))
     for k in range(Z16):
-        out_ref[k, :, :feat] = codes[2 * k : 2 * k + 2]
-        out_ref[k, :, feat:wide] = top[2 * k : 2 * k + 2]
+        out_ref[k, :, :feat] = codes[2 * k : 2 * k + 2].astype(BF16)
+        out_ref[k, :, feat:wide] = top[2 * k : 2 * k + 2].astype(BF16)
         out_ref[k, :, wide:] = acts_ref[...]
 
 
@@ -146,12 +146,12 @@
     )(parts, acts)
 
 
-def spread_kernel(in_ref, out_ref, held_ref):
+def spread_kernel(in_ref, out_ref):
     feat = out_ref.shape[2]
-    for k in range(Z16):
-        held_ref[2 * k : 2 * k + 2, :] = in_ref[k, :, in_ref.shape[2] - feat :]
+    held = [in_ref[k, :, in_ref.shape[2] - feat :].astype(F32) for k in range(Z16)]
+    held = jnp.concatenate(held, axis=0).astype(BF16)
     for j in range(Y * Z0):
-        out_ref[j] = held_ref[...]
+        out_ref[j] = held
 
 
 def spread(parts, feat):
@@ -159,7 +159,6 @@
     return pl.pallas_call(
         spread_kernel,
         out_shape=jax.ShapeDtypeStruct((Y * Z0, places * rows, feat), BF16),
-        scratch_shapes=[pltpu.VMEM((places * rows, feat), BF16)],
         compiler_params=pltpu.CompilerParams(vmem_limit_bytes=16 * 2**20),
         cost_estimate=pl.CostEstimate(flops=0, bytes_accessed=20 * places * rows * feat, transcendentals=0),
     )(parts)

time: 123 us -> 123 us (level)
  no operation moved by 1% of the time
where the time goes in v9:
time: 123 us; the launch traced here: 122 us
  blocking collectives  84.2 us (68%)
  waiting for transfers between devices  18.1 us (15%)
  Pallas kernels  8.51 us (7%)
  starting transfers between devices  7.86 us (6%)
  local copies, waits for them, and re-layouts  2.94 us (2%)
    all_to_all x1, blocking collectives, local(): parts = lax.all_to_all(add_near(sums, acts), far, 0, 0)  62.4 us
    all_to_all x1, blocking collectives, local(): sums = lax.all_to_all(partial_sums(g, fetch(weight.T)), near, 0, 0)  21.8 us
    all_to_all x1, waiting for transfers between devices, local(): all_acts = lax.all_to_all(spread(parts, feat), near, 0, 0)  12.3 us
    all_to_all x1, waiting for transfers between devices, local(): g = lax.all_to_all(copies, row, 0, 0).reshape(8 * own, ff)  5.8 us
    all_to_all x1, starting transfers between devices, local(): g = lax.all_to_all(copies, row, 0, 0).reshape(8 * own, ff)  4.3 us
    all_to_all x1, starting transfers between devices, local(): all_acts = lax.all_to_all(spread(parts, feat), near, 0, 0)  3.56 us
    pallas_call x1, Pallas kernels, weight_grad(): pl.pallas_call(weight_kernel, out_shape=jax.ShapeDtypeStruct((ff, feat),...  3.19 us
  transfers between devices with their start and end apart: 2, of which 2 were waited for; matrix products, arithmetic and copies ran while one was open for 0% of the time, Pallas kernels for 1%

profile of v9, /device:TPU:64, one launch (start us, length us, event | category | flops | bytes accessed | tf_op | source)
XLA Modules:
  0.0 122.2 jit_solution(8709563469423118889)
XLA Ops:
  0.6 1.5 %broadcast_in_dim.2 = bf16[8,32,416]{2,1,0:T(8,128)(2,1)} broadcast(bf16[32,416]{1,0:T(8,128)(2,1)} %param.3), dimensions={1,2} | broadcast | bytes 239616 | tf_op jit(solution)/shard_map/broadcast_in_dim | solution.py:245
  2.1 4.3 %all-to-all-start = ((bf16[8,32,416]{2,1,0:T(8,128)(2,1)}), bf16[8,32,416]{2,1,0:T(8,128)(2,1)S(1)}, u32[]{:S(2)}, u32[]{:S(2)}) async-start(bf16[8,32,416]{2,1,0:T(8,128)(2,1)} %broadcast_in_dim.2), calls=%async_computation | async-start | bytes 524288 | tf_op jit(solution)/shard_map/all_to_all | solution.py:246
  6.4 0.0 copy-start
  6.4 1.4 %copy-done = bf16[2048,416]{0,1:T(8,128)(2,1)S(1)} copy-done((bf16[2048,416]{0,1:T(8,128)(2,1)S(1)}, bf16[2048,416]{0,1:T(8,128)(2,1)}, u32[]{:S(2)}) %copy-start) | copy-done | bytes 1703960
  7.9 0.3 shard_map.50.w_ref
  8.2 5.8 %all-to-all-done = bf16[8,32,416]{2,1,0:T(8,128)(2,1)S(1)} async-done(((bf16[8,32,416]{2,1,0:T(8,128)(2,1)}), bf16[8,32,416]{2,1,0:T(8,128)(2,1)S(1)}, u32[]{:S(2)}, u32[]{:S(2)}) %all-to-all-start) | async-done | bytes 213024 | tf_op jit(solution)/shard_map/all_to_all | solution.py:246
  14.0 1.8 %shard_map.51 = bf16[8,32,2176]{2,1,0:T(8,128)(2,1)S(1)} custom-call(bf16[256,416]{1,0:T(8,128)(2,1)S(1)} %bitcast.5, bf16[416,2048]{1,0:T(8,128)(2,1)S(1)} %shard_map.50.w_ref), custom_call_target="tpu_custom_call" | custom-call | flops 436207616 | bytes 2752512 | tf_op jit(solution)/shard_map/pallas_call | solution.py:118
  15.8 0.0 copy-start.1
  15.8 21.8 %all_to_all.20.in_ref = bf16[8,32,2176]{2,1,0:T(8,128)(2,1)S(1)} all-to-all(bf16[8,32,2176]{2,1,0:T(8,128)(2,1)S(1)} %shard_map.51), channel_id=1, replica_groups=mesh['x'=4,'core'=2,'y'=4,'zh'=8,'zm'=2,'z0'=2] {'y','z0'}, dimensions={0} | all-to-all | bytes 2228224 | tf_op jit(solution)/shard_map/all_to_all | solution.py:247
  37.5 0.0 copy-done.1
  37.5 0.8 shard_map.52
  38.4 62.4 %all_to_all.21.in_ref = bf16[16,2,4224]{2,1,0:T(2,128)(2,1)S(1)} all-to-all(bf16[16,2,4224]{2,1,0:T(2,128)(2,1)S(1)} %shard_map.52), channel_id=1, replica_groups=mesh['x'=4,'core'=2,'y'=4,'zh'=8,'zm'=2,'z0'=2] {'zh','zm'}, dimensions={0} | all-to-all | bytes 540672 | tf_op jit(solution)/shard_map/all_to_all | solution.py:248
  100.8 1.1 shard_map.55
  101.9 3.6 %all-to-all-start.3 = ((bf16[8,32,2048]{2,1,0:T(8,128)(2,1)}), bf16[8,32,2048]{2,1,0:T(8,128)(2,1)S(1)}, u32[]{:S(2)}, u32[]{:S(2)}) async-start(bf16[8,32,2048]{2,1,0:T(8,128)(2,1)} %shard_map.55), calls=%async_computation.3 | async-start | bytes 2097152 | tf_op jit(solution)/shard_map/all_to_all | solution.py:249
  105.4 0.6 shard_map.54.toks_ref
  106.0 0.7 shard_map.53
  106.8 12.3 %all-to-all-done.3 = bf16[8,32,2048]{2,1,0:T(8,128)(2,1)S(1)} async-done(((bf16[8,32,2048]{2,1,0:T(8,128)(2,1)}), bf16[8,32,2048]{2,1,0:T(8,128)(2,1)S(1)}, u32[]{:S(2)}, u32[]{:S(2)}) %all-to-all-start.3) | async-done | bytes 1048608 | tf_op jit(solution)/shard_map/all_to_all | solution.py:249
  119.0 3.2 %shard_map.56 = bf16[416,2048]{1,0:T(8,128)(2,1)} custom-call(bf16[416,256]{1,0:T(8,128)(2,1)S(1)} %shard_map.54.toks_ref, bf16[256,2048]{1,0:T(8,128)(2,1)S(1)} %bitcast.4), custom_call_target="tpu_custom_call" | custom-call | flops 446693376 | bytes 2752512 | tf_op jit(solution)/shard_map/pallas_call | solution.py:226
Async XLA Ops:
  2.1 11.8 %all-to-all-start = ((bf16[8,32,416]{2,1,0:T(8,128)(2,1)}), bf16[8,32,416]{2,1,0:T(8,128)(2,1)S(1)}, u32[]{:S(2)}, u32[]{:S(2)}) async-start(bf16[8,32,416]{2,1,0:T(8,128)(2,1)} %broadcast_in_dim.2), calls=%async_computation | async-start | bytes 524288 | tf_op jit(solution)/shard_map/all_to_all | solution.py:246
  6.4 1.5 %copy-start = (bf16[2048,416]{0,1:T(8,128)(2,1)S(1)}, bf16[2048,416]{0,1:T(8,128)(2,1)}, u32[]{:S(2)}) copy-start(bf16[2048,416]{0,1:T(8,128)(2,1)} %param.5) | copy-start | bytes 5111812
  15.8 21.8 %copy-start.1 = (bf16[2,2048]{1,0:T(2,128)(2,1)S(1)}, bf16[2,2048]{1,0:T(2,128)(2,1)}, u32[]{:S(2)}) copy-start(bf16[2,2048]{1,0:T(2,128)(2,1)} %acts_ref.1) | copy-start | bytes 24580
  101.9 17.2 %all-to-all-start.3 = ((bf16[8,32,2048]{2,1,0:T(8,128)(2,1)}), bf16[8,32,2048]{2,1,0:T(8,128)(2,1)S(1)}, u32[]{:S(2)}, u32[]{:S(2)}) async-start(bf16[8,32,2048]{2,1,0:T(8,128)(2,1)} %shard_map.55), calls=%async_computation.3 | async-start | bytes 2097152 | tf_op jit(solution)/shard_map/all_to_all | solution.py:249

commit v10 on v9

--- a/solution.py
+++ b/solution.py
@@ -146,12 +146,31 @@
     )(parts, acts)
 
 
-def spread_kernel(in_ref, out_ref):
+def send_copies(held_ref, out_ref, sems):
+    copies = [pltpu.make_async_copy(held_ref, out_ref.at[j], sems.at[j]) for j in range(out_ref.shape[0])]
+    for copy in copies:
+        copy.start()
+    for copy in copies:
+        copy.wait()
+
+
+def repeat(x, times):
+    return pl.pallas_call(
+        send_copies,
+        out_shape=jax.ShapeDtypeStruct((times,) + x.shape, x.dtype),
+        in_specs=[pl.BlockSpec(memory_space=pltpu.VMEM)],
+        out_specs=pl.BlockSpec(memory_space=pl.ANY),
+        scratch_shapes=[pltpu.SemaphoreType.DMA((times,))],
+        compiler_params=pltpu.CompilerParams(vmem_limit_bytes=16 * 2**20),
+        cost_estimate=pl.CostEstimate(flops=0, bytes_accessed=2 * times * x.size, transcendentals=0),
+    )(x)
+
+
+def spread_kernel(in_ref, out_ref, held_ref, sems):
     feat = out_ref.shape[2]
     held = [in_ref[k, :, in_ref.shape[2] - feat :].astype(F32) for k in range(Z16)]
-    held = jnp.concatenate(held, axis=0).astype(BF16)
-    for j in range(Y * Z0):
-        out_ref[j] = held
+    held_ref[...] = jnp.concatenate(held, axis=0).astype(BF16)
+    send_copies(held_ref, out_ref, sems)
 
 
 def spread(parts, feat):
@@ -159,6 +178,9 @@
     return pl.pallas_call(
         spread_kernel,
         out_shape=jax.ShapeDtypeStruct((Y * Z0, places * rows, feat), BF16),
+        in_specs=[pl.BlockSpec(memory_space=pltpu.VMEM)],
+        out_specs=pl.BlockSpec(memory_space=pl.ANY),
+        scratch_shapes=[pltpu.VMEM((places * rows, feat), BF16), pltpu.SemaphoreType.DMA((Y * Z0,))],
         compiler_params=pltpu.CompilerParams(vmem_limit_bytes=16 * 2**20),
         cost_estimate=pl.CostEstimate(flops=0, bytes_accessed=20 * places * rows * feat, transcendentals=0),
     )(parts)
@@ -242,8 +264,7 @@
     own, ff = grad_out.shape
     feat = acts.shape[1]
     row, near, far = ("x", "core"), ("y", "z0"), ("zh", "zm")
-    copies = jnp.broadcast_to(grad_out[None], (8, own, ff))
-    g = lax.all_to_all(copies, row, 0, 0).reshape(8 * own, ff)
+    g = lax.all_to_all(repeat(grad_out, 8), row, 0, 0).reshape(8 * own, ff)
     sums = lax.all_to_all(partial_sums(g, fetch(weight.T)), near, 0, 0)
     parts = lax.all_to_all(add_near(sums, acts), far, 0, 0)
     all_acts = lax.all_to_all(spread(parts, feat), near, 0, 0)

time: 123 us -> 123 us (level)
    broadcast_in_dim x1 -> x0, local copies, waits for them, and re-layouts: 1.48 us -> none  [local(): copies = jnp.broadcast_to(grad_out[None], (8, own, ff))]
where the time goes in v10:
time: 123 us
  blocking collectives  84.2 us (68%)
  waiting for transfers between devices  18.5 us (15%)
  Pallas kernels  9.3 us (8%)
  starting transfers between devices  7.88 us (6%)
  local copies, waits for them, and re-layouts  2.21 us (2%)
    all_to_all x1, blocking collectives, local(): parts = lax.all_to_all(add_near(sums, acts), far, 0, 0)  62.4 us
    all_to_all x1, blocking collectives, local(): sums = lax.all_to_all(partial_sums(g, fetch(weight.T)), near, 0, 0)  21.8 us
    all_to_all x1, waiting for transfers between devices, local(): all_acts = lax.all_to_all(spread(parts, feat), near, 0, 0)  12.7 us
    all_to_all x1, waiting for transfers between devices, local(): g = lax.all_to_all(repeat(grad_out, 8), row, 0, 0).reshape(8 * own, ff)  5.8 us
    all_to_all x1, starting transfers between devices, local(): g = lax.all_to_all(repeat(grad_out, 8), row, 0, 0).reshape(8 * own, ff)  4.31 us
    all_to_all x1, starting transfers between devices, local(): all_acts = lax.all_to_all(spread(parts, feat), near, 0, 0)  3.57 us
    pallas_call x1, Pallas kernels, weight_grad(): pl.pallas_call(weight_kernel, out_shape=jax.ShapeDtypeStruct((ff, feat),...  3.19 us
  transfers between devices with their start and end apart: 2, of which 2 were waited for; matrix products, arithmetic and copies ran while one was open for 0% of the time, Pallas kernels for 1%

profile of v10, /device:TPU:64, one launch (start us, length us, event | category | flops | bytes accessed | tf_op | source)
XLA Modules:
  0.0 122.7 jit_solution(275576052333118551)
XLA Ops:
  0.6 0.0 copy-start.1
  0.6 0.7 copy-done.1
  1.4 0.8 shard_map.50
  2.2 4.3 %all-to-all-start = ((bf16[8,32,416]{2,1,0:T(8,128)(2,1)}), bf16[8,32,416]{2,1,0:T(8,128)(2,1)S(1)}, u32[]{:S(2)}, u32[]{:S(2)}) async-start(bf16[8,32,416]{2,1,0:T(8,128)(2,1)} %shard_map.50), calls=%async_computation | async-start | bytes 524288 | tf_op jit(solution)/shard_map/all_to_all | solution.py:267
  6.5 0.0 copy-start
  6.5 1.4 %copy-done = bf16[2048,416]{0,1:T(8,128)(2,1)S(1)} copy-done((bf16[2048,416]{0,1:T(8,128)(2,1)S(1)}, bf16[2048,416]{0,1:T(8,128)(2,1)}, u32[]{:S(2)}) %copy-start) | copy-done | bytes 1703960
  7.9 0.3 shard_map.51.w_ref
  8.2 5.8 %all-to-all-done = bf16[8,32,416]{2,1,0:T(8,128)(2,1)S(1)} async-done(((bf16[8,32,416]{2,1,0:T(8,128)(2,1)}), bf16[8,32,416]{2,1,0:T(8,128)(2,1)S(1)}, u32[]{:S(2)}, u32[]{:S(2)}) %all-to-all-start) | async-done | bytes 213024 | tf_op jit(solution)/shard_map/all_to_all | solution.py:267
  14.0 1.8 %shard_map.52 = bf16[8,32,2176]{2,1,0:T(8,128)(2,1)S(1)} custom-call(bf16[256,416]{1,0:T(8,128)(2,1)S(1)} %bitcast.5, bf16[416,2048]{1,0:T(8,128)(2,1)S(1)} %shard_map.51.w_ref), custom_call_target="tpu_custom_call" | custom-call | flops 436207616 | bytes 2752512 | tf_op jit(solution)/shard_map/pallas_call | solution.py:118
  15.8 0.0 copy-start.2
  15.8 21.8 %all_to_all.20.in_ref = bf16[8,32,2176]{2,1,0:T(8,128)(2,1)S(1)} all-to-all(bf16[8,32,2176]{2,1,0:T(8,128)(2,1)S(1)} %shard_map.52), channel_id=1, replica_groups=mesh['x'=4,'core'=2,'y'=4,'zh'=8,'zm'=2,'z0'=2] {'y','z0'}, dimensions={0} | all-to-all | bytes 2228224 | tf_op jit(solution)/shard_map/all_to_all | solution.py:268
  37.6 0.0 copy-done.2
  37.6 0.8 shard_map.53
  38.5 62.4 %all_to_all.21.in_ref = bf16[16,2,4224]{2,1,0:T(2,128)(2,1)S(1)} all-to-all(bf16[16,2,4224]{2,1,0:T(2,128)(2,1)S(1)} %shard_map.53), channel_id=1, replica_groups=mesh['x'=4,'core'=2,'y'=4,'zh'=8,'zm'=2,'z0'=2] {'zh','zm'}, dimensions={0} | all-to-all | bytes 540672 | tf_op jit(solution)/shard_map/all_to_all | solution.py:269
  100.9 1.1 shard_map.56
  102.0 3.6 %all-to-all-start.3 = ((bf16[8,32,2048]{2,1,0:T(8,128)(2,1)}), bf16[8,32,2048]{2,1,0:T(8,128)(2,1)S(1)}, u32[]{:S(2)}, u32[]{:S(2)}) async-start(bf16[8,32,2048]{2,1,0:T(8,128)(2,1)} %shard_map.56), calls=%async_computation.3 | async-start | bytes 2097152 | tf_op jit(solution)/shard_map/all_to_all | solution.py:270
  105.6 0.6 shard_map.55.toks_ref
  106.1 0.7 shard_map.54
  106.9 12.7 %all-to-all-done.3 = bf16[8,32,2048]{2,1,0:T(8,128)(2,1)S(1)} async-done(((bf16[8,32,2048]{2,1,0:T(8,128)(2,1)}), bf16[8,32,2048]{2,1,0:T(8,128)(2,1)S(1)}, u32[]{:S(2)}, u32[]{:S(2)}) %all-to-all-start.3) | async-done | bytes 1048608 | tf_op jit(solution)/shard_map/all_to_all | solution.py:270
  119.5 3.2 %shard_map.57 = bf16[416,2048]{1,0:T(8,128)(2,1)} custom-call(bf16[416,256]{1,0:T(8,128)(2,1)S(1)} %shard_map.55.toks_ref, bf16[256,2048]{1,0:T(8,128)(2,1)S(1)} %bitcast.4), custom_call_target="tpu_custom_call" | custom-call | flops 446693376 | bytes 2752512 | tf_op jit(solution)/shard_map/pallas_call | solution.py:248
Async XLA Ops:
  0.6 0.8 copy-start.1
  2.2 11.9 %all-to-all-start = ((bf16[8,32,416]{2,1,0:T(8,128)(2,1)}), bf16[8,32,416]{2,1,0:T(8,128)(2,1)S(1)}, u32[]{:S(2)}, u32[]{:S(2)}) async-start(bf16[8,32,416]{2,1,0:T(8,128)(2,1)} %shard_map.50), calls=%async_computation | async-start | bytes 524288 | tf_op jit(solution)/shard_map/all_to_all | solution.py:267
  6.5 1.5 %copy-start = (bf16[2048,416]{0,1:T(8,128)(2,1)S(1)}, bf16[2048,416]{0,1:T(8,128)(2,1)}, u32[]{:S(2)}) copy-start(bf16[2048,416]{0,1:T(8,128)(2,1)} %param.5) | copy-start | bytes 5111812
  15.8 21.8 %copy-start.2 = (bf16[2,2048]{1,0:T(2,128)(2,1)S(1)}, bf16[2,2048]{1,0:T(2,128)(2,1)}, u32[]{:S(2)}) copy-start(bf16[2,2048]{1,0:T(2,128)(2,1)} %acts_ref.1) | copy-start | bytes 24580
  102.0 17.6 %all-to-all-start.3 = ((bf16[8,32,2048]{2,1,0:T(8,128)(2,1)}), bf16[8,32,2048]{2,1,0:T(8,128)(2,1)S(1)}, u32[]{:S(2)}, u32[]{:S(2)}) async-start(bf16[8,32,2048]{2,1,0:T(8,128)(2,1)} %shard_map.56), calls=%async_computation.3 | async-start | bytes 2097152 | tf_op jit(solution)/shard_map/all_to_all | solution.py:270
